TPU v7x, 32 devices: a whole 2x2x4 slice. The times are simulated.
32 devices in a mesh: dp: 4 (over y, x), seq: 8 (over z, core).
Axes of the slice: x: 2, y: 2, z: 4, core: 2. Of those that a mesh axis runs over, the one named last changes fastest.
Arguments:
- latents: bfloat16 [4, 8, 256, 1152], P('dp', 'seq'), may hold values from -6 to 6
- in_weight: bfloat16 [1152, 3456], replicated
- out_weight: bfloat16 [1152, 1152], replicated, may hold values from -0.1875 to 0.1875
- cotangent: bfloat16 [4, 8, 256, 1152], P('dp', 'seq'), may hold values from -6 to 6
- clip_lengths: int32 [4, 4], P('dp'), may hold values from 1 to 4, 8 in all within a row
Outputs:
- mixed: bfloat16 [4, 8, 256, 1152], P('dp', 'seq')
- grad_latents: bfloat16 [4, 8, 256, 1152], P('dp', 'seq')
- out_grad: float32 [1152, 1152], P('seq')
Inputs may be any that keep to these rules, and one draw needn't show every extreme that they name: `clip_lengths`: the 4 lengths of a sequence sum to 8; in every sequence the longest is exactly 4.
All inputs are finite; a program needn't handle non-finite values.
Results may differ from a plain program's by a relative error of at most 0.013.
The roundings to bfloat16 on the way count: a program that leaves them out, or rounds other values in their place, can miss the bound.
Values may be sent and summed in bfloat16 or wider, within the bound.
No kernel may reach another device: no remote copies, remote signals or barrier semaphores. Data moves between devices by JAX's collectives and lax.ppermute only.
A program may use at most 128 MiB of HBM per device.

v0:
```python
import functools

import jax
import jax.numpy as jnp
import numpy as np
from jax import lax
from jax.experimental import pallas as pl
from jax.experimental.pallas import tpu as pltpu
from jax.sharding import PartitionSpec as P

HEADS = 16
HD = 72


def clip_index(lengths, frames):
    ends = jnp.cumsum(lengths)
    position = jnp.arange(frames, dtype=jnp.int32)
    return jnp.sum((ends[None, :] <= position[:, None]).astype(jnp.int32), axis=1)


def softmax_weights(query, key_rows, same):
    scale = 1.0 / jnp.sqrt(jnp.float32(HD))
    scores = (
        jnp.einsum("fphd,gphd->phfg", query, key_rows, preferred_element_type=jnp.float32) * scale
    )
    scores = jnp.where(same[None, None], scores, -jnp.inf)
    return jax.nn.softmax(scores, axis=-1)


def contract_rows(left, right):
    return lax.dot_general(
        left, right, (((0,), (0,)), ((), ())), preferred_element_type=jnp.float32
    )


def contract_cols(left, right):
    return lax.dot_general(
        left, right, (((1,), (1,)), ((), ())), preferred_element_type=jnp.float32
    )


def swap(value, axis, flip):
    size = lax.axis_size(axis)
    return lax.ppermute(value, axis, [(i, i ^ flip) for i in range(size)])


def reduce_out(part):
    mine = lax.psum_scatter(part, "seq", scatter_dimension=0, tiled=True)
    return lax.psum(mine.astype(jnp.bfloat16), "dp").astype(jnp.float32)


def patch_body(latents, in_weight, out_weight, cotangent, clip_lengths):
    shards = lax.axis_size("seq")
    local_frames = latents.shape[1]
    patches = latents.shape[2]
    width = latents.shape[3]
    frames = local_frames * shards
    local_patches = patches // shards
    inner = HEADS * HD

    def to_patches(rows):
        return lax.all_to_all(rows, "seq", split_axis=2, concat_axis=1, tiled=True)

    def to_frames(rows):
        return lax.all_to_all(rows, "seq", split_axis=1, concat_axis=2, tiled=True)

    lat_rows = to_patches(latents).reshape(frames * local_patches, width)
    cot_rows = to_patches(cotangent).reshape(frames * local_patches, width)
    projected = jnp.dot(lat_rows, in_weight, preferred_element_type=jnp.float32).astype(
        jnp.bfloat16
    )
    split = projected.reshape(frames, local_patches, 3, HEADS, HD)
    query, key_rows, value_rows = (split[:, :, 0], split[:, :, 1], split[:, :, 2])
    clip = clip_index(clip_lengths[0], frames)
    same = clip[:, None] == clip[None, :]
    weights32 = softmax_weights(query, key_rows, same)
    weights = weights32.astype(jnp.bfloat16)
    attended = jnp.einsum(
        "phfg,gphd->fphd", weights, value_rows, preferred_element_type=jnp.float32
    ).astype(jnp.bfloat16)
    att_rows = attended.reshape(frames * local_patches, inner)
    out_grad = reduce_out(contract_rows(att_rows, cot_rows))
    mixed = jnp.dot(att_rows, out_weight, preferred_element_type=jnp.float32).astype(jnp.bfloat16)
    mixed = to_frames(mixed.reshape(1, frames, local_patches, width))
    grad_att = contract_cols(cot_rows, out_weight).astype(jnp.bfloat16)
    grad_heads = grad_att.reshape(frames, local_patches, HEADS, HD)
    grad_weights = jnp.einsum(
        "fphd,gphd->phfg", grad_heads, value_rows, preferred_element_type=jnp.float32
    )
    grad_values = jnp.einsum(
        "phfg,fphd->gphd", weights, grad_heads, preferred_element_type=jnp.float32
    ).astype(jnp.bfloat16)
    totals = jnp.sum(weights32 * grad_weights, axis=-1, keepdims=True)
    scale = 1.0 / jnp.sqrt(jnp.float32(HD))
    grad_scores = (weights32 * (grad_weights - totals) * scale).astype(jnp.bfloat16)
    grad_query = jnp.einsum(
        "phfg,gphd->fphd", grad_scores, key_rows, preferred_element_type=jnp.float32
    ).astype(jnp.bfloat16)
    grad_keys = jnp.einsum(
        "phfg,fphd->gphd", grad_scores, query, preferred_element_type=jnp.float32
    ).astype(jnp.bfloat16)
    grad_proj = jnp.stack([grad_query, grad_keys, grad_values], axis=2)
    grad_rows = grad_proj.reshape(frames * local_patches, 3 * inner)
    grad_latents = contract_cols(grad_rows, in_weight).astype(jnp.bfloat16)
    grad_latents = to_frames(grad_latents.reshape(1, frames, local_patches, width))
    return (mixed.reshape(latents.shape), grad_latents.reshape(latents.shape), out_grad)


ROWS = 64
PAIRS = 16
TILE = 128
INNER = HEADS * HD
PIECE = 40
SMEM = pl.BlockSpec(memory_space=pltpu.SMEM)
VMEM = pl.BlockSpec(memory_space=pltpu.VMEM)
HBM = pl.BlockSpec(memory_space=pltpu.HBM)
CHUNKS = ((0, 256), (256, 256), (512, 256), (768, 256), (1024, 128))


def shaped(shape, dtype=jnp.bfloat16):
    return jax.ShapeDtypeStruct(shape, dtype)


def dot(left, right):
    return jnp.dot(left, right, preferred_element_type=jnp.float32)


def flat(value):
    return value.reshape(value.shape[0] * ROWS, value.shape[2])


def call(kernel, scalars, inputs, outs, scratch=(), limit=8, flops=10**6, to_hbm=False, size=None):
    size = size or sum(x.size * x.dtype.itemsize for x in (*inputs, *outs))
    return pl.pallas_call(
        kernel,
        out_shape=list(outs),
        in_specs=[SMEM] * len(scalars) + [VMEM] * len(inputs),
        out_specs=[HBM if to_hbm else VMEM] * len(outs),
        scratch_shapes=[x if hasattr(x, "memory_space") else pltpu.VMEM(*x) for x in scratch],
        compiler_params=pltpu.CompilerParams(vmem_limit_bytes=limit << 20),
        cost_estimate=pl.CostEstimate(flops=flops, bytes_accessed=size, transcendentals=0),
    )(*scalars, *inputs)


def roles(spot):
    zpos, lens = spot[0] // 2, [spot[2 + i] for i in range(3)]
    first = 2 * zpos
    ends = [lens[0], lens[0] + lens[1], lens[0] + lens[1] + lens[2]]
    long = jnp.where(
        lens[0] == 4, 0, jnp.where(lens[1] == 4, ends[0], jnp.where(lens[2] == 4, ends[1], ends[2]))
    )

    def clip(frame):
        return sum((end <= frame).astype(jnp.int32) for end in ends)

    ids = [
        jnp.where(zpos == 0, -1, clip(first - 1)),
        clip(first),
        clip(first + 1),
        jnp.where(zpos == 3, -2, clip(first + 2)),
    ]
    return {
        "core": spot[0] % 2,
        "odd": zpos % 2,
        "left": 6 - 2 * (zpos % 2),
        "right": 4 + 2 * (zpos % 2),
        "ids": ids,
        "low": long == first,
        "high": long == first - 2,
        "middle": long == first - 1,
        "tail": long == first - 3,
        "head": long == first + 1,
    }


def slots(role, window):
    low, high, left, right = role["low"], role["high"], role["left"], role["right"]
    in_low = ((0, 2, right, right + 1), (1, 3, left, left + 1))[window]
    in_high = ((left, left + 1, 1, 3), (0, 2, right, right + 1))[window]
    usual = (left + window, window, 2 + window, right + window)
    blocks = [
        jnp.where(low, a, jnp.where(high, b, c)) for a, b, c in zip(in_low, in_high, usual)
    ]
    even, middle = low | high, role["middle"]
    odd = [middle, ~even & ~role["tail"], ~even & ~role["head"], middle]
    return blocks, [even | x for x in odd] if window == 0 else odd


def own_kernel(spot, rows, mine):
    for i in range(2):
        mine[i] = rows[2 * (spot[0] % 2) + i]


def pick_kernel(spot, own, sib, near, far, both):
    role = roles(spot)
    core, odd = role["core"], role["odd"]
    for i in range(2):
        both[2 * core + i] = own[i if own.shape[0] == 2 else 2 * core + i]
        both[2 * (1 - core) + i] = sib[2 * core + i]
    right = (jnp.where(role["low"], 1, 2), 3)
    left = (0, jnp.where(role["high"], 2, 1))
    for i in range(2):
        near[i] = both[jnp.where(odd == 1, left[i], right[i])]
        far[i] = both[jnp.where(odd == 1, right[i], left[i])]


def early_kernel(lat_ab, wi_ref, qkv_ref):
    x = flat(lat_ab[...])
    for j in range(3):
        cols = slice(j * INNER, (j + 1) * INNER)
        qkv_ref[:, :, cols] = dot(x, wi_ref[:, cols]).astype(jnp.bfloat16).reshape(4, ROWS, INNER)


def pair(f, g, w=0, count=1):
    start = (4 * f + g) * 2 * ROWS + w * ROWS
    return slice(start, start + count * ROWS)


def lanes(t, offset=0):
    return slice(offset + TILE * t, offset + TILE * (t + 1))


def forward_kernel(
    spot, near, far, wi_ref, ab_ref, heads_ref, qkv_ref, att_ref, p_ref, wide_ref,
    x_scr, hi_scr, w_scr,
):
    x_scr[:2] = near[...]
    x_scr[2:] = far[...]
    qkv_ref[:4] = ab_ref[...]
    x = flat(x_scr[...])
    for j in range(3):
        cols = slice(j * INNER, (j + 1) * INNER)
        qkv_ref[4:, :, cols] = dot(x, wi_ref[:, cols]).astype(jnp.bfloat16).reshape(4, ROWS, INNER)
    role = roles(spot)
    even, ids = role["low"] | role["high"], role["ids"]
    windows = [slots(role, w) for w in range(2)]
    for w, (blocks, _) in enumerate(windows):
        for t in range(INNER // TILE):
            q = [qkv_ref[blocks[f], :, lanes(t)] for f in range(4)]
            k = [qkv_ref[blocks[g], :, lanes(t, INNER)] for g in range(4)]
            for f in range(4):
                for g in range(4):
                    hi_scr[pair(f, g, w), lanes(t)] = q[f] * k[g]
    scores = contract_cols(heads_ref[...], hi_scr[...])
    for f in range(4):
        line = []
        for g in range(4):
            bias = jnp.where(even | (ids[f] == ids[g]), 0.0, -jnp.inf)
            line.append(scores[:, pair(f, g, 0, 2)] * HD**-0.5 + bias)
        top = jnp.maximum(jnp.maximum(line[0], line[1]), jnp.maximum(line[2], line[3]))
        line = [jnp.exp(x - top) for x in line]
        share = 1.0 / (line[0] + line[1] + line[2] + line[3])
        for g in range(4):
            p_ref[:, pair(f, g, 0, 2)] = line[g] * share
    w_scr[...] = p_ref[...].T.astype(jnp.bfloat16)
    for f in range(4):
        rows = pair(f, 0, 0, 8)
        for start, size in CHUNKS:
            cols = slice(start, start + size)
            spread = dot(w_scr[rows, :], heads_ref[:, cols])
            wide_ref[rows, cols] = spread.astype(jnp.bfloat16)
            for w, (blocks, kept) in enumerate(windows):
                base = 2 * INNER + start
                total = sum(
                    spread[pair(0, g, w)] * qkv_ref[blocks[g], :, base : base + size].astype(jnp.float32)
                    for g in range(4)
                )
                total = total * jnp.where(kept[f], 1.0, 0.0)
                att_ref[blocks[f], :, cols] = total.astype(jnp.bfloat16)


def part_rows(core, att_t, cot, rows):
    height = att_t.shape[0] // 8
    for z in range(4):
        start = pl.multiple_of((2 * z + core) * height, 16)
        rows[z * height : (z + 1) * height, :] = att_t[pl.ds(start, height), :]
    return dot(rows[...], flat(cot[...])).reshape(4, height, -1)


def part_kernel(spot, att_ref, ab_ref, near, far, sib_ref, att_t, cot, rows):
    cot[:4] = ab_ref[...]
    cot[4:6] = near[...]
    cot[6:] = far[...]
    att_t[...] = flat(att_ref[...]).T
    sib_ref[...] = part_rows(1 - spot[0] % 2, att_t, cot, rows).astype(jnp.bfloat16)


def mix_kernel(att_ref, w_ref, here_ref, near_ref, far_ref):
    made = dot(flat(att_ref[...]), w_ref[...]).astype(jnp.bfloat16).reshape(8, ROWS, -1)
    here_ref[...] = made[:4]
    near_ref[...] = made[4:6]
    far_ref[...] = made[6:]


def grad_att_kernel(cot, wo_ref, ga_ref):
    made = contract_cols(flat(cot[...]), wo_ref[...])
    ga_ref[...] = made.astype(jnp.bfloat16).reshape(8, ROWS, INNER)


def backward_kernel(
    spot, ga_ref, qkv_ref, p_ref, wide_ref, heads_ref, d_ref, hi_scr, t_scr, s_scr
):
    role = roles(spot)
    windows = [slots(role, w)[0] for w in range(2)]
    for w, blocks in enumerate(windows):
        for t in range(INNER // TILE):
            do = [ga_ref[blocks[f], :, lanes(t)] for f in range(4)]
            v = [qkv_ref[blocks[g], :, lanes(t, 2 * INNER)] for g in range(4)]
            for f in range(4):
                for g in range(4):
                    hi_scr[pair(f, g, w), lanes(t)] = do[f] * v[g]
    grads = contract_cols(heads_ref[...], hi_scr[...])
    for f in range(4):
        p = [p_ref[:, pair(f, g, 0, 2)] for g in range(4)]
        line = [grads[:, pair(f, g, 0, 2)] for g in range(4)]
        total = sum(p[g] * line[g] for g in range(4))
        for g in range(4):
            t_scr[:, pair(f, g, 0, 2)] = p[g] * (line[g] - total) * HD**-0.5
    s_scr[...] = t_scr[...].T.astype(jnp.bfloat16)
    for start, size in CHUNKS:
        cols = slice(start, start + size)
        spread = dot(s_scr[...], heads_ref[:, cols])
        for w, blocks in enumerate(windows):

            def take(ref, block, offset=0):
                return ref[block, :, offset + start : offset + start + size].astype(jnp.float32)

            def put(block, offset, value):
                d_ref[block, :, offset + start : offset + start + size] = value.astype(jnp.bfloat16)

            do = [take(ga_ref, blocks[f]) for f in range(4)]
            for g in range(4):
                put(
                    blocks[g], 2 * INNER,
                    sum(wide_ref[pair(f, g, w), cols].astype(jnp.float32) * do[f] for f in range(4)),
                )
            q = [take(qkv_ref, blocks[f]) for f in range(4)]
            k = [take(qkv_ref, blocks[g], INNER) for g in range(4)]
            for f in range(4):
                put(blocks[f], 0, sum(spread[pair(f, g, w)] * k[g] for g in range(4)))
            for g in range(4):
                put(blocks[g], INNER, sum(spread[pair(f, g, w)] * q[f] for f in range(4)))


def latents_kernel(d_ref, wi_ref, *outs, first):
    tile = 384
    for j in range(wi_ref.shape[0] // tile):
        cols = slice(j * tile, (j + 1) * tile)
        made = contract_cols(flat(d_ref[first : first + 4]), wi_ref[cols, :]).astype(jnp.bfloat16)
        made = made.reshape(4, ROWS, tile)
        size = 4 // len(outs)
        for i, out in enumerate(outs):
            out[:, :, cols] = made[i * size : (i + 1) * size]


def settle_kernel(spot, *refs):
    *given, own, sib, held = refs
    role = roles(spot)
    core, left, right = role["core"], role["left"], role["right"]
    low, high, tail, head = role["low"], role["high"], role["tail"], role["head"]
    where = [
        jnp.where(high | tail, left, 0),
        jnp.where(low, right, jnp.where(tail, left + 1, 1)),
        jnp.where(high, left + 1, jnp.where(head, right, 2)),
        jnp.where(low | head, right + 1, 3),
    ]
    for base in (0, 2):
        here, near, far = given[:3] if base == 0 else given[3:]
        held[:4] = here[...]
        held[4:6] = near[...]
        held[6:] = far[...]
        for i in range(2):
            own[base + i] = held[jnp.where(core == 0, where[i], where[2 + i])]
            sib[base + i] = held[jnp.where(core == 0, where[2 + i], where[i])]


def cut(zpos, group):
    wide_first = jnp.where(group < 2, 40 * group, 32 * group + 16)
    wide_last = jnp.where(group < 2, 32 * group, 40 * group - 16)
    return pl.multiple_of(jnp.where(zpos % 2 == 0, wide_first, wide_last), 8)


def packed(zpos, group):
    first = jnp.where(zpos == 0, 0, jnp.where(zpos == 1, 40, jnp.where(zpos == 2, 72, 112)))
    second = jnp.where(zpos == 0, 0, jnp.where(zpos == 1, 32, jnp.where(zpos == 2, 72, 104)))
    return pl.multiple_of(jnp.where(group < 2, first, second), 8)


def cores_kernel(spot, att_t, cot, got, keep, *sends):
    group = spot[1]
    *sends, rows, total, pack = sends
    height = got.shape[1]
    made = part_rows(spot[0] % 2, att_t, cot, rows)
    for z in range(4):
        total[z * height : (z + 1) * height, :] = made[z] + got[z].astype(jnp.float32)
    for flip, out in enumerate((keep, *sends)):
        whose = group ^ flip
        for z in range(4):
            start = pl.multiple_of(z * height + cut(z, whose), 8)
            pack[pl.ds(packed(z, whose), PIECE), :] = total[pl.ds(start, PIECE), :]
        out[...] = pack[:height, :].astype(out.dtype)


def groups_kernel(spot, own, one, two, three, keep, *sends):
    zpos, group = spot[0] // 2, spot[1]
    *sends, total = sends
    height = own.shape[0]
    total[:height, :] = own[...] + sum(x[...].astype(jnp.float32) for x in (one, two, three))
    total[height:, :] = jnp.zeros((total.shape[0] - height, total.shape[1]), jnp.float32)
    for flip, out in enumerate((keep, *sends)):
        out[...] = total[pl.ds(packed(zpos ^ flip, group), PIECE), :].astype(out.dtype)


def chips_kernel(own, one, two, three, out):
    total = own[...] + sum(x[...].astype(jnp.float32) for x in (one, two, three))
    out[...] = total.astype(jnp.bfloat16)


def gather_kernel(spot, own, one, two, three, out, held, rows):
    zpos, group = spot[0] // 2, spot[1]
    for flip, value in enumerate((own, one, two, three)):
        held[group ^ flip] = value[...].astype(jnp.float32)
    for whose in range(4):
        rows[pl.ds(cut(zpos, whose), PIECE), :] = held[whose]
    out[...] = rows[: out.shape[0], :]


def final_kernel(spot, own, sib, rows, mixed, grad, out, sems):
    core = spot[0] % 2
    here, there = pl.ds(2 * core, 2), pl.ds(2 * (1 - core), 2)
    moves = [(rows, out)]
    for base, made in ((0, mixed), (2, grad)):
        moves.append((own.at[base : base + 2], made.at[here]))
        moves.append((sib.at[base : base + 2], made.at[there]))
    copies = [pltpu.make_async_copy(x, y, sems.at[i]) for i, (x, y) in enumerate(moves)]
    for copy in copies:
        copy.start()
    for copy in copies:
        copy.wait()


def after(later, earlier):
    return lax.optimization_barrier((later, earlier))


def swap_near(value):
    return swap(value, "seq", 2)


def swap_far(value):
    return lax.ppermute(value, "seq", [(2, 4), (4, 2), (3, 5), (5, 3)])


def clip_body(latents, in_weight, out_weight, cotangent, clip_lengths):
    width = latents.shape[3]
    rows = INNER // 8
    wide = jnp.float32
    place = jnp.arange(2 + clip_lengths.shape[1], dtype=jnp.int32)
    spot = jnp.where(place == 0, lax.axis_index("seq"), jnp.where(place == 1, lax.axis_index("dp"), 0))
    spot = spot + jnp.pad(clip_lengths[0], (2, 0))
    heads = jnp.asarray(np.arange(INNER) // HD == np.arange(HEADS)[:, None], jnp.bfloat16)
    lat = latents.reshape(4, ROWS, width)
    cot = cotangent.reshape(4, ROWS, width)

    bf16 = jnp.bfloat16
    four, two, eight = shaped((4, ROWS, width)), shaped((2, ROWS, width)), shaped((8, ROWS, INNER))

    def pick(own, sib):
        near, far, both = call(pick_kernel, [spot], [own, sib], [two, two, four], flops=4 * 10**9)
        return swap_near(near), swap_far(far), both

    lat_sib, cot_sib = swap(lat, "seq", 1), swap(cot, "seq", 1)
    (lat_own,) = call(own_kernel, [spot], [lat], [two], flops=4 * 10**9)
    lat_near, lat_far, lat_ab = pick(lat_own, lat_sib)
    cot, lat_ab = after(cot, lat_ab)
    cot_near, cot_far, cot_ab = pick(cot, cot_sib)
    (qkv_ab,) = call(
        early_kernel, [], [lat_ab, in_weight], [shaped((4, ROWS, 3 * INNER))], limit=16, flops=27 * 10**8
    )
    pairs = 2 * PAIRS * ROWS
    products, columns = ((pairs, INNER), bf16), ((pairs, HEADS), bf16)
    qkv, att, probs, wides = call(
        forward_kernel, [spot], [lat_near, lat_far, in_weight, qkv_ab, heads],
        [shaped((8, ROWS, 3 * INNER)), eight, shaped((HEADS, pairs), wide), shaped((pairs, INNER))],
        [((4, ROWS, width), bf16), products, columns], limit=24, flops=8 * 10**9,
    )
    part_scr = ((4 * rows, 8 * ROWS), bf16)
    other, att_t, cot_all = call(
        part_kernel, [spot], [att, cot_ab, cot_near, cot_far],
        [shaped((4, rows, width)), shaped((INNER, 8 * ROWS)), eight], [part_scr],
        limit=16, flops=7 * 10**8,
    )
    got = swap(other, "seq", 1)
    cot_all, other = after(cot_all, other)
    (ga,) = call(grad_att_kernel, [], [cot_all, out_weight], [eight], limit=16, flops=14 * 10**8)
    att_t, ga = after(att_t, ga)
    part, piece = (rows, width), (PIECE, width)
    keep, *sends = call(
        cores_kernel, [spot], [att_t, cot_all, got], [shaped(part, wide)] + [shaped(part)] * 3,
        [part_scr, ((4 * rows, width), wide), ((rows + 8, width), wide)], limit=16, flops=7 * 10**8,
    )
    att, sends = after(att, sends)
    sends = [swap(x, "dp", flip) for flip, x in enumerate(sends, 1)]
    mixed = call(mix_kernel, [], [att, out_weight], [four, two, two], limit=16, size=10**3)
    qkv, mixed = after(qkv, mixed)
    mixed = [mixed[0], swap_near(mixed[1]), swap_far(mixed[2])]
    (d_all,) = call(
        backward_kernel, [spot], [ga, qkv, probs, wides, heads], [shaped((8, ROWS, 3 * INNER))],
        [products, ((HEADS, pairs), wide), columns], limit=24, size=10**3,
    )
    theirs = functools.partial(latents_kernel, first=4)
    grad = call(theirs, [], [d_all, in_weight], [two, two], limit=16, size=10**3)
    keep, (grad, mixed) = after(keep, (grad, mixed))
    keep, *sends = call(
        groups_kernel, [spot], [keep, *sends], [shaped(piece, wide)] + [shaped(piece)] * 3,
        [((rows + 8, width), wide)],
    )
    sends = [swap(x, "seq", 2 * flip) for flip, x in enumerate(sends, 1)]
    grad, sends[0] = after(grad, sends[0])
    d_all, grad = after(d_all, grad)
    ours = functools.partial(latents_kernel, first=0)
    (own,) = call(ours, [], [d_all, in_weight], [four], limit=16, flops=8 * 10**9)
    grad = [own, swap_near(grad[0]), swap_far(grad[1])]
    keep, grad[0] = after(keep, grad[0])
    (last,) = call(chips_kernel, [], [keep, *sends], [shaped(piece)])
    grad[0], last = after(grad[0], last)
    others = [swap(last, "dp", flip) for flip in (1, 2, 3)]
    own, sib = call(settle_kernel, [spot], [*mixed, *grad], [four, four], [((8, ROWS, width), bf16)])
    (out_grad,) = call(
        gather_kernel, [spot], [last, *others], [shaped(part, wide)],
        [((4, *piece), wide), ((rows + 8, width), wide)], flops=8 * 10**9,
    )
    mixed, grad, out_grad = call(
        final_kernel, [spot], [own, swap(sib, "seq", 1), out_grad],
        [four, four, shaped((rows, width), wide)], [pltpu.SemaphoreType.DMA((5,))], to_hbm=True,
    )
    return mixed.reshape(latents.shape), grad.reshape(latents.shape), out_grad


def body(latents, *others):
    frames, patches = latents.shape[1] * lax.axis_size("seq"), latents.shape[2]
    small = (lax.axis_size("dp"), lax.axis_size("seq"), frames, patches) == (4, 8, 8, 4 * ROWS)
    return (clip_body if small else patch_body)(latents, *others)


def solution(mesh):
    placed = (P("dp", "seq", None, None), P(), P(), P("dp", "seq", None, None), P("dp", None))
    return jax.shard_map(
        body,
        mesh=mesh,
        in_specs=placed,
        out_specs=(P("dp", "seq", None, None), P("dp", "seq", None, None), P("seq", None)),
        check_vma=False,
    )
```

profile of v0, /device:TPU:0, one launch (start us, length us, event | category | flops | bytes accessed | tf_op | source)
XLA Modules:
  0.0 73.5 jit_solution(15579531172488882690)
XLA Ops:
  0.6 0.5 collective-permute-start
  1.1 0.1 collective-permute-start.3
  1.2 0.7 fusion.spot
  2.0 1.1 %copy-done.2 = bf16[1,1,256,1152]{3,2,1,0:T(8,128)(2,1)S(1)} copy-done((bf16[1,1,256,1152]{3,2,1,0:T(8,128)(2,1)S(1)}, bf16[1,1,256,1152]{3,2,1,0:T(8,128)(2,1)}, u32[]{:S(2)}) %copy-start.2) | copy-done | bytes 589848
  3.0 0.6 shard_map.85.own
  3.6 0.0 copy-start.3
  3.6 0.6 shard_map.86
  4.3 3.1 %collective-permute-start.1 = (bf16[2,64,1152]{2,1,0:T(8,128)(2,1)S(1)}, bf16[2,64,1152]{2,1,0:T(8,128)(2,1)S(1)}, u32[]{:S(2)}, u32[]{:S(2)}) collective-permute-start(bf16[2,64,1152]{2,1,0:T(8,128)(2,1)S(1)} %get-tuple-element.63), channel_id=1, source_target_pairs={{0,2},{1,3},{2,0},{3,1},{4,6},{5,7},{6,4},{7,5},{8,10},{9,11},{10,... | collective-permute-start | bytes 884744 | tf_op jit(solution)/shard_map/ppermute | solution.py:44
  7.3 0.8 %collective-permute-start.2 = (bf16[2,64,1152]{2,1,0:T(8,128)(2,1)S(1)}, bf16[2,64,1152]{2,1,0:T(8,128)(2,1)S(1)}, u32[]{:S(2)}, u32[]{:S(2)}) collective-permute-start(bf16[2,64,1152]{2,1,0:T(8,128)(2,1)S(1)} %get-tuple-element.64), channel_id=1, source_target_pairs={{2,4},{4,2},{3,5},{5,3},{10,12},{12,10},{11,13},{13,11},{18,20},{2... | collective-permute-start | bytes 884744 | tf_op jit(solution)/shard_map/ppermute | solution.py:451
  8.2 0.6 shard_map.89
  8.8 4.6 %collective-permute-start.4 = (bf16[2,64,1152]{2,1,0:T(8,128)(2,1)S(1)}, bf16[2,64,1152]{2,1,0:T(8,128)(2,1)S(1)}, u32[]{:S(2)}, u32[]{:S(2)}) collective-permute-start(bf16[2,64,1152]{2,1,0:T(8,128)(2,1)S(1)} %get-tuple-element.70), channel_id=1, source_target_pairs={{0,2},{1,3},{2,0},{3,1},{4,6},{5,7},{6,4},{7,5},{8,10},{9,11},{10,... | collective-permute-start | bytes 884744 | tf_op jit(solution)/shard_map/ppermute | solution.py:44
  13.4 0.8 %collective-permute-start.5 = (bf16[2,64,1152]{2,1,0:T(8,128)(2,1)S(1)}, bf16[2,64,1152]{2,1,0:T(8,128)(2,1)S(1)}, u32[]{:S(2)}, u32[]{:S(2)}) collective-permute-start(bf16[2,64,1152]{2,1,0:T(8,128)(2,1)S(1)} %get-tuple-element.71), channel_id=1, source_target_pairs={{2,4},{4,2},{3,5},{5,3},{10,12},{12,10},{11,13},{13,11},{18,20},{2... | collective-permute-start | bytes 884744 | tf_op jit(solution)/shard_map/ppermute | solution.py:451
  14.2 2.7 %shard_map.87.ab_ref = bf16[4,64,3456]{2,1,0:T(8,128)(2,1)S(1)} custom-call(bf16[4,64,1152]{2,1,0:T(8,128)(2,1)S(1)} %get-tuple-element.66.lat_ab, bf16[1152,3456]{1,0:T(8,128)(2,1)S(1)} %bitcast.6), custom_call_target="tpu_custom_call" | custom-call | flops 2700000000 | bytes 10321920 | tf_op jit(solution)/shard_map/pallas_call | solution.py:134
  17.0 0.0 copy-start
  17.0 6.7 %shard_map.88 = (bf16[8,64,3456]{2,1,0:T(8,128)(2,1)S(1)}, bf16[8,64,1152]{2,1,0:T(8,128)(2,1)S(1)}, f32[16,2048]{1,0:T(8,128)S(1)}, bf16[2048,1152]{1,0:T(8,128)(2,1)S(1)}) custom-call(s32[6]{0:T(128)S(1)} %fusion.spot, bf16[2,64,1152]{2,1,0:T(8,128)(2,1)S(1)} %collective-permute-done.1.near, bf16[2,64,1152]{2,1,0:T(8,128)(2,1)S(1)} %collective-permute-done.2.far, ...), custom_call_target="tpu_custom_call" | custom-call | flops 8000000000 | bytes 19927040 | tf_op jit(solution)/shard_map/pallas_call | solution.py:134
  23.7 1.7 %shard_map.90 = (bf16[4,144,1152]{2,1,0:T(8,128)(2,1)S(1)}, bf16[1152,512]{1,0:T(8,128)(2,1)S(1)}, bf16[8,64,1152]{2,1,0:T(8,128)(2,1)S(1)}) custom-call(s32[6]{0:T(128)S(1)} %fusion.spot, bf16[8,64,1152]{2,1,0:T(8,128)(2,1)S(1)} %get-tuple-element.83.att_ref, bf16[4,64,1152]{2,1,0:T(8,128)(2,1)S(1)} %get-tuple-element.69.ab_ref, ...), custom_call_target="tpu_custom_call" | custom-call | flops 700000000 | bytes 6045696 | tf_op jit(solution)/shard_map/pallas_call | solution.py:134
  25.5 0.1 collective-permute-start.6
  25.6 1.9 %shard_map.91.ga_ref = bf16[8,64,1152]{2,1,0:T(8,128)(2,1)S(1)} custom-call(bf16[8,64,1152]{2,1,0:T(8,128)(2,1)S(1)} %get-tuple-element.75.cot, bf16[1152,1152]{1,0:T(8,128)(2,1)S(1)} %copy-done), custom_call_target="tpu_custom_call" | custom-call | flops 1400000000 | bytes 5013504 | tf_op jit(solution)/shard_map/pallas_call | solution.py:134
  27.5 1.1 %collective-permute-done.6.got = bf16[4,144,1152]{2,1,0:T(8,128)(2,1)S(1)} collective-permute-done((bf16[4,144,1152]{2,1,0:T(8,128)(2,1)S(1)}, bf16[4,144,1152]{2,1,0:T(8,128)(2,1)S(1)}, u32[]{:S(2)}, u32[]{:S(2)}) %collective-permute-start.6) | collective-permute-done | bytes 1327136 | tf_op jit(solution)/shard_map/ppermute | solution.py:44
  28.6 1.8 %shard_map.92 = (f32[144,1152]{1,0:T(8,128)S(1)}, bf16[144,1152]{1,0:T(8,128)(2,1)S(1)}, bf16[144,1152]{1,0:T(8,128)(2,1)S(1)}, bf16[144,1152]{1,0:T(8,128)(2,1)S(1)}) custom-call(s32[6]{0:T(128)S(1)} %fusion.spot, bf16[1152,512]{1,0:T(8,128)(2,1)S(1)} %get-tuple-element.76.att_t, bf16[8,64,1152]{2,1,0:T(8,128)(2,1)S(1)} %get-tuple-element.75.cot, ...), custom_call_target="tpu_custom_call" | custom-call | flops 700000000 | bytes 5345280 | tf_op jit(solution)/shard_map/pallas_call | solution.py:134
  30.4 1.6 %collective-permute-start.9 = (bf16[144,1152]{1,0:T(8,128)(2,1)S(1)}, bf16[144,1152]{1,0:T(8,128)(2,1)S(1)}, u32[]{:S(2)}, u32[]{:S(2)}) collective-permute-start(bf16[144,1152]{1,0:T(8,128)(2,1)S(1)} %get-tuple-element.99), channel_id=1, source_target_pairs={{0,8},{8,0},{16,24},{24,16},{1,9},{9,1},{17,25},{25,17},{2,10},{10... | collective-permute-start | bytes 995336 | tf_op jit(solution)/shard_map/ppermute | solution.py:44
  31.9 1.5 %collective-permute-start.10 = (bf16[144,1152]{1,0:T(8,128)(2,1)S(1)}, bf16[144,1152]{1,0:T(8,128)(2,1)S(1)}, u32[]{:S(2)}, u32[]{:S(2)}) collective-permute-start(bf16[144,1152]{1,0:T(8,128)(2,1)S(1)} %get-tuple-element.100), channel_id=1, source_target_pairs={{0,16},{8,24},{16,0},{24,8},{1,17},{9,25},{17,1},{25,9},{2,18},{10... | collective-permute-start | bytes 995336 | tf_op jit(solution)/shard_map/ppermute | solution.py:44
  33.4 0.5 collective-permute-start.11
  33.9 2.0 %shard_map.93 = (bf16[4,64,1152]{2,1,0:T(8,128)(2,1)S(1)}, bf16[2,64,1152]{2,1,0:T(8,128)(2,1)S(1)}, bf16[2,64,1152]{2,1,0:T(8,128)(2,1)S(1)}) custom-call(bf16[8,64,1152]{2,1,0:T(8,128)(2,1)S(1)} %get-tuple-element.83.att_ref, bf16[1152,1152]{1,0:T(8,128)(2,1)S(1)} %copy-done), custom_call_target="tpu_custom_call" | custom-call | flops 1000000 | bytes 1000 | tf_op jit(solution)/shard_map/pallas_call | solution.py:134
  36.0 3.7 %collective-permute-start.7 = (bf16[2,64,1152]{2,1,0:T(8,128)(2,1)S(1)}, bf16[2,64,1152]{2,1,0:T(8,128)(2,1)S(1)}, u32[]{:S(2)}, u32[]{:S(2)}) collective-permute-start(bf16[2,64,1152]{2,1,0:T(8,128)(2,1)S(1)} %get-tuple-element.93), channel_id=1, source_target_pairs={{0,2},{1,3},{2,0},{3,1},{4,6},{5,7},{6,4},{7,5},{8,10},{9,11},{10,... | collective-permute-start | bytes 884744 | tf_op jit(solution)/shard_map/ppermute | solution.py:44
  39.7 0.7 collective-permute-start.8
  40.4 5.6 %shard_map.94.d_ref = bf16[8,64,3456]{2,1,0:T(8,128)(2,1)S(1)} custom-call(s32[6]{0:T(128)S(1)} %fusion.spot, bf16[8,64,1152]{2,1,0:T(8,128)(2,1)S(1)} %shard_map.91.ga_ref, bf16[8,64,3456]{2,1,0:T(8,128)(2,1)S(1)} %get-tuple-element.87.qkv_ref, f32[16,2048]{1,0:T(8,128)S(1)} %get-tuple-element.88.p_ref, bf16[2048,1152]{1,0:T(8,128)(2,1)S(1)} %get-tuple-element.89.wide_ref, ...), custom_call_target="tpu_custom_call" | custom-call | flops 1000000 | bytes 1000 | tf_op jit(solution)/shard_map/pallas_call | solution.py:134
  46.0 3.0 %shard_map.95 = (bf16[2,64,1152]{2,1,0:T(8,128)(2,1)S(1)}, bf16[2,64,1152]{2,1,0:T(8,128)(2,1)S(1)}) custom-call(bf16[8,64,3456]{2,1,0:T(8,128)(2,1)S(1)} %shard_map.94.d_ref, bf16[1152,3456]{1,0:T(8,128)(2,1)S(1)} %bitcast.6), custom_call_target="tpu_custom_call" | custom-call | flops 1000000 | bytes 1000 | tf_op jit(solution)/shard_map/pallas_call | solution.py:134
  49.0 0.8 %shard_map.96 = (f32[40,1152]{1,0:T(8,128)S(1)}, bf16[40,1152]{1,0:T(8,128)(2,1)S(1)}, bf16[40,1152]{1,0:T(8,128)(2,1)S(1)}, bf16[40,1152]{1,0:T(8,128)(2,1)S(1)}) custom-call(s32[6]{0:T(128)S(1)} %fusion.spot, f32[144,1152]{1,0:T(8,128)S(1)} %get-tuple-element.98.own, bf16[144,1152]{1,0:T(8,128)(2,1)S(1)} %collective-permute-done.9.one, ...), custom_call_target="tpu_custom_call" | custom-call | flops 1000000 | bytes 2119680 | tf_op jit(solution)/shard_map/pallas_call | solution.py:134
  49.8 3.3 %collective-permute-start.12 = (bf16[40,1152]{1,0:T(8,128)(2,1)S(1)}, bf16[40,1152]{1,0:T(8,128)(2,1)S(1)}, u32[]{:S(2)}, u32[]{:S(2)}) collective-permute-start(bf16[40,1152]{1,0:T(8,128)(2,1)S(1)} %get-tuple-element.105), channel_id=1, source_target_pairs={{0,2},{1,3},{2,0},{3,1},{4,6},{5,7},{6,4},{7,5},{8,10},{9,11},{10,... | collective-permute-start | bytes 276488 | tf_op jit(solution)/shard_map/ppermute | solution.py:44
  53.2 1.4 %collective-permute-start.13 = (bf16[40,1152]{1,0:T(8,128)(2,1)S(1)}, bf16[40,1152]{1,0:T(8,128)(2,1)S(1)}, u32[]{:S(2)}, u32[]{:S(2)}) collective-permute-start(bf16[40,1152]{1,0:T(8,128)(2,1)S(1)} %get-tuple-element.112), channel_id=1, source_target_pairs={{0,4},{1,5},{2,6},{3,7},{4,0},{5,1},{6,2},{7,3},{8,12},{9,13},{10,... | collective-permute-start | bytes 276488 | tf_op jit(solution)/shard_map/ppermute | solution.py:44
  54.6 1.4 %collective-permute-start.14 = (bf16[40,1152]{1,0:T(8,128)(2,1)S(1)}, bf16[40,1152]{1,0:T(8,128)(2,1)S(1)}, u32[]{:S(2)}, u32[]{:S(2)}) collective-permute-start(bf16[40,1152]{1,0:T(8,128)(2,1)S(1)} %get-tuple-element.113), channel_id=1, source_target_pairs={{0,6},{1,7},{2,4},{3,5},{4,2},{5,3},{6,0},{7,1},{8,14},{9,15},{10,... | collective-permute-start | bytes 276488 | tf_op jit(solution)/shard_map/ppermute | solution.py:44
  56.0 0.7 collective-permute-done.12.one
  56.7 1.9 %collective-permute-start.15 = (bf16[2,64,1152]{2,1,0:T(8,128)(2,1)S(1)}, bf16[2,64,1152]{2,1,0:T(8,128)(2,1)S(1)}, u32[]{:S(2)}, u32[]{:S(2)}) collective-permute-start(bf16[2,64,1152]{2,1,0:T(8,128)(2,1)S(1)} %get-tuple-element.115), channel_id=1, source_target_pairs={{0,2},{1,3},{2,0},{3,1},{4,6},{5,7},{6,4},{7,5},{8,10},{9,11},{10,... | collective-permute-start | bytes 884744 | tf_op jit(solution)/shard_map/ppermute | solution.py:44
  58.6 0.7 collective-permute-start.16
  59.3 3.0 %shard_map.97.refs_3_ = bf16[4,64,1152]{2,1,0:T(8,128)(2,1)S(1)} custom-call(bf16[8,64,3456]{2,1,0:T(8,128)(2,1)S(1)} %shard_map.94.d_ref, bf16[1152,3456]{1,0:T(8,128)(2,1)S(1)} %bitcast.6), custom_call_target="tpu_custom_call" | custom-call | flops 8000000000 | bytes 12091392 | tf_op jit(solution)/shard_map/pallas_call | solution.py:134
  62.3 1.1 %collective-permute-done.14.three = bf16[40,1152]{1,0:T(8,128)(2,1)S(1)} collective-permute-done((bf16[40,1152]{1,0:T(8,128)(2,1)S(1)}, bf16[40,1152]{1,0:T(8,128)(2,1)S(1)}, u32[]{:S(2)}, u32[]{:S(2)}) %collective-permute-start.14) | collective-permute-done | bytes 92192 | tf_op jit(solution)/shard_map/ppermute | solution.py:44
  63.3 0.1 shard_map.98.own
  63.4 1.6 %collective-permute-start.20 = (bf16[40,1152]{1,0:T(8,128)(2,1)S(1)}, bf16[40,1152]{1,0:T(8,128)(2,1)S(1)}, u32[]{:S(2)}, u32[]{:S(2)}) collective-permute-start(bf16[40,1152]{1,0:T(8,128)(2,1)S(1)} %shard_map.98.own), channel_id=1, source_target_pairs={{0,24},{8,16},{16,8},{24,0},{1,25},{9,17},{17,9},{25,1},{2,26},{10... | collective-permute-start | bytes 276488 | tf_op jit(solution)/shard_map/ppermute | solution.py:44
  65.0 1.3 %collective-permute-start.19 = (bf16[40,1152]{1,0:T(8,128)(2,1)S(1)}, bf16[40,1152]{1,0:T(8,128)(2,1)S(1)}, u32[]{:S(2)}, u32[]{:S(2)}) collective-permute-start(bf16[40,1152]{1,0:T(8,128)(2,1)S(1)} %shard_map.98.own), channel_id=1, source_target_pairs={{0,16},{8,24},{16,0},{24,8},{1,17},{9,25},{17,1},{25,9},{2,18},{10... | collective-permute-start | bytes 276488 | tf_op jit(solution)/shard_map/ppermute | solution.py:44
  66.3 0.6 collective-permute-start.18
  67.0 0.8 %shard_map.99 = (bf16[4,64,1152]{2,1,0:T(8,128)(2,1)S(1)}, bf16[4,64,1152]{2,1,0:T(8,128)(2,1)S(1)}) custom-call(s32[6]{0:T(128)S(1)} %fusion.spot, bf16[4,64,1152]{2,1,0:T(8,128)(2,1)S(1)} %get-tuple-element.95.refs_0_, bf16[2,64,1152]{2,1,0:T(8,128)(2,1)S(1)} %collective-permute-done.7.refs_1_, bf16[2,64,1152]{2,1,0:T(8,128)(2,1)S(1)} %collective-permute-done.8.refs_2_, ...), custom_call_target="tpu_custom_call" | custom-call | flops 1000000 | bytes 3538944 | tf_op jit(solution)/shard_map/pallas_call | solution.py:134
  67.8 0.1 collective-permute-start.17
  67.9 1.1 %collective-permute-done.20.three = bf16[40,1152]{1,0:T(8,128)(2,1)S(1)} collective-permute-done((bf16[40,1152]{1,0:T(8,128)(2,1)S(1)}, bf16[40,1152]{1,0:T(8,128)(2,1)S(1)}, u32[]{:S(2)}, u32[]{:S(2)}) %collective-permute-start.20) | collective-permute-done | bytes 92192 | tf_op jit(solution)/shard_map/ppermute | solution.py:44
  69.0 0.9 %collective-permute-done.19.two = bf16[40,1152]{1,0:T(8,128)(2,1)S(1)} collective-permute-done((bf16[40,1152]{1,0:T(8,128)(2,1)S(1)}, bf16[40,1152]{1,0:T(8,128)(2,1)S(1)}, u32[]{:S(2)}, u32[]{:S(2)}) %collective-permute-start.19) | collective-permute-done | bytes 92192 | tf_op jit(solution)/shard_map/ppermute | solution.py:44
  69.9 1.0 %collective-permute-done.18.one = bf16[40,1152]{1,0:T(8,128)(2,1)S(1)} collective-permute-done((bf16[40,1152]{1,0:T(8,128)(2,1)S(1)}, bf16[40,1152]{1,0:T(8,128)(2,1)S(1)}, u32[]{:S(2)}, u32[]{:S(2)}) %collective-permute-start.18) | collective-permute-done | bytes 92192 | tf_op jit(solution)/shard_map/ppermute | solution.py:44
  70.9 0.7 shard_map.100.rows
  71.6 1.8 %shard_map.101 = (bf16[4,64,1152]{2,1,0:T(8,128)(2,1)}, bf16[4,64,1152]{2,1,0:T(8,128)(2,1)}, f32[144,1152]{1,0:T(8,128)}) custom-call(s32[6]{0:T(128)S(1)} %fusion.spot, bf16[4,64,1152]{2,1,0:T(8,128)(2,1)S(1)} %get-tuple-element.117.own, bf16[4,64,1152]{2,1,0:T(8,128)(2,1)S(1)} %collective-permute-done.17.sib, f32[144,1152]{1,0:T(8,128)S(1)} %shard_map.100.rows), custom_call_target="tpu_custom_call" | custom-call | flops 1000000 | bytes 3686400 | tf_op jit(solution)/shard_map/pallas_call | solution.py:134
  (25 shorter events, 0.1 us)
Async XLA Ops:
  0.6 3.0 %collective-permute-start = (bf16[4,64,1152]{2,1,0:T(8,128)(2,1)}, bf16[4,64,1152]{2,1,0:T(8,128)(2,1)S(1)}, u32[]{:S(2)}, u32[]{:S(2)}) collective-permute-start(bf16[4,64,1152]{2,1,0:T(8,128)(2,1)} %bitcast.7), channel_id=1, source_target_pairs={{0,1},{1,0},{2,3},{3,2},{4,5},{5,4},{6,7},{7,6},{8,9},{9,8},{10,11... | collective-permute-start | bytes 1769480 | tf_op jit(solution)/shard_map/ppermute | solution.py:44
  1.1 7.0 %collective-permute-start.3 = (bf16[4,64,1152]{2,1,0:T(8,128)(2,1)}, bf16[4,64,1152]{2,1,0:T(8,128)(2,1)S(1)}, u32[]{:S(2)}, u32[]{:S(2)}) collective-permute-start(bf16[4,64,1152]{2,1,0:T(8,128)(2,1)} %bitcast.9), channel_id=1, source_target_pairs={{0,1},{1,0},{2,3},{3,2},{4,5},{5,4},{6,7},{7,6},{8,9},{9,8},{10,11... | collective-permute-start | bytes 1769480 | tf_op jit(solution)/shard_map/ppermute | solution.py:44
  2.0 1.1 %copy-start.2 = (bf16[1,1,256,1152]{3,2,1,0:T(8,128)(2,1)S(1)}, bf16[1,1,256,1152]{3,2,1,0:T(8,128)(2,1)}, u32[]{:S(2)}) copy-start(bf16[1,1,256,1152]{3,2,1,0:T(8,128)(2,1)} %param.6) | copy-start | bytes 1769476
  3.6 4.6 %copy-start.3 = (bf16[1,1,256,1152]{3,2,1,0:T(8,128)(2,1)S(1)}, bf16[1,1,256,1152]{3,2,1,0:T(8,128)(2,1)}, u32[]{:S(2)}) copy-start(bf16[1,1,256,1152]{3,2,1,0:T(8,128)(2,1)} %param.9) | copy-start | bytes 1769476
  4.3 12.7 %collective-permute-start.1 = (bf16[2,64,1152]{2,1,0:T(8,128)(2,1)S(1)}, bf16[2,64,1152]{2,1,0:T(8,128)(2,1)S(1)}, u32[]{:S(2)}, u32[]{:S(2)}) collective-permute-start(bf16[2,64,1152]{2,1,0:T(8,128)(2,1)S(1)} %get-tuple-element.63), channel_id=1, source_target_pairs={{0,2},{1,3},{2,0},{3,1},{4,6},{5,7},{6,4},{7,5},{8,10},{9,11},{10,... | collective-permute-start | bytes 884744 | tf_op jit(solution)/shard_map/ppermute | solution.py:44
  7.3 6.9 %slice-start = ((s8[7962624]{0:T(1024)(128)(4,1)}), s8[4194304]{0:T(1024)(128)(4,1)S(1)}, s32[]{:S(2)}) async-start(s8[7962624]{0:T(1024)(128)(4,1)} %bitcast.5), calls=%async_computation | async-start | bytes 8388608
  7.3 6.9 %slice-start.1 = ((s8[7962624]{0:T(1024)(128)(4,1)}), s8[3768320]{0:T(1024)(128)(4,1)S(1)}, s32[]{:S(2)}) async-start(s8[7962624]{0:T(1024)(128)(4,1)} %bitcast.5), calls=%async_computation.1 | async-start | bytes 7536640
  7.3 9.6 %collective-permute-start.2 = (bf16[2,64,1152]{2,1,0:T(8,128)(2,1)S(1)}, bf16[2,64,1152]{2,1,0:T(8,128)(2,1)S(1)}, u32[]{:S(2)}, u32[]{:S(2)}) collective-permute-start(bf16[2,64,1152]{2,1,0:T(8,128)(2,1)S(1)} %get-tuple-element.64), channel_id=1, source_target_pairs={{2,4},{4,2},{3,5},{5,3},{10,12},{12,10},{11,13},{13,11},{18,20},{2... | collective-permute-start | bytes 884744 | tf_op jit(solution)/shard_map/ppermute | solution.py:451
  8.8 14.9 %collective-permute-start.4 = (bf16[2,64,1152]{2,1,0:T(8,128)(2,1)S(1)}, bf16[2,64,1152]{2,1,0:T(8,128)(2,1)S(1)}, u32[]{:S(2)}, u32[]{:S(2)}) collective-permute-start(bf16[2,64,1152]{2,1,0:T(8,128)(2,1)S(1)} %get-tuple-element.70), channel_id=1, source_target_pairs={{0,2},{1,3},{2,0},{3,1},{4,6},{5,7},{6,4},{7,5},{8,10},{9,11},{10,... | collective-permute-start | bytes 884744 | tf_op jit(solution)/shard_map/ppermute | solution.py:44
  13.4 3.6 %copy-start.1 = (bf16[16,1152]{1,0:T(8,128)(2,1)S(1)}, bf16[16,1152]{1,0:T(8,128)(2,1)}, u32[]{:S(2)}) copy-start(bf16[16,1152]{1,0:T(8,128)(2,1)} %constant.15.clone.heads_ref) | copy-start | bytes 110596
  13.4 10.3 %collective-permute-start.5 = (bf16[2,64,1152]{2,1,0:T(8,128)(2,1)S(1)}, bf16[2,64,1152]{2,1,0:T(8,128)(2,1)S(1)}, u32[]{:S(2)}, u32[]{:S(2)}) collective-permute-start(bf16[2,64,1152]{2,1,0:T(8,128)(2,1)S(1)} %get-tuple-element.71), channel_id=1, source_target_pairs={{2,4},{4,2},{3,5},{5,3},{10,12},{12,10},{11,13},{13,11},{18,20},{2... | collective-permute-start | bytes 884744 | tf_op jit(solution)/shard_map/ppermute | solution.py:451
  17.0 8.6 %copy-start = (bf16[1152,1152]{1,0:T(8,128)(2,1)S(1)}, bf16[1152,1152]{1,0:T(8,128)(2,1)}, u32[]{:S(2)}) copy-start(bf16[1152,1152]{1,0:T(8,128)(2,1)} %w_ref.1) | copy-start | bytes 7962628
  25.5 3.1 %collective-permute-start.6 = (bf16[4,144,1152]{2,1,0:T(8,128)(2,1)S(1)}, bf16[4,144,1152]{2,1,0:T(8,128)(2,1)S(1)}, u32[]{:S(2)}, u32[]{:S(2)}) collective-permute-start(bf16[4,144,1152]{2,1,0:T(8,128)(2,1)S(1)} %get-tuple-element.74), channel_id=1, source_target_pairs={{0,1},{1,0},{2,3},{3,2},{4,5},{5,4},{6,7},{7,6},{8,9},{9,8},{10,11... | collective-permute-start | bytes 3981320 | tf_op jit(solution)/shard_map/ppermute | solution.py:44
  30.4 18.6 %collective-permute-start.9 = (bf16[144,1152]{1,0:T(8,128)(2,1)S(1)}, bf16[144,1152]{1,0:T(8,128)(2,1)S(1)}, u32[]{:S(2)}, u32[]{:S(2)}) collective-permute-start(bf16[144,1152]{1,0:T(8,128)(2,1)S(1)} %get-tuple-element.99), channel_id=1, source_target_pairs={{0,8},{8,0},{16,24},{24,16},{1,9},{9,1},{17,25},{25,17},{2,10},{10... | collective-permute-start | bytes 995336 | tf_op jit(solution)/shard_map/ppermute | solution.py:44
  31.9 17.1 %collective-permute-start.10 = (bf16[144,1152]{1,0:T(8,128)(2,1)S(1)}, bf16[144,1152]{1,0:T(8,128)(2,1)S(1)}, u32[]{:S(2)}, u32[]{:S(2)}) collective-permute-start(bf16[144,1152]{1,0:T(8,128)(2,1)S(1)} %get-tuple-element.100), channel_id=1, source_target_pairs={{0,16},{8,24},{16,0},{24,8},{1,17},{9,25},{17,1},{25,9},{2,18},{10... | collective-permute-start | bytes 995336 | tf_op jit(solution)/shard_map/ppermute | solution.py:44
  33.4 15.5 %collective-permute-start.11 = (bf16[144,1152]{1,0:T(8,128)(2,1)S(1)}, bf16[144,1152]{1,0:T(8,128)(2,1)S(1)}, u32[]{:S(2)}, u32[]{:S(2)}) collective-permute-start(bf16[144,1152]{1,0:T(8,128)(2,1)S(1)} %get-tuple-element.101), channel_id=1, source_target_pairs={{0,24},{8,16},{16,8},{24,0},{1,25},{9,17},{17,9},{25,1},{2,26},{10... | collective-permute-start | bytes 995336 | tf_op jit(solution)/shard_map/ppermute | solution.py:44
  36.0 13.0 %collective-permute-start.7 = (bf16[2,64,1152]{2,1,0:T(8,128)(2,1)S(1)}, bf16[2,64,1152]{2,1,0:T(8,128)(2,1)S(1)}, u32[]{:S(2)}, u32[]{:S(2)}) collective-permute-start(bf16[2,64,1152]{2,1,0:T(8,128)(2,1)S(1)} %get-tuple-element.93), channel_id=1, source_target_pairs={{0,2},{1,3},{2,0},{3,1},{4,6},{5,7},{6,4},{7,5},{8,10},{9,11},{10,... | collective-permute-start | bytes 884744 | tf_op jit(solution)/shard_map/ppermute | solution.py:44
  39.7 9.3 %collective-permute-start.8 = (bf16[2,64,1152]{2,1,0:T(8,128)(2,1)S(1)}, bf16[2,64,1152]{2,1,0:T(8,128)(2,1)S(1)}, u32[]{:S(2)}, u32[]{:S(2)}) collective-permute-start(bf16[2,64,1152]{2,1,0:T(8,128)(2,1)S(1)} %get-tuple-element.94), channel_id=1, source_target_pairs={{2,4},{4,2},{3,5},{5,3},{10,12},{12,10},{11,13},{13,11},{18,20},{2... | collective-permute-start | bytes 884744 | tf_op jit(solution)/shard_map/ppermute | solution.py:451
  49.8 6.8 %collective-permute-start.12 = (bf16[40,1152]{1,0:T(8,128)(2,1)S(1)}, bf16[40,1152]{1,0:T(8,128)(2,1)S(1)}, u32[]{:S(2)}, u32[]{:S(2)}) collective-permute-start(bf16[40,1152]{1,0:T(8,128)(2,1)S(1)} %get-tuple-element.105), channel_id=1, source_target_pairs={{0,2},{1,3},{2,0},{3,1},{4,6},{5,7},{6,4},{7,5},{8,10},{9,11},{10,... | collective-permute-start | bytes 276488 | tf_op jit(solution)/shard_map/ppermute | solution.py:44
  53.2 9.1 %collective-permute-start.13 = (bf16[40,1152]{1,0:T(8,128)(2,1)S(1)}, bf16[40,1152]{1,0:T(8,128)(2,1)S(1)}, u32[]{:S(2)}, u32[]{:S(2)}) collective-permute-start(bf16[40,1152]{1,0:T(8,128)(2,1)S(1)} %get-tuple-element.112), channel_id=1, source_target_pairs={{0,4},{1,5},{2,6},{3,7},{4,0},{5,1},{6,2},{7,3},{8,12},{9,13},{10,... | collective-permute-start | bytes 276488 | tf_op jit(solution)/shard_map/ppermute | solution.py:44
  54.6 8.8 %collective-permute-start.14 = (bf16[40,1152]{1,0:T(8,128)(2,1)S(1)}, bf16[40,1152]{1,0:T(8,128)(2,1)S(1)}, u32[]{:S(2)}, u32[]{:S(2)}) collective-permute-start(bf16[40,1152]{1,0:T(8,128)(2,1)S(1)} %get-tuple-element.113), channel_id=1, source_target_pairs={{0,6},{1,7},{2,4},{3,5},{4,2},{5,3},{6,0},{7,1},{8,14},{9,15},{10,... | collective-permute-start | bytes 276488 | tf_op jit(solution)/shard_map/ppermute | solution.py:44
  56.7 10.3 %collective-permute-start.15 = (bf16[2,64,1152]{2,1,0:T(8,128)(2,1)S(1)}, bf16[2,64,1152]{2,1,0:T(8,128)(2,1)S(1)}, u32[]{:S(2)}, u32[]{:S(2)}) collective-permute-start(bf16[2,64,1152]{2,1,0:T(8,128)(2,1)S(1)} %get-tuple-element.115), channel_id=1, source_target_pairs={{0,2},{1,3},{2,0},{3,1},{4,6},{5,7},{6,4},{7,5},{8,10},{9,11},{10,... | collective-permute-start | bytes 884744 | tf_op jit(solution)/shard_map/ppermute | solution.py:44
  58.6 8.4 %collective-permute-start.16 = (bf16[2,64,1152]{2,1,0:T(8,128)(2,1)S(1)}, bf16[2,64,1152]{2,1,0:T(8,128)(2,1)S(1)}, u32[]{:S(2)}, u32[]{:S(2)}) collective-permute-start(bf16[2,64,1152]{2,1,0:T(8,128)(2,1)S(1)} %get-tuple-element.116), channel_id=1, source_target_pairs={{2,4},{4,2},{3,5},{5,3},{10,12},{12,10},{11,13},{13,11},{18,20},{2... | collective-permute-start | bytes 884744 | tf_op jit(solution)/shard_map/ppermute | solution.py:451
  63.4 5.6 %collective-permute-start.20 = (bf16[40,1152]{1,0:T(8,128)(2,1)S(1)}, bf16[40,1152]{1,0:T(8,128)(2,1)S(1)}, u32[]{:S(2)}, u32[]{:S(2)}) collective-permute-start(bf16[40,1152]{1,0:T(8,128)(2,1)S(1)} %shard_map.98.own), channel_id=1, source_target_pairs={{0,24},{8,16},{16,8},{24,0},{1,25},{9,17},{17,9},{25,1},{2,26},{10... | collective-permute-start | bytes 276488 | tf_op jit(solution)/shard_map/ppermute | solution.py:44
  65.0 4.9 %collective-permute-start.19 = (bf16[40,1152]{1,0:T(8,128)(2,1)S(1)}, bf16[40,1152]{1,0:T(8,128)(2,1)S(1)}, u32[]{:S(2)}, u32[]{:S(2)}) collective-permute-start(bf16[40,1152]{1,0:T(8,128)(2,1)S(1)} %shard_map.98.own), channel_id=1, source_target_pairs={{0,16},{8,24},{16,0},{24,8},{1,17},{9,25},{17,1},{25,9},{2,18},{10... | collective-permute-start | bytes 276488 | tf_op jit(solution)/shard_map/ppermute | solution.py:44
  66.3 4.6 %collective-permute-start.18 = (bf16[40,1152]{1,0:T(8,128)(2,1)S(1)}, bf16[40,1152]{1,0:T(8,128)(2,1)S(1)}, u32[]{:S(2)}, u32[]{:S(2)}) collective-permute-start(bf16[40,1152]{1,0:T(8,128)(2,1)S(1)} %shard_map.98.own), channel_id=1, source_target_pairs={{0,8},{8,0},{16,24},{24,16},{1,9},{9,1},{17,25},{25,17},{2,10},{10... | collective-permute-start | bytes 276488 | tf_op jit(solution)/shard_map/ppermute | solution.py:44
  67.8 3.8 %collective-permute-start.17 = (bf16[4,64,1152]{2,1,0:T(8,128)(2,1)S(1)}, bf16[4,64,1152]{2,1,0:T(8,128)(2,1)S(1)}, u32[]{:S(2)}, u32[]{:S(2)}) collective-permute-start(bf16[4,64,1152]{2,1,0:T(8,128)(2,1)S(1)} %get-tuple-element.118), channel_id=1, source_target_pairs={{0,1},{1,0},{2,3},{3,2},{4,5},{5,4},{6,7},{7,6},{8,9},{9,8},{10,11... | collective-permute-start | bytes 1769480 | tf_op jit(solution)/shard_map/ppermute | solution.py:44
where the time goes:
time: 73.8 us; the launch traced here: 73.5 us
  Pallas kernels  34.4 us (47%)
  starting transfers between devices  30.2 us (41%)
  waiting for transfers between devices  5.95 us (8%)
  between operations  1.12 us (2%)
  local copies, waits for them, and re-layouts  1.09 us (1%)
    pallas_call x17, Pallas kernels, call(): pl.pallas_call(kernel, out_shape=list(outs), in_specs=[SMEM] * len(scalar...  34.4 us
    ppermute x17, starting transfers between devices, swap(): return lax.ppermute(value, axis, [(i, i ^ flip) for i in range(size)])  27.3 us
    ppermute x17, waiting for transfers between devices, swap(): return lax.ppermute(value, axis, [(i, i ^ flip) for i in range(size)])  5.94 us
    ppermute x4, starting transfers between devices, swap_far(): return lax.ppermute(value, 'seq', [(2, 4), (4, 2), (3, 5), (5, 3)])  2.93 us
  transfers between devices with their start and end apart: 21, of which 6 were waited for; matrix products, arithmetic and copies ran while one was open for 1% of the time, Pallas kernels for 38%

commit v1 on v0

--- a/solution.py
+++ b/solution.py
@@ -110,7 +110,7 @@
 PAIRS = 16
 TILE = 128
 INNER = HEADS * HD
-PIECE = 40
+PIECE = 41 * 8
 SMEM = pl.BlockSpec(memory_space=pltpu.SMEM)
 VMEM = pl.BlockSpec(memory_space=pltpu.VMEM)
 HBM = pl.BlockSpec(memory_space=pltpu.HBM)
@@ -129,7 +129,7 @@
     return value.reshape(value.shape[0] * ROWS, value.shape[2])
 
 
-def call(kernel, scalars, inputs, outs, scratch=(), limit=8, flops=10**6, to_hbm=False, size=None):
+def call(kernel, scalars, inputs, outs, scratch=(), limit=8, flops=10**6, to_hbm=False, size=None, same=None):
     size = size or sum(x.size * x.dtype.itemsize for x in (*inputs, *outs))
     return pl.pallas_call(
         kernel,
@@ -137,6 +137,7 @@
         in_specs=[SMEM] * len(scalars) + [VMEM] * len(inputs),
         out_specs=[HBM if to_hbm else VMEM] * len(outs),
         scratch_shapes=[x if hasattr(x, "memory_space") else pltpu.VMEM(*x) for x in scratch],
+        input_output_aliases={len(scalars) + same[0]: same[1]} if same else {},
         compiler_params=pltpu.CompilerParams(vmem_limit_bytes=limit << 20),
         cost_estimate=pl.CostEstimate(flops=flops, bytes_accessed=size, transcendentals=0),
     )(*scalars, *inputs)
@@ -186,11 +187,6 @@
     return blocks, [even | x for x in odd] if window == 0 else odd
 
 
-def own_kernel(spot, rows, mine):
-    for i in range(2):
-        mine[i] = rows[2 * (spot[0] % 2) + i]
-
-
 def pick_kernel(spot, own, sib, near, far, both):
     role = roles(spot)
     core, odd = role["core"], role["odd"]
@@ -208,7 +204,7 @@
     x = flat(lat_ab[...])
     for j in range(3):
         cols = slice(j * INNER, (j + 1) * INNER)
-        qkv_ref[:, :, cols] = dot(x, wi_ref[:, cols]).astype(jnp.bfloat16).reshape(4, ROWS, INNER)
+        qkv_ref[:4, :, cols] = dot(x, wi_ref[:, cols]).astype(jnp.bfloat16).reshape(4, ROWS, INNER)
 
 
 def pair(f, g, w=0, count=1):
@@ -221,12 +217,11 @@
 
 
 def forward_kernel(
-    spot, near, far, wi_ref, ab_ref, heads_ref, qkv_ref, att_ref, p_ref, wide_ref,
+    spot, near, far, wi_ref, _, heads_ref, qkv_ref, att_ref, p_ref, wide_ref,
     x_scr, hi_scr, w_scr,
 ):
     x_scr[:2] = near[...]
     x_scr[2:] = far[...]
-    qkv_ref[:4] = ab_ref[...]
     x = flat(x_scr[...])
     for j in range(3):
         cols = slice(j * INNER, (j + 1) * INNER)
@@ -374,41 +369,31 @@
             sib[base + i] = held[jnp.where(core == 0, where[2 + i], where[i])]
 
 
-def cut(zpos, group):
-    wide_first = jnp.where(group < 2, 40 * group, 32 * group + 16)
-    wide_last = jnp.where(group < 2, 32 * group, 40 * group - 16)
-    return pl.multiple_of(jnp.where(zpos % 2 == 0, wide_first, wide_last), 8)
-
-
-def packed(zpos, group):
-    first = jnp.where(zpos == 0, 0, jnp.where(zpos == 1, 40, jnp.where(zpos == 2, 72, 112)))
-    second = jnp.where(zpos == 0, 0, jnp.where(zpos == 1, 32, jnp.where(zpos == 2, 72, 104)))
-    return pl.multiple_of(jnp.where(group < 2, first, second), 8)
+def first_row(group, block):
+    return pl.multiple_of((group * 81 // 2 + block * 162) * 8, 8)
 
 
 def cores_kernel(spot, att_t, cot, got, keep, *sends):
     group = spot[1]
-    *sends, rows, total, pack = sends
-    height = got.shape[1]
+    *sends, rows, total = sends
+    height, width = got.shape[1:]
     made = part_rows(spot[0] % 2, att_t, cot, rows)
     for z in range(4):
-        total[z * height : (z + 1) * height, :] = made[z] + got[z].astype(jnp.float32)
+        block = made[z] + got[z].astype(jnp.float32)
+        for t in range(width // TILE):
+            start = (z * width // TILE + t) * height
+            total[start : start + height, :] = block[:, lanes(t)]
     for flip, out in enumerate((keep, *sends)):
-        whose = group ^ flip
         for z in range(4):
-            start = pl.multiple_of(z * height + cut(z, whose), 8)
-            pack[pl.ds(packed(z, whose), PIECE), :] = total[pl.ds(start, PIECE), :]
-        out[...] = pack[:height, :].astype(out.dtype)
+            out[z] = total[pl.ds(first_row(group ^ flip, z), PIECE), :].astype(out.dtype)
 
 
 def groups_kernel(spot, own, one, two, three, keep, *sends):
-    zpos, group = spot[0] // 2, spot[1]
+    zpos = spot[0] // 2
     *sends, total = sends
-    height = own.shape[0]
-    total[:height, :] = own[...] + sum(x[...].astype(jnp.float32) for x in (one, two, three))
-    total[height:, :] = jnp.zeros((total.shape[0] - height, total.shape[1]), jnp.float32)
+    total[...] = own[...] + sum(x[...].astype(jnp.float32) for x in (one, two, three))
     for flip, out in enumerate((keep, *sends)):
-        out[...] = total[pl.ds(packed(zpos ^ flip, group), PIECE), :].astype(out.dtype)
+        out[...] = total[zpos ^ flip].astype(out.dtype)
 
 
 def chips_kernel(own, one, two, three, out):
@@ -417,18 +402,19 @@
 
 
 def gather_kernel(spot, own, one, two, three, out, held, rows):
-    zpos, group = spot[0] // 2, spot[1]
     for flip, value in enumerate((own, one, two, three)):
-        held[group ^ flip] = value[...].astype(jnp.float32)
-    for whose in range(4):
-        rows[pl.ds(cut(zpos, whose), PIECE), :] = held[whose]
-    out[...] = rows[: out.shape[0], :]
+        held[spot[1] ^ flip] = value[...].astype(jnp.float32)
+    for group in range(4):
+        rows[pl.ds(first_row(group, 0), PIECE), :] = held[group]
+    height, width = out.shape
+    for t in range(width // TILE):
+        out[:, lanes(t)] = rows[t * height : (t + 1) * height, :]
 
 
 def final_kernel(spot, own, sib, rows, mixed, grad, out, sems):
     core = spot[0] % 2
     here, there = pl.ds(2 * core, 2), pl.ds(2 * (1 - core), 2)
-    moves = [(rows, out)]
+    moves = [(rows.at[i : i + 48], out.at[i : i + 48]) for i in range(0, out.shape[0], 48)]
     for base, made in ((0, mixed), (2, grad)):
         moves.append((own.at[base : base + 2], made.at[here]))
         moves.append((sib.at[base : base + 2], made.at[there]))
@@ -448,7 +434,9 @@
 
 
 def swap_far(value):
-    return lax.ppermute(value, "seq", [(2, 4), (4, 2), (3, 5), (5, 3)])
+    return lax.ppermute(
+        value, "seq", [(0, 0), (1, 1), (2, 4), (4, 2), (3, 5), (5, 3), (6, 6), (7, 7)]
+    )
 
 
 def clip_body(latents, in_weight, out_weight, cotangent, clip_lengths):
@@ -470,19 +458,19 @@
         return swap_near(near), swap_far(far), both
 
     lat_sib, cot_sib = swap(lat, "seq", 1), swap(cot, "seq", 1)
-    (lat_own,) = call(own_kernel, [spot], [lat], [two], flops=4 * 10**9)
+    lat_own = lax.dynamic_slice_in_dim(lat, 2 * (lax.axis_index("seq") % 2), 2, 0)
     lat_near, lat_far, lat_ab = pick(lat_own, lat_sib)
-    cot, lat_ab = after(cot, lat_ab)
+    (qkv_ab,) = call(
+        early_kernel, [], [lat_ab, in_weight], [shaped((8, ROWS, 3 * INNER))], limit=16, flops=27 * 10**8
+    )
+    cot_sib, qkv_ab = after(cot_sib, qkv_ab)
     cot_near, cot_far, cot_ab = pick(cot, cot_sib)
-    (qkv_ab,) = call(
-        early_kernel, [], [lat_ab, in_weight], [shaped((4, ROWS, 3 * INNER))], limit=16, flops=27 * 10**8
-    )
     pairs = 2 * PAIRS * ROWS
     products, columns = ((pairs, INNER), bf16), ((pairs, HEADS), bf16)
     qkv, att, probs, wides = call(
         forward_kernel, [spot], [lat_near, lat_far, in_weight, qkv_ab, heads],
         [shaped((8, ROWS, 3 * INNER)), eight, shaped((HEADS, pairs), wide), shaped((pairs, INNER))],
-        [((4, ROWS, width), bf16), products, columns], limit=24, flops=8 * 10**9,
+        [((4, ROWS, width), bf16), products, columns], limit=24, flops=8 * 10**9, same=(3, 0),
     )
     part_scr = ((4 * rows, 8 * ROWS), bf16)
     other, att_t, cot_all = call(
@@ -494,10 +482,11 @@
     cot_all, other = after(cot_all, other)
     (ga,) = call(grad_att_kernel, [], [cot_all, out_weight], [eight], limit=16, flops=14 * 10**8)
     att_t, ga = after(att_t, ga)
-    part, piece = (rows, width), (PIECE, width)
+    part, piece = (4, PIECE, TILE), (PIECE, TILE)
+    tiles = rows * width // TILE
     keep, *sends = call(
         cores_kernel, [spot], [att_t, cot_all, got], [shaped(part, wide)] + [shaped(part)] * 3,
-        [part_scr, ((4 * rows, width), wide), ((rows + 8, width), wide)], limit=16, flops=7 * 10**8,
+        [part_scr, ((4 * tiles, TILE), wide)], limit=16, flops=7 * 10**8,
     )
     att, sends = after(att, sends)
     sends = [swap(x, "dp", flip) for flip, x in enumerate(sends, 1)]
@@ -513,10 +502,10 @@
     keep, (grad, mixed) = after(keep, (grad, mixed))
     keep, *sends = call(
         groups_kernel, [spot], [keep, *sends], [shaped(piece, wide)] + [shaped(piece)] * 3,
-        [((rows + 8, width), wide)],
-    )
+        [(part, wide)],
+    )
+    grad, keep = after(grad, keep)
     sends = [swap(x, "seq", 2 * flip) for flip, x in enumerate(sends, 1)]
-    grad, sends[0] = after(grad, sends[0])
     d_all, grad = after(d_all, grad)
     ours = functools.partial(latents_kernel, first=0)
     (own,) = call(ours, [], [d_all, in_weight], [four], limit=16, flops=8 * 10**9)
@@ -527,12 +516,12 @@
     others = [swap(last, "dp", flip) for flip in (1, 2, 3)]
     own, sib = call(settle_kernel, [spot], [*mixed, *grad], [four, four], [((8, ROWS, width), bf16)])
     (out_grad,) = call(
-        gather_kernel, [spot], [last, *others], [shaped(part, wide)],
-        [((4, *piece), wide), ((rows + 8, width), wide)], flops=8 * 10**9,
+        gather_kernel, [spot], [last, *others], [shaped((rows, width), wide)],
+        [(part, wide), ((tiles, TILE), wide)], flops=8 * 10**9,
     )
     mixed, grad, out_grad = call(
         final_kernel, [spot], [own, swap(sib, "seq", 1), out_grad],
-        [four, four, shaped((rows, width), wide)], [pltpu.SemaphoreType.DMA((5,))], to_hbm=True,
+        [four, four, shaped((rows, width), wide)], [pltpu.SemaphoreType.DMA((7,))], to_hbm=True,
     )
     return mixed.reshape(latents.shape), grad.reshape(latents.shape), out_grad
 

time: 73.8 us -> 71.5 us (0.969)
  starting transfers between devices: 30.2 us -> 28 us
  Pallas kernels: 34.4 us -> 33.5 us
  waiting for transfers between devices: 5.95 us -> 6.75 us
    ppermute x17, starting transfers between devices: 27.3 us -> 24.8 us  [swap(): return lax.ppermute(value, axis, [(i, i ^ flip) for i in range(size)])]
    dynamic_slice x0 -> x1, local copies, waits for them, and re-layouts: none -> 1.13 us  [clip_body(): lax.dynamic_slice_in_dim(lat, 2 * (lax.axis_index('seq') % 2), 2, 0)]
    unnamed x12 -> x10, local copies, waits for them, and re-layouts: 1.09 us -> 0.03 us
    pallas_call x17 -> x16, Pallas kernels: 34.4 us -> 33.5 us  [call(): pl.pallas_call(kernel, out_shape=list(outs), in_specs=[SMEM] * len(scalar...]
    ppermute x17, waiting for transfers between devices: 5.94 us -> 6.74 us  [swap(): return lax.ppermute(value, axis, [(i, i ^ flip) for i in range(size)])]
  transfers between devices with their start and end apart: 21 -> 21, of which waited for: 6 -> 7; matrix products, arithmetic and copies ran while one was open for 1% -> 3% of each run, Pallas kernels for 38% -> 39%
where the time goes in v1:
time: 71.5 us; the launch traced here: 71.3 us
  Pallas kernels  33.5 us (47%)
  starting transfers between devices  28 us (39%)
  waiting for transfers between devices  6.75 us (9%)
  local copies, waits for them, and re-layouts  1.16 us (2%)
  between operations  1.12 us (2%)
  other arithmetic  0.73 us (1%)
    pallas_call x16, Pallas kernels, call(): pl.pallas_call(kernel, out_shape=list(outs), in_specs=[SMEM] * len(scalar...  33.5 us
    ppermute x17, starting transfers between devices, swap(): return lax.ppermute(value, axis, [(i, i ^ flip) for i in range(size)])  24.8 us
    ppermute x17, waiting for transfers between devices, swap(): return lax.ppermute(value, axis, [(i, i ^ flip) for i in range(size)])  6.74 us
    ppermute x4, starting transfers between devices, swap_far(): lax.ppermute(value, 'seq', [(0, 0), (1, 1), (2, 4), (4, 2), (3, 5), (5, 3...  3.2 us
  transfers between devices with their start and end apart: 21, of which 7 were waited for; matrix products, arithmetic and copies ran while one was open for 3% of the time, Pallas kernels for 39%

profile of v1, /device:TPU:0, one launch (start us, length us, event | category | flops | bytes accessed | tf_op | source)
XLA Modules:
  0.0 71.3 jit_solution(7510283485145057712)
XLA Ops:
  0.6 0.5 collective-permute-start
  1.1 0.1 collective-permute-start.3
  1.2 0.7 %fusion.spot = s32[6]{0:T(128)S(1)} fusion(s32[4]{0:T(128)} %bitcast.11, s32[]{:T(128)S(6)} %axis_index.29, s32[]{:T(128)S(6)} %axis_index.26), kind=kLoop, calls=%fused_computation.2 | loop fusion | flops 30 | bytes 48 | tf_op jit(solution)/shard_map/add | solution.py:448
  2.0 1.1 %constant_dynamic-slice_fusion.own = bf16[2,64,1152]{2,1,0:T(8,128)(2,1)S(1)} fusion(bf16[4,64,1152]{2,1,0:T(8,128)(2,1)} %bitcast.10, s32[]{:T(128)S(6)} %select_n.21), kind=kLoop, calls=%fused_computation.3 | loop fusion | bytes 589828 | tf_op jit(solution)/shard_map/dynamic_slice | solution.py:461
  3.1 0.0 slice-start.1
  3.1 0.6 shard_map.85
  3.8 3.1 %collective-permute-start.1 = (bf16[2,64,1152]{2,1,0:T(8,128)(2,1)S(1)}, bf16[2,64,1152]{2,1,0:T(8,128)(2,1)S(1)}, u32[]{:S(2)}, u32[]{:S(2)}) collective-permute-start(bf16[2,64,1152]{2,1,0:T(8,128)(2,1)S(1)} %get-tuple-element.63), channel_id=1, source_target_pairs={{0,2},{1,3},{2,0},{3,1},{4,6},{5,7},{6,4},{7,5},{8,10},{9,11},{10,... | collective-permute-start | bytes 884744 | tf_op jit(solution)/shard_map/ppermute | solution.py:44
  6.8 0.7 collective-permute-start.2
  7.5 0.0 copy-start.2
  7.6 2.7 %shard_map.86._ = bf16[8,64,3456]{2,1,0:T(8,128)(2,1)S(1)} custom-call(bf16[4,64,1152]{2,1,0:T(8,128)(2,1)S(1)} %get-tuple-element.65.lat_ab, bf16[1152,3456]{1,0:T(8,128)(2,1)S(1)} %bitcast.6), custom_call_target="tpu_custom_call" | custom-call | flops 2700000000 | bytes 12091392 | tf_op jit(solution)/shard_map/pallas_call | solution.py:134
  10.3 0.0 copy-start.1
  10.3 0.6 shard_map.88
  10.9 4.4 %collective-permute-start.4 = (bf16[2,64,1152]{2,1,0:T(8,128)(2,1)S(1)}, bf16[2,64,1152]{2,1,0:T(8,128)(2,1)S(1)}, u32[]{:S(2)}, u32[]{:S(2)}) collective-permute-start(bf16[2,64,1152]{2,1,0:T(8,128)(2,1)S(1)} %get-tuple-element.70), channel_id=1, source_target_pairs={{0,2},{1,3},{2,0},{3,1},{4,6},{5,7},{6,4},{7,5},{8,10},{9,11},{10,... | collective-permute-start | bytes 884744 | tf_op jit(solution)/shard_map/ppermute | solution.py:44
  15.4 1.0 %collective-permute-start.5 = (bf16[2,64,1152]{2,1,0:T(8,128)(2,1)S(1)}, bf16[2,64,1152]{2,1,0:T(8,128)(2,1)S(1)}, u32[]{:S(2)}, u32[]{:S(2)}) collective-permute-start(bf16[2,64,1152]{2,1,0:T(8,128)(2,1)S(1)} %get-tuple-element.71), channel_id=1, source_target_pairs={{0,0},{1,1},{2,4},{4,2},{3,5},{5,3},{6,6},{7,7},{8,8},{9,9},{10,12... | collective-permute-start | bytes 884744 | tf_op jit(solution)/shard_map/ppermute | solution.py:437
  16.4 6.7 %shard_map.87 = (bf16[8,64,3456]{2,1,0:T(8,128)(2,1)S(1)}, bf16[8,64,1152]{2,1,0:T(8,128)(2,1)S(1)}, f32[16,2048]{1,0:T(8,128)S(1)}, bf16[2048,1152]{1,0:T(8,128)(2,1)S(1)}) custom-call(s32[6]{0:T(128)S(1)} %fusion.spot, bf16[2,64,1152]{2,1,0:T(8,128)(2,1)S(1)} %collective-permute-done.1.near, ...), custom_call_target="tpu_custom_call", output_to_operand_aliasing={{0}: (4, {})} | custom-call | flops 8000000000 | bytes 21696512 | tf_op jit(solution)/shard_map/pallas_call | solution.py:134
  23.1 1.8 %shard_map.89 = (bf16[4,144,1152]{2,1,0:T(8,128)(2,1)S(1)}, bf16[1152,512]{1,0:T(8,128)(2,1)S(1)}, bf16[8,64,1152]{2,1,0:T(8,128)(2,1)S(1)}) custom-call(s32[6]{0:T(128)S(1)} %fusion.spot, bf16[8,64,1152]{2,1,0:T(8,128)(2,1)S(1)} %get-tuple-element.83.att_ref, bf16[4,64,1152]{2,1,0:T(8,128)(2,1)S(1)} %get-tuple-element.69.ab_ref, ...), custom_call_target="tpu_custom_call" | custom-call | flops 700000000 | bytes 6045696 | tf_op jit(solution)/shard_map/pallas_call | solution.py:134
  24.9 0.1 collective-permute-start.6
  25.0 1.9 %shard_map.90.ga_ref = bf16[8,64,1152]{2,1,0:T(8,128)(2,1)S(1)} custom-call(bf16[8,64,1152]{2,1,0:T(8,128)(2,1)S(1)} %get-tuple-element.75.cot, bf16[1152,1152]{1,0:T(8,128)(2,1)S(1)} %copy-done), custom_call_target="tpu_custom_call" | custom-call | flops 1400000000 | bytes 5013504 | tf_op jit(solution)/shard_map/pallas_call | solution.py:134
  26.9 1.1 %collective-permute-done.6.got = bf16[4,144,1152]{2,1,0:T(8,128)(2,1)S(1)} collective-permute-done((bf16[4,144,1152]{2,1,0:T(8,128)(2,1)S(1)}, bf16[4,144,1152]{2,1,0:T(8,128)(2,1)S(1)}, u32[]{:S(2)}, u32[]{:S(2)}) %collective-permute-start.6) | collective-permute-done | bytes 1327136 | tf_op jit(solution)/shard_map/ppermute | solution.py:44
  28.0 1.6 %shard_map.91 = (f32[4,328,128]{2,1,0:T(8,128)S(1)}, bf16[4,328,128]{2,1,0:T(8,128)(2,1)S(1)}, bf16[4,328,128]{2,1,0:T(8,128)(2,1)S(1)}, bf16[4,328,128]{2,1,0:T(8,128)(2,1)S(1)}) custom-call(s32[6]{0:T(128)S(1)} %fusion.spot, bf16[1152,512]{1,0:T(8,128)(2,1)S(1)} %get-tuple-element.76.att_t, bf16[8,64,1152]{2,1,0:T(8,128)(2,1)S(1)} %get-tuple-element.75.cot, ...), custom_call_target="tpu_custom_call" | custom-call | flops 700000000 | bytes 5365760 | tf_op jit(solution)/shard_map/pallas_call | solution.py:134
  29.6 1.6 %collective-permute-start.9 = (bf16[4,328,128]{2,1,0:T(8,128)(2,1)S(1)}, bf16[4,328,128]{2,1,0:T(8,128)(2,1)S(1)}, u32[]{:S(2)}, u32[]{:S(2)}) collective-permute-start(bf16[4,328,128]{2,1,0:T(8,128)(2,1)S(1)} %get-tuple-element.101), channel_id=1, source_target_pairs={{0,8},{8,0},{16,24},{24,16},{1,9},{9,1},{17,25},{25,17},{2,10},{10... | collective-permute-start | bytes 1007624 | tf_op jit(solution)/shard_map/ppermute | solution.py:44
  31.2 1.5 %collective-permute-start.10 = (bf16[4,328,128]{2,1,0:T(8,128)(2,1)S(1)}, bf16[4,328,128]{2,1,0:T(8,128)(2,1)S(1)}, u32[]{:S(2)}, u32[]{:S(2)}) collective-permute-start(bf16[4,328,128]{2,1,0:T(8,128)(2,1)S(1)} %get-tuple-element.102), channel_id=1, source_target_pairs={{0,16},{8,24},{16,0},{24,8},{1,17},{9,25},{17,1},{25,9},{2,18},{10... | collective-permute-start | bytes 1007624 | tf_op jit(solution)/shard_map/ppermute | solution.py:44
  32.7 0.5 collective-permute-start.11
  33.2 1.8 %shard_map.92 = (bf16[4,64,1152]{2,1,0:T(8,128)(2,1)S(1)}, bf16[2,64,1152]{2,1,0:T(8,128)(2,1)S(1)}, bf16[2,64,1152]{2,1,0:T(8,128)(2,1)S(1)}) custom-call(bf16[8,64,1152]{2,1,0:T(8,128)(2,1)S(1)} %get-tuple-element.83.att_ref, bf16[1152,1152]{1,0:T(8,128)(2,1)S(1)} %copy-done), custom_call_target="tpu_custom_call" | custom-call | flops 1000000 | bytes 1000 | tf_op jit(solution)/shard_map/pallas_call | solution.py:134
  35.0 3.0 %collective-permute-start.7 = (bf16[2,64,1152]{2,1,0:T(8,128)(2,1)S(1)}, bf16[2,64,1152]{2,1,0:T(8,128)(2,1)S(1)}, u32[]{:S(2)}, u32[]{:S(2)}) collective-permute-start(bf16[2,64,1152]{2,1,0:T(8,128)(2,1)S(1)} %get-tuple-element.93), channel_id=1, source_target_pairs={{0,2},{1,3},{2,0},{3,1},{4,6},{5,7},{6,4},{7,5},{8,10},{9,11},{10,... | collective-permute-start | bytes 884744 | tf_op jit(solution)/shard_map/ppermute | solution.py:44
  38.0 0.9 %collective-permute-start.8 = (bf16[2,64,1152]{2,1,0:T(8,128)(2,1)S(1)}, bf16[2,64,1152]{2,1,0:T(8,128)(2,1)S(1)}, u32[]{:S(2)}, u32[]{:S(2)}) collective-permute-start(bf16[2,64,1152]{2,1,0:T(8,128)(2,1)S(1)} %get-tuple-element.94), channel_id=1, source_target_pairs={{0,0},{1,1},{2,4},{4,2},{3,5},{5,3},{6,6},{7,7},{8,8},{9,9},{10,12... | collective-permute-start | bytes 884744 | tf_op jit(solution)/shard_map/ppermute | solution.py:437
  38.9 5.6 %shard_map.93.d_ref = bf16[8,64,3456]{2,1,0:T(8,128)(2,1)S(1)} custom-call(s32[6]{0:T(128)S(1)} %fusion.spot, bf16[8,64,1152]{2,1,0:T(8,128)(2,1)S(1)} %shard_map.90.ga_ref, bf16[8,64,3456]{2,1,0:T(8,128)(2,1)S(1)} %get-tuple-element.87.qkv_ref, f32[16,2048]{1,0:T(8,128)S(1)} %get-tuple-element.88.p_ref, bf16[2048,1152]{1,0:T(8,128)(2,1)S(1)} %get-tuple-element.89.wide_ref, ...), custom_call_target="tpu_custom_call" | custom-call | flops 1000000 | bytes 1000 | tf_op jit(solution)/shard_map/pallas_call | solution.py:134
  44.5 3.0 %shard_map.94 = (bf16[2,64,1152]{2,1,0:T(8,128)(2,1)S(1)}, bf16[2,64,1152]{2,1,0:T(8,128)(2,1)S(1)}) custom-call(bf16[8,64,3456]{2,1,0:T(8,128)(2,1)S(1)} %shard_map.93.d_ref, bf16[1152,3456]{1,0:T(8,128)(2,1)S(1)} %bitcast.6), custom_call_target="tpu_custom_call" | custom-call | flops 1000000 | bytes 1000 | tf_op jit(solution)/shard_map/pallas_call | solution.py:134
  47.5 0.5 collective-permute-done.10.two
  48.0 0.8 %shard_map.95 = (f32[328,128]{1,0:T(8,128)S(1)}, bf16[328,128]{1,0:T(8,128)(2,1)S(1)}, bf16[328,128]{1,0:T(8,128)(2,1)S(1)}, bf16[328,128]{1,0:T(8,128)(2,1)S(1)}) custom-call(s32[6]{0:T(128)S(1)} %fusion.spot, f32[4,328,128]{2,1,0:T(8,128)S(1)} %get-tuple-element.100.own, bf16[4,328,128]{2,1,0:T(8,128)(2,1)S(1)} %collective-permute-done.9.one, ...), custom_call_target="tpu_custom_call" | custom-call | flops 1000000 | bytes 2099200 | tf_op jit(solution)/shard_map/pallas_call | solution.py:134
  48.9 2.9 %collective-permute-start.12 = (bf16[328,128]{1,0:T(8,128)(2,1)S(1)}, bf16[328,128]{1,0:T(8,128)(2,1)S(1)}, u32[]{:S(2)}, u32[]{:S(2)}) collective-permute-start(bf16[328,128]{1,0:T(8,128)(2,1)S(1)} %get-tuple-element.111), channel_id=1, source_target_pairs={{0,2},{1,3},{2,0},{3,1},{4,6},{5,7},{6,4},{7,5},{8,10},{9,11},{10,... | collective-permute-start | bytes 251912 | tf_op jit(solution)/shard_map/ppermute | solution.py:44
  51.8 1.3 %collective-permute-start.13 = (bf16[328,128]{1,0:T(8,128)(2,1)S(1)}, bf16[328,128]{1,0:T(8,128)(2,1)S(1)}, u32[]{:S(2)}, u32[]{:S(2)}) collective-permute-start(bf16[328,128]{1,0:T(8,128)(2,1)S(1)} %get-tuple-element.112), channel_id=1, source_target_pairs={{0,4},{1,5},{2,6},{3,7},{4,0},{5,1},{6,2},{7,3},{8,12},{9,13},{10,... | collective-permute-start | bytes 251912 | tf_op jit(solution)/shard_map/ppermute | solution.py:44
  53.1 1.4 %collective-permute-start.14 = (bf16[328,128]{1,0:T(8,128)(2,1)S(1)}, bf16[328,128]{1,0:T(8,128)(2,1)S(1)}, u32[]{:S(2)}, u32[]{:S(2)}) collective-permute-start(bf16[328,128]{1,0:T(8,128)(2,1)S(1)} %get-tuple-element.113), channel_id=1, source_target_pairs={{0,6},{1,7},{2,4},{3,5},{4,2},{5,3},{6,0},{7,1},{8,14},{9,15},{10,... | collective-permute-start | bytes 251912 | tf_op jit(solution)/shard_map/ppermute | solution.py:44
  54.5 0.8 %collective-permute-start.15 = (bf16[2,64,1152]{2,1,0:T(8,128)(2,1)S(1)}, bf16[2,64,1152]{2,1,0:T(8,128)(2,1)S(1)}, u32[]{:S(2)}, u32[]{:S(2)}) collective-permute-start(bf16[2,64,1152]{2,1,0:T(8,128)(2,1)S(1)} %get-tuple-element.115), channel_id=1, source_target_pairs={{0,2},{1,3},{2,0},{3,1},{4,6},{5,7},{6,4},{7,5},{8,10},{9,11},{10,... | collective-permute-start | bytes 884744 | tf_op jit(solution)/shard_map/ppermute | solution.py:44
  55.3 0.7 collective-permute-start.16
  56.0 3.0 %shard_map.96.refs_3_ = bf16[4,64,1152]{2,1,0:T(8,128)(2,1)S(1)} custom-call(bf16[8,64,3456]{2,1,0:T(8,128)(2,1)S(1)} %shard_map.93.d_ref, bf16[1152,3456]{1,0:T(8,128)(2,1)S(1)} %bitcast.6), custom_call_target="tpu_custom_call" | custom-call | flops 8000000000 | bytes 12091392 | tf_op jit(solution)/shard_map/pallas_call | solution.py:134
  59.0 1.4 %collective-permute-done.13.two = bf16[328,128]{1,0:T(8,128)(2,1)S(1)} collective-permute-done((bf16[328,128]{1,0:T(8,128)(2,1)S(1)}, bf16[328,128]{1,0:T(8,128)(2,1)S(1)}, u32[]{:S(2)}, u32[]{:S(2)}) %collective-permute-start.13) | collective-permute-done | bytes 84000 | tf_op jit(solution)/shard_map/ppermute | solution.py:44
  60.4 0.8 %collective-permute-done.14.three = bf16[328,128]{1,0:T(8,128)(2,1)S(1)} collective-permute-done((bf16[328,128]{1,0:T(8,128)(2,1)S(1)}, bf16[328,128]{1,0:T(8,128)(2,1)S(1)}, u32[]{:S(2)}, u32[]{:S(2)}) %collective-permute-start.14) | collective-permute-done | bytes 84000 | tf_op jit(solution)/shard_map/ppermute | solution.py:44
  61.2 1.6 %collective-permute-start.20 = (bf16[328,128]{1,0:T(8,128)(2,1)S(1)}, bf16[328,128]{1,0:T(8,128)(2,1)S(1)}, u32[]{:S(2)}, u32[]{:S(2)}) collective-permute-start(bf16[328,128]{1,0:T(8,128)(2,1)S(1)} %shard_map.97.own), channel_id=1, source_target_pairs={{0,24},{8,16},{16,8},{24,0},{1,25},{9,17},{17,9},{25,1},{2,26},{10... | collective-permute-start | bytes 251912 | tf_op jit(solution)/shard_map/ppermute | solution.py:44
  62.8 1.3 %collective-permute-start.19 = (bf16[328,128]{1,0:T(8,128)(2,1)S(1)}, bf16[328,128]{1,0:T(8,128)(2,1)S(1)}, u32[]{:S(2)}, u32[]{:S(2)}) collective-permute-start(bf16[328,128]{1,0:T(8,128)(2,1)S(1)} %shard_map.97.own), channel_id=1, source_target_pairs={{0,16},{8,24},{16,0},{24,8},{1,17},{9,25},{17,1},{25,9},{2,18},{10... | collective-permute-start | bytes 251912 | tf_op jit(solution)/shard_map/ppermute | solution.py:44
  64.1 0.6 collective-permute-start.18
  64.8 0.8 %shard_map.98 = (bf16[4,64,1152]{2,1,0:T(8,128)(2,1)S(1)}, bf16[4,64,1152]{2,1,0:T(8,128)(2,1)S(1)}) custom-call(s32[6]{0:T(128)S(1)} %fusion.spot, bf16[4,64,1152]{2,1,0:T(8,128)(2,1)S(1)} %get-tuple-element.95.refs_0_, bf16[2,64,1152]{2,1,0:T(8,128)(2,1)S(1)} %collective-permute-done.7.refs_1_, bf16[2,64,1152]{2,1,0:T(8,128)(2,1)S(1)} %collective-permute-done.8.refs_2_, ...), custom_call_target="tpu_custom_call" | custom-call | flops 1000000 | bytes 3538944 | tf_op jit(solution)/shard_map/pallas_call | solution.py:134
  65.6 0.1 collective-permute-start.17
  65.7 1.0 %collective-permute-done.20.three = bf16[328,128]{1,0:T(8,128)(2,1)S(1)} collective-permute-done((bf16[328,128]{1,0:T(8,128)(2,1)S(1)}, bf16[328,128]{1,0:T(8,128)(2,1)S(1)}, u32[]{:S(2)}, u32[]{:S(2)}) %collective-permute-start.20) | collective-permute-done | bytes 84000 | tf_op jit(solution)/shard_map/ppermute | solution.py:44
  66.7 0.9 %collective-permute-done.19.two = bf16[328,128]{1,0:T(8,128)(2,1)S(1)} collective-permute-done((bf16[328,128]{1,0:T(8,128)(2,1)S(1)}, bf16[328,128]{1,0:T(8,128)(2,1)S(1)}, u32[]{:S(2)}, u32[]{:S(2)}) %collective-permute-start.19) | collective-permute-done | bytes 84000 | tf_op jit(solution)/shard_map/ppermute | solution.py:44
  67.5 1.1 %collective-permute-done.18.one = bf16[328,128]{1,0:T(8,128)(2,1)S(1)} collective-permute-done((bf16[328,128]{1,0:T(8,128)(2,1)S(1)}, bf16[328,128]{1,0:T(8,128)(2,1)S(1)}, u32[]{:S(2)}, u32[]{:S(2)}) %collective-permute-start.18) | collective-permute-done | bytes 84000 | tf_op jit(solution)/shard_map/ppermute | solution.py:44
  68.6 0.6 shard_map.99.rows
  69.2 1.8 %shard_map.100 = (bf16[4,64,1152]{2,1,0:T(8,128)(2,1)}, bf16[4,64,1152]{2,1,0:T(8,128)(2,1)}, f32[144,1152]{1,0:T(8,128)}) custom-call(s32[6]{0:T(128)S(1)} %fusion.spot, bf16[4,64,1152]{2,1,0:T(8,128)(2,1)S(1)} %get-tuple-element.117.own, bf16[4,64,1152]{2,1,0:T(8,128)(2,1)S(1)} %collective-permute-done.17.sib, f32[144,1152]{1,0:T(8,128)S(1)} %shard_map.99.rows), custom_call_target="tpu_custom_call" | custom-call | flops 1000000 | bytes 3686400 | tf_op jit(solution)/shard_map/pallas_call | solution.py:134
  (23 shorter events, 0.1 us)
Async XLA Ops:
  0.6 2.5 %collective-permute-start = (bf16[4,64,1152]{2,1,0:T(8,128)(2,1)}, bf16[4,64,1152]{2,1,0:T(8,128)(2,1)S(1)}, u32[]{:S(2)}, u32[]{:S(2)}) collective-permute-start(bf16[4,64,1152]{2,1,0:T(8,128)(2,1)} %bitcast.9), channel_id=1, source_target_pairs={{0,1},{1,0},{2,3},{3,2},{4,5},{5,4},{6,7},{7,6},{8,9},{9,8},{10,11... | collective-permute-start | bytes 1769480 | tf_op jit(solution)/shard_map/ppermute | solution.py:44
  1.1 9.1 %collective-permute-start.3 = (bf16[4,64,1152]{2,1,0:T(8,128)(2,1)}, bf16[4,64,1152]{2,1,0:T(8,128)(2,1)S(1)}, u32[]{:S(2)}, u32[]{:S(2)}) collective-permute-start(bf16[4,64,1152]{2,1,0:T(8,128)(2,1)} %bitcast.7), channel_id=1, source_target_pairs={{0,1},{1,0},{2,3},{3,2},{4,5},{5,4},{6,7},{7,6},{8,9},{9,8},{10,11... | collective-permute-start | bytes 1769480 | tf_op jit(solution)/shard_map/ppermute | solution.py:44
  2.0 5.6 %slice-start = ((s8[7962624]{0:T(1024)(128)(4,1)}), s8[4194304]{0:T(1024)(128)(4,1)S(1)}, s32[]{:S(2)}) async-start(s8[7962624]{0:T(1024)(128)(4,1)} %bitcast.5), calls=%async_computation | async-start | bytes 8388608
  3.1 4.4 %slice-start.1 = ((s8[7962624]{0:T(1024)(128)(4,1)}), s8[3768320]{0:T(1024)(128)(4,1)S(1)}, s32[]{:S(2)}) async-start(s8[7962624]{0:T(1024)(128)(4,1)} %bitcast.5), calls=%async_computation.1 | async-start | bytes 7536640
  3.8 12.6 %collective-permute-start.1 = (bf16[2,64,1152]{2,1,0:T(8,128)(2,1)S(1)}, bf16[2,64,1152]{2,1,0:T(8,128)(2,1)S(1)}, u32[]{:S(2)}, u32[]{:S(2)}) collective-permute-start(bf16[2,64,1152]{2,1,0:T(8,128)(2,1)S(1)} %get-tuple-element.63), channel_id=1, source_target_pairs={{0,2},{1,3},{2,0},{3,1},{4,6},{5,7},{6,4},{7,5},{8,10},{9,11},{10,... | collective-permute-start | bytes 884744 | tf_op jit(solution)/shard_map/ppermute | solution.py:44
  6.8 9.6 %collective-permute-start.2 = (bf16[2,64,1152]{2,1,0:T(8,128)(2,1)S(1)}, bf16[2,64,1152]{2,1,0:T(8,128)(2,1)S(1)}, u32[]{:S(2)}, u32[]{:S(2)}) collective-permute-start(bf16[2,64,1152]{2,1,0:T(8,128)(2,1)S(1)} %get-tuple-element.64), channel_id=1, source_target_pairs={{0,0},{1,1},{2,4},{4,2},{3,5},{5,3},{6,6},{7,7},{8,8},{9,9},{10,12... | collective-permute-start | bytes 884744 | tf_op jit(solution)/shard_map/ppermute | solution.py:437
  7.5 2.7 %copy-start.2 = (bf16[1,1,256,1152]{3,2,1,0:T(8,128)(2,1)S(1)}, bf16[1,1,256,1152]{3,2,1,0:T(8,128)(2,1)}, u32[]{:S(2)}) copy-start(bf16[1,1,256,1152]{3,2,1,0:T(8,128)(2,1)} %param.9) | copy-start | bytes 1769476
  10.3 6.1 %copy-start.1 = (bf16[16,1152]{1,0:T(8,128)(2,1)S(1)}, bf16[16,1152]{1,0:T(8,128)(2,1)}, u32[]{:S(2)}) copy-start(bf16[16,1152]{1,0:T(8,128)(2,1)} %constant.28.clone.heads_ref) | copy-start | bytes 110596
  10.9 12.1 %collective-permute-start.4 = (bf16[2,64,1152]{2,1,0:T(8,128)(2,1)S(1)}, bf16[2,64,1152]{2,1,0:T(8,128)(2,1)S(1)}, u32[]{:S(2)}, u32[]{:S(2)}) collective-permute-start(bf16[2,64,1152]{2,1,0:T(8,128)(2,1)S(1)} %get-tuple-element.70), channel_id=1, source_target_pairs={{0,2},{1,3},{2,0},{3,1},{4,6},{5,7},{6,4},{7,5},{8,10},{9,11},{10,... | collective-permute-start | bytes 884744 | tf_op jit(solution)/shard_map/ppermute | solution.py:44
  15.4 9.6 %copy-start = (bf16[1152,1152]{1,0:T(8,128)(2,1)S(1)}, bf16[1152,1152]{1,0:T(8,128)(2,1)}, u32[]{:S(2)}) copy-start(bf16[1152,1152]{1,0:T(8,128)(2,1)} %w_ref.1) | copy-start | bytes 7962628
  15.4 7.7 %collective-permute-start.5 = (bf16[2,64,1152]{2,1,0:T(8,128)(2,1)S(1)}, bf16[2,64,1152]{2,1,0:T(8,128)(2,1)S(1)}, u32[]{:S(2)}, u32[]{:S(2)}) collective-permute-start(bf16[2,64,1152]{2,1,0:T(8,128)(2,1)S(1)} %get-tuple-element.71), channel_id=1, source_target_pairs={{0,0},{1,1},{2,4},{4,2},{3,5},{5,3},{6,6},{7,7},{8,8},{9,9},{10,12... | collective-permute-start | bytes 884744 | tf_op jit(solution)/shard_map/ppermute | solution.py:437
  24.9 3.1 %collective-permute-start.6 = (bf16[4,144,1152]{2,1,0:T(8,128)(2,1)S(1)}, bf16[4,144,1152]{2,1,0:T(8,128)(2,1)S(1)}, u32[]{:S(2)}, u32[]{:S(2)}) collective-permute-start(bf16[4,144,1152]{2,1,0:T(8,128)(2,1)S(1)} %get-tuple-element.74), channel_id=1, source_target_pairs={{0,1},{1,0},{2,3},{3,2},{4,5},{5,4},{6,7},{7,6},{8,9},{9,8},{10,11... | collective-permute-start | bytes 3981320 | tf_op jit(solution)/shard_map/ppermute | solution.py:44
  29.6 17.9 %collective-permute-start.9 = (bf16[4,328,128]{2,1,0:T(8,128)(2,1)S(1)}, bf16[4,328,128]{2,1,0:T(8,128)(2,1)S(1)}, u32[]{:S(2)}, u32[]{:S(2)}) collective-permute-start(bf16[4,328,128]{2,1,0:T(8,128)(2,1)S(1)} %get-tuple-element.101), channel_id=1, source_target_pairs={{0,8},{8,0},{16,24},{24,16},{1,9},{9,1},{17,25},{25,17},{2,10},{10... | collective-permute-start | bytes 1007624 | tf_op jit(solution)/shard_map/ppermute | solution.py:44
  31.2 16.8 %collective-permute-start.10 = (bf16[4,328,128]{2,1,0:T(8,128)(2,1)S(1)}, bf16[4,328,128]{2,1,0:T(8,128)(2,1)S(1)}, u32[]{:S(2)}, u32[]{:S(2)}) collective-permute-start(bf16[4,328,128]{2,1,0:T(8,128)(2,1)S(1)} %get-tuple-element.102), channel_id=1, source_target_pairs={{0,16},{8,24},{16,0},{24,8},{1,17},{9,25},{17,1},{25,9},{2,18},{10... | collective-permute-start | bytes 1007624 | tf_op jit(solution)/shard_map/ppermute | solution.py:44
  32.7 15.4 %collective-permute-start.11 = (bf16[4,328,128]{2,1,0:T(8,128)(2,1)S(1)}, bf16[4,328,128]{2,1,0:T(8,128)(2,1)S(1)}, u32[]{:S(2)}, u32[]{:S(2)}) collective-permute-start(bf16[4,328,128]{2,1,0:T(8,128)(2,1)S(1)} %get-tuple-element.103), channel_id=1, source_target_pairs={{0,24},{8,16},{16,8},{24,0},{1,25},{9,17},{17,9},{25,1},{2,26},{10... | collective-permute-start | bytes 1007624 | tf_op jit(solution)/shard_map/ppermute | solution.py:44
  35.0 12.5 %collective-permute-start.7 = (bf16[2,64,1152]{2,1,0:T(8,128)(2,1)S(1)}, bf16[2,64,1152]{2,1,0:T(8,128)(2,1)S(1)}, u32[]{:S(2)}, u32[]{:S(2)}) collective-permute-start(bf16[2,64,1152]{2,1,0:T(8,128)(2,1)S(1)} %get-tuple-element.93), channel_id=1, source_target_pairs={{0,2},{1,3},{2,0},{3,1},{4,6},{5,7},{6,4},{7,5},{8,10},{9,11},{10,... | collective-permute-start | bytes 884744 | tf_op jit(solution)/shard_map/ppermute | solution.py:44
  38.0 9.5 %collective-permute-start.8 = (bf16[2,64,1152]{2,1,0:T(8,128)(2,1)S(1)}, bf16[2,64,1152]{2,1,0:T(8,128)(2,1)S(1)}, u32[]{:S(2)}, u32[]{:S(2)}) collective-permute-start(bf16[2,64,1152]{2,1,0:T(8,128)(2,1)S(1)} %get-tuple-element.94), channel_id=1, source_target_pairs={{0,0},{1,1},{2,4},{4,2},{3,5},{5,3},{6,6},{7,7},{8,8},{9,9},{10,12... | collective-permute-start | bytes 884744 | tf_op jit(solution)/shard_map/ppermute | solution.py:437
  48.9 10.1 %collective-permute-start.12 = (bf16[328,128]{1,0:T(8,128)(2,1)S(1)}, bf16[328,128]{1,0:T(8,128)(2,1)S(1)}, u32[]{:S(2)}, u32[]{:S(2)}) collective-permute-start(bf16[328,128]{1,0:T(8,128)(2,1)S(1)} %get-tuple-element.111), channel_id=1, source_target_pairs={{0,2},{1,3},{2,0},{3,1},{4,6},{5,7},{6,4},{7,5},{8,10},{9,11},{10,... | collective-permute-start | bytes 251912 | tf_op jit(solution)/shard_map/ppermute | solution.py:44
  51.8 8.6 %collective-permute-start.13 = (bf16[328,128]{1,0:T(8,128)(2,1)S(1)}, bf16[328,128]{1,0:T(8,128)(2,1)S(1)}, u32[]{:S(2)}, u32[]{:S(2)}) collective-permute-start(bf16[328,128]{1,0:T(8,128)(2,1)S(1)} %get-tuple-element.112), channel_id=1, source_target_pairs={{0,4},{1,5},{2,6},{3,7},{4,0},{5,1},{6,2},{7,3},{8,12},{9,13},{10,... | collective-permute-start | bytes 251912 | tf_op jit(solution)/shard_map/ppermute | solution.py:44
  53.1 8.0 %collective-permute-start.14 = (bf16[328,128]{1,0:T(8,128)(2,1)S(1)}, bf16[328,128]{1,0:T(8,128)(2,1)S(1)}, u32[]{:S(2)}, u32[]{:S(2)}) collective-permute-start(bf16[328,128]{1,0:T(8,128)(2,1)S(1)} %get-tuple-element.113), channel_id=1, source_target_pairs={{0,6},{1,7},{2,4},{3,5},{4,2},{5,3},{6,0},{7,1},{8,14},{9,15},{10,... | collective-permute-start | bytes 251912 | tf_op jit(solution)/shard_map/ppermute | solution.py:44
  54.5 10.3 %collective-permute-start.15 = (bf16[2,64,1152]{2,1,0:T(8,128)(2,1)S(1)}, bf16[2,64,1152]{2,1,0:T(8,128)(2,1)S(1)}, u32[]{:S(2)}, u32[]{:S(2)}) collective-permute-start(bf16[2,64,1152]{2,1,0:T(8,128)(2,1)S(1)} %get-tuple-element.115), channel_id=1, source_target_pairs={{0,2},{1,3},{2,0},{3,1},{4,6},{5,7},{6,4},{7,5},{8,10},{9,11},{10,... | collective-permute-start | bytes 884744 | tf_op jit(solution)/shard_map/ppermute | solution.py:44
  55.3 9.5 %collective-permute-start.16 = (bf16[2,64,1152]{2,1,0:T(8,128)(2,1)S(1)}, bf16[2,64,1152]{2,1,0:T(8,128)(2,1)S(1)}, u32[]{:S(2)}, u32[]{:S(2)}) collective-permute-start(bf16[2,64,1152]{2,1,0:T(8,128)(2,1)S(1)} %get-tuple-element.116), channel_id=1, source_target_pairs={{0,0},{1,1},{2,4},{4,2},{3,5},{5,3},{6,6},{7,7},{8,8},{9,9},{10,12... | collective-permute-start | bytes 884744 | tf_op jit(solution)/shard_map/ppermute | solution.py:437
  61.2 5.4 %collective-permute-start.20 = (bf16[328,128]{1,0:T(8,128)(2,1)S(1)}, bf16[328,128]{1,0:T(8,128)(2,1)S(1)}, u32[]{:S(2)}, u32[]{:S(2)}) collective-permute-start(bf16[328,128]{1,0:T(8,128)(2,1)S(1)} %shard_map.97.own), channel_id=1, source_target_pairs={{0,24},{8,16},{16,8},{24,0},{1,25},{9,17},{17,9},{25,1},{2,26},{10... | collective-permute-start | bytes 251912 | tf_op jit(solution)/shard_map/ppermute | solution.py:44
  62.8 4.7 %collective-permute-start.19 = (bf16[328,128]{1,0:T(8,128)(2,1)S(1)}, bf16[328,128]{1,0:T(8,128)(2,1)S(1)}, u32[]{:S(2)}, u32[]{:S(2)}) collective-permute-start(bf16[328,128]{1,0:T(8,128)(2,1)S(1)} %shard_map.97.own), channel_id=1, source_target_pairs={{0,16},{8,24},{16,0},{24,8},{1,17},{9,25},{17,1},{25,9},{2,18},{10... | collective-permute-start | bytes 251912 | tf_op jit(solution)/shard_map/ppermute | solution.py:44
  64.1 4.5 %collective-permute-start.18 = (bf16[328,128]{1,0:T(8,128)(2,1)S(1)}, bf16[328,128]{1,0:T(8,128)(2,1)S(1)}, u32[]{:S(2)}, u32[]{:S(2)}) collective-permute-start(bf16[328,128]{1,0:T(8,128)(2,1)S(1)} %shard_map.97.own), channel_id=1, source_target_pairs={{0,8},{8,0},{16,24},{24,16},{1,9},{9,1},{17,25},{25,17},{2,10},{10... | collective-permute-start | bytes 251912 | tf_op jit(solution)/shard_map/ppermute | solution.py:44
  65.6 3.7 %collective-permute-start.17 = (bf16[4,64,1152]{2,1,0:T(8,128)(2,1)S(1)}, bf16[4,64,1152]{2,1,0:T(8,128)(2,1)S(1)}, u32[]{:S(2)}, u32[]{:S(2)}) collective-permute-start(bf16[4,64,1152]{2,1,0:T(8,128)(2,1)S(1)} %get-tuple-element.118), channel_id=1, source_target_pairs={{0,1},{1,0},{2,3},{3,2},{4,5},{5,4},{6,7},{7,6},{8,9},{9,8},{10,11... | collective-permute-start | bytes 1769480 | tf_op jit(solution)/shard_map/ppermute | solution.py:44

commit v2 on v1

--- a/solution.py
+++ b/solution.py
@@ -217,7 +217,7 @@
 
 
 def forward_kernel(
-    spot, near, far, wi_ref, _, heads_ref, qkv_ref, att_ref, p_ref, wide_ref,
+    spot, far, near, wi_ref, _, heads_ref, qkv_ref, att_ref, p_ref, wide_ref,
     x_scr, hi_scr, w_scr,
 ):
     x_scr[:2] = near[...]
@@ -272,7 +272,7 @@
     return dot(rows[...], flat(cot[...])).reshape(4, height, -1)
 
 
-def part_kernel(spot, att_ref, ab_ref, near, far, sib_ref, att_t, cot, rows):
+def part_kernel(spot, att_ref, ab_ref, far, near, sib_ref, att_t, cot, rows):
     cot[:4] = ab_ref[...]
     cot[4:6] = near[...]
     cot[6:] = far[...]
@@ -287,9 +287,10 @@
     far_ref[...] = made[6:]
 
 
-def grad_att_kernel(cot, wo_ref, ga_ref):
-    made = contract_cols(flat(cot[...]), wo_ref[...])
-    ga_ref[...] = made.astype(jnp.bfloat16).reshape(8, ROWS, INNER)
+def grad_att_kernel(cot, wo_ref, *refs, first):
+    rows = cot[first : first + 4]
+    made = contract_cols(flat(rows), wo_ref[...])
+    refs[-1][first : first + 4] = made.astype(jnp.bfloat16).reshape(4, ROWS, INNER)
 
 
 def backward_kernel(
@@ -349,7 +350,7 @@
 
 
 def settle_kernel(spot, *refs):
-    *given, own, sib, held = refs
+    *given, own, sib = refs
     role = roles(spot)
     core, left, right = role["core"], role["left"], role["right"]
     low, high, tail, head = role["low"], role["high"], role["tail"], role["head"]
@@ -359,30 +360,42 @@
         jnp.where(high, left + 1, jnp.where(head, right, 2)),
         jnp.where(low | head, right + 1, 3),
     ]
+
+    def put(out, row, block, here, far, near):
+        for source, first, count in ((here, 0, 4), (near, 4, 2), (far, 6, 2)):
+
+            @pl.when((block >= first) & (block < first + count))
+            def _():
+                out[row] = source[block - first]
+
     for base in (0, 2):
-        here, near, far = given[:3] if base == 0 else given[3:]
-        held[:4] = here[...]
-        held[4:6] = near[...]
-        held[6:] = far[...]
+        sources = given[:3] if base == 0 else given[3:]
         for i in range(2):
-            own[base + i] = held[jnp.where(core == 0, where[i], where[2 + i])]
-            sib[base + i] = held[jnp.where(core == 0, where[2 + i], where[i])]
+            put(own, base + i, jnp.where(core == 0, where[i], where[2 + i]), *sources)
+            put(sib, base + i, jnp.where(core == 0, where[2 + i], where[i]), *sources)
 
 
 def first_row(group, block):
     return pl.multiple_of((group * 81 // 2 + block * 162) * 8, 8)
 
 
-def cores_kernel(spot, att_t, cot, got, keep, *sends):
-    group = spot[1]
-    *sends, rows, total = sends
-    height, width = got.shape[1:]
+def mine_kernel(spot, att_t, cot, total, rows):
+    height, width = att_t.shape[0] // 8, cot.shape[2]
     made = part_rows(spot[0] % 2, att_t, cot, rows)
     for z in range(4):
-        block = made[z] + got[z].astype(jnp.float32)
         for t in range(width // TILE):
             start = (z * width // TILE + t) * height
-            total[start : start + height, :] = block[:, lanes(t)]
+            total[start : start + height, :] = made[z][:, lanes(t)]
+
+
+def cores_kernel(spot, mine, got, keep, *sends):
+    group = spot[1]
+    *sends, total = sends
+    height, width = got.shape[1:]
+    for z in range(4):
+        for t in range(width // TILE):
+            rows = slice((z * width // TILE + t) * height, (z * width // TILE + t + 1) * height)
+            total[rows, :] = mine[rows, :] + got[z, :, lanes(t)].astype(jnp.float32)
     for flip, out in enumerate((keep, *sends)):
         for z in range(4):
             out[z] = total[pl.ds(first_row(group ^ flip, z), PIECE), :].astype(out.dtype)
@@ -429,14 +442,9 @@
     return lax.optimization_barrier((later, earlier))
 
 
-def swap_near(value):
-    return swap(value, "seq", 2)
-
-
-def swap_far(value):
-    return lax.ppermute(
-        value, "seq", [(0, 0), (1, 1), (2, 4), (4, 2), (3, 5), (5, 3), (6, 6), (7, 7)]
-    )
+def exchange(near, far):
+    pairs = [(0, 0), (1, 1), (2, 4), (4, 2), (3, 5), (5, 3), (6, 6), (7, 7)]
+    return lax.ppermute(far, "seq", pairs), swap(near, "seq", 2)
 
 
 def clip_body(latents, in_weight, out_weight, cotangent, clip_lengths):
@@ -453,46 +461,54 @@
     bf16 = jnp.bfloat16
     four, two, eight = shaped((4, ROWS, width)), shaped((2, ROWS, width)), shaped((8, ROWS, INNER))
 
-    def pick(own, sib):
-        near, far, both = call(pick_kernel, [spot], [own, sib], [two, two, four], flops=4 * 10**9)
-        return swap_near(near), swap_far(far), both
+    def pick(own, sib, flops):
+        near, far, both = call(pick_kernel, [spot], [own, sib], [two, two, four], flops=flops)
+        return exchange(near, far), both
 
     lat_sib, cot_sib = swap(lat, "seq", 1), swap(cot, "seq", 1)
     lat_own = lax.dynamic_slice_in_dim(lat, 2 * (lax.axis_index("seq") % 2), 2, 0)
-    lat_near, lat_far, lat_ab = pick(lat_own, lat_sib)
+    (lat_far, lat_near), lat_ab = pick(lat_own, lat_sib, 4 * 10**9)
     (qkv_ab,) = call(
         early_kernel, [], [lat_ab, in_weight], [shaped((8, ROWS, 3 * INNER))], limit=16, flops=27 * 10**8
     )
     cot_sib, qkv_ab = after(cot_sib, qkv_ab)
-    cot_near, cot_far, cot_ab = pick(cot, cot_sib)
+    (cot_far, cot_near), cot_ab = pick(cot, cot_sib, 10**6)
+    grad_att = functools.partial(grad_att_kernel, first=0)
+    (ga,) = call(grad_att, [], [cot_ab, out_weight], [eight], limit=16, flops=7 * 10**8)
+    lat_far, ga = after(lat_far, ga)
     pairs = 2 * PAIRS * ROWS
     products, columns = ((pairs, INNER), bf16), ((pairs, HEADS), bf16)
     qkv, att, probs, wides = call(
-        forward_kernel, [spot], [lat_near, lat_far, in_weight, qkv_ab, heads],
+        forward_kernel, [spot], [lat_far, lat_near, in_weight, qkv_ab, heads],
         [shaped((8, ROWS, 3 * INNER)), eight, shaped((HEADS, pairs), wide), shaped((pairs, INNER))],
         [((4, ROWS, width), bf16), products, columns], limit=24, flops=8 * 10**9, same=(3, 0),
     )
     part_scr = ((4 * rows, 8 * ROWS), bf16)
     other, att_t, cot_all = call(
-        part_kernel, [spot], [att, cot_ab, cot_near, cot_far],
+        part_kernel, [spot], [att, cot_ab, cot_far, cot_near],
         [shaped((4, rows, width)), shaped((INNER, 8 * ROWS)), eight], [part_scr],
         limit=16, flops=7 * 10**8,
     )
     got = swap(other, "seq", 1)
     cot_all, other = after(cot_all, other)
-    (ga,) = call(grad_att_kernel, [], [cot_all, out_weight], [eight], limit=16, flops=14 * 10**8)
-    att_t, ga = after(att_t, ga)
+    grad_att = functools.partial(grad_att_kernel, first=4)
+    (ga,) = call(grad_att, [], [cot_all, out_weight, ga], [eight], limit=16, flops=7 * 10**8, same=(2, 0))
     part, piece = (4, PIECE, TILE), (PIECE, TILE)
     tiles = rows * width // TILE
+    (mine,) = call(
+        mine_kernel, [spot], [att_t, cot_all], [shaped((4 * tiles, TILE), wide)], [part_scr],
+        limit=16, flops=7 * 10**8,
+    )
+    mine, ga = after(mine, ga)
     keep, *sends = call(
-        cores_kernel, [spot], [att_t, cot_all, got], [shaped(part, wide)] + [shaped(part)] * 3,
-        [part_scr, ((4 * tiles, TILE), wide)], limit=16, flops=7 * 10**8,
+        cores_kernel, [spot], [mine, got], [shaped(part, wide)] + [shaped(part)] * 3,
+        [((4 * tiles, TILE), wide)], limit=16, flops=7 * 10**8,
     )
     att, sends = after(att, sends)
-    sends = [swap(x, "dp", flip) for flip, x in enumerate(sends, 1)]
+    sends = [swap(sends[flip - 1], "dp", flip) for flip in (3, 1, 2)]
     mixed = call(mix_kernel, [], [att, out_weight], [four, two, two], limit=16, size=10**3)
     qkv, mixed = after(qkv, mixed)
-    mixed = [mixed[0], swap_near(mixed[1]), swap_far(mixed[2])]
+    mixed = [mixed[0], *exchange(mixed[1], mixed[2])]
     (d_all,) = call(
         backward_kernel, [spot], [ga, qkv, probs, wides, heads], [shaped((8, ROWS, 3 * INNER))],
         [products, ((HEADS, pairs), wide), columns], limit=24, size=10**3,
@@ -509,12 +525,12 @@
     d_all, grad = after(d_all, grad)
     ours = functools.partial(latents_kernel, first=0)
     (own,) = call(ours, [], [d_all, in_weight], [four], limit=16, flops=8 * 10**9)
-    grad = [own, swap_near(grad[0]), swap_far(grad[1])]
+    grad = [own, *exchange(grad[0], grad[1])]
     keep, grad[0] = after(keep, grad[0])
     (last,) = call(chips_kernel, [], [keep, *sends], [shaped(piece)])
     grad[0], last = after(grad[0], last)
     others = [swap(last, "dp", flip) for flip in (1, 2, 3)]
-    own, sib = call(settle_kernel, [spot], [*mixed, *grad], [four, four], [((8, ROWS, width), bf16)])
+    own, sib = call(settle_kernel, [spot], [*mixed, *grad], [four, four])
     (out_grad,) = call(
         gather_kernel, [spot], [last, *others], [shaped((rows, width), wide)],
         [(part, wide), ((tiles, TILE), wide)], flops=8 * 10**9,

time: 71.5 us -> 70.8 us (level)
  waiting for transfers between devices: 6.75 us -> 4.23 us
  Pallas kernels: 33.5 us -> 34.5 us
  starting transfers between devices: 28 us -> 28.9 us
    ppermute x17, waiting for transfers between devices: 6.74 us -> 4.21 us  [swap(): return lax.ppermute(value, axis, [(i, i ^ flip) for i in range(size)])]
    pallas_call x16 -> x18, Pallas kernels: 33.5 us -> 34.5 us  [call(): pl.pallas_call(kernel, out_shape=list(outs), in_specs=[SMEM] * len(scalar...]
    ppermute x17, starting transfers between devices: 24.8 us -> 25.7 us  [swap(): return lax.ppermute(value, axis, [(i, i ^ flip) for i in range(size)])]
  transfers between devices with their start and end apart: 21 -> 21, of which waited for: 7 -> 7; matrix products, arithmetic and copies ran while one was open for 3% -> 3% of each run, Pallas kernels for 39% -> 41%
where the time goes in v2:
time: 70.8 us; the launch traced here: 70.6 us
  Pallas kernels  34.5 us (49%)
  starting transfers between devices  28.9 us (41%)
  waiting for transfers between devices  4.23 us (6%)
  local copies, waits for them, and re-layouts  1.16 us (2%)
  between operations  1.11 us (2%)
  other arithmetic  0.73 us (1%)
    pallas_call x18, Pallas kernels, call(): pl.pallas_call(kernel, out_shape=list(outs), in_specs=[SMEM] * len(scalar...  34.5 us
    ppermute x17, starting transfers between devices, swap(): return lax.ppermute(value, axis, [(i, i ^ flip) for i in range(size)])  25.7 us
    ppermute x17, waiting for transfers between devices, swap(): return lax.ppermute(value, axis, [(i, i ^ flip) for i in range(size)])  4.21 us
    ppermute x4, starting transfers between devices, exchange(): return (lax.ppermute(far, 'seq', pairs), swap(near, 'seq', 2))  3.24 us
  transfers between devices with their start and end apart: 21, of which 7 were waited for; matrix products, arithmetic and copies ran while one was open for 3% of the time, Pallas kernels for 41%

profile of v2, /device:TPU:0, one launch (start us, length us, event | category | flops | bytes accessed | tf_op | source)
XLA Modules:
  0.0 70.6 jit_solution(2643697266093240115)
XLA Ops:
  0.6 0.5 collective-permute-start
  1.1 0.1 collective-permute-start.2
  1.2 0.7 %fusion.spot = s32[6]{0:T(128)S(1)} fusion(s32[4]{0:T(128)} %bitcast.11, s32[]{:T(128)S(6)} %axis_index.29, s32[]{:T(128)S(6)} %axis_index.26), kind=kLoop, calls=%fused_computation.2 | loop fusion | flops 30 | bytes 48 | tf_op jit(solution)/shard_map/add | solution.py:456
  2.0 1.1 %constant_dynamic-slice_fusion.own = bf16[2,64,1152]{2,1,0:T(8,128)(2,1)S(1)} fusion(bf16[4,64,1152]{2,1,0:T(8,128)(2,1)} %bitcast.10, s32[]{:T(128)S(6)} %select_n.21), kind=kLoop, calls=%fused_computation.3 | loop fusion | bytes 589828 | tf_op jit(solution)/shard_map/dynamic_slice | solution.py:469
  3.1 0.0 slice-start.1
  3.1 0.6 shard_map.85
  3.8 0.8 %collective-permute-start.1 = (bf16[2,64,1152]{2,1,0:T(8,128)(2,1)S(1)}, bf16[2,64,1152]{2,1,0:T(8,128)(2,1)S(1)}, u32[]{:S(2)}, u32[]{:S(2)}) collective-permute-start(bf16[2,64,1152]{2,1,0:T(8,128)(2,1)S(1)} %get-tuple-element.65), channel_id=1, source_target_pairs={{0,0},{1,1},{2,4},{4,2},{3,5},{5,3},{6,6},{7,7},{8,8},{9,9},{10,12... | collective-permute-start | bytes 884744 | tf_op jit(solution)/shard_map/ppermute | solution.py:447
  4.6 5.9 %collective-permute-start.3 = (bf16[2,64,1152]{2,1,0:T(8,128)(2,1)S(1)}, bf16[2,64,1152]{2,1,0:T(8,128)(2,1)S(1)}, u32[]{:S(2)}, u32[]{:S(2)}) collective-permute-start(bf16[2,64,1152]{2,1,0:T(8,128)(2,1)S(1)} %get-tuple-element.70), channel_id=1, source_target_pairs={{0,2},{1,3},{2,0},{3,1},{4,6},{5,7},{6,4},{7,5},{8,10},{9,11},{10,... | collective-permute-start | bytes 884744 | tf_op jit(solution)/shard_map/ppermute | solution.py:44
  10.5 2.7 %shard_map.86._ = bf16[8,64,3456]{2,1,0:T(8,128)(2,1)S(1)} custom-call(bf16[4,64,1152]{2,1,0:T(8,128)(2,1)S(1)} %get-tuple-element.66.lat_ab, bf16[1152,3456]{1,0:T(8,128)(2,1)S(1)} %bitcast.6), custom_call_target="tpu_custom_call" | custom-call | flops 2700000000 | bytes 12091392 | tf_op jit(solution)/shard_map/pallas_call | solution.py:134
  13.2 0.6 shard_map.87
  13.9 0.9 %collective-permute-start.4 = (bf16[2,64,1152]{2,1,0:T(8,128)(2,1)S(1)}, bf16[2,64,1152]{2,1,0:T(8,128)(2,1)S(1)}, u32[]{:S(2)}, u32[]{:S(2)}) collective-permute-start(bf16[2,64,1152]{2,1,0:T(8,128)(2,1)S(1)} %get-tuple-element.73), channel_id=1, source_target_pairs={{0,0},{1,1},{2,4},{4,2},{3,5},{5,3},{6,6},{7,7},{8,8},{9,9},{10,12... | collective-permute-start | bytes 884744 | tf_op jit(solution)/shard_map/ppermute | solution.py:447
  14.7 1.8 %collective-permute-start.5 = (bf16[2,64,1152]{2,1,0:T(8,128)(2,1)S(1)}, bf16[2,64,1152]{2,1,0:T(8,128)(2,1)S(1)}, u32[]{:S(2)}, u32[]{:S(2)}) collective-permute-start(bf16[2,64,1152]{2,1,0:T(8,128)(2,1)S(1)} %get-tuple-element.74), channel_id=1, source_target_pairs={{0,2},{1,3},{2,0},{3,1},{4,6},{5,7},{6,4},{7,5},{8,10},{9,11},{10,... | collective-permute-start | bytes 884744 | tf_op jit(solution)/shard_map/ppermute | solution.py:44
  16.5 1.0 %shard_map.88.refs_0_ = bf16[8,64,1152]{2,1,0:T(8,128)(2,1)S(1)} custom-call(bf16[4,64,1152]{2,1,0:T(8,128)(2,1)S(1)} %get-tuple-element.68.cot.ab_ref, bf16[1152,1152]{1,0:T(8,128)(2,1)S(1)} %copy-done), custom_call_target="tpu_custom_call" | custom-call | flops 700000000 | bytes 4423680 | tf_op jit(solution)/shard_map/pallas_call | solution.py:134
  17.6 0.3 collective-permute-done.3.near
  17.9 6.7 %shard_map.89 = (bf16[8,64,3456]{2,1,0:T(8,128)(2,1)S(1)}, bf16[8,64,1152]{2,1,0:T(8,128)(2,1)S(1)}, f32[16,2048]{1,0:T(8,128)S(1)}, bf16[2048,1152]{1,0:T(8,128)(2,1)S(1)}) custom-call(s32[6]{0:T(128)S(1)} %fusion.spot, bf16[2,64,1152]{2,1,0:T(8,128)(2,1)S(1)} %collective-permute-done.1.far, ...), custom_call_target="tpu_custom_call", output_to_operand_aliasing={{0}: (4, {})} | custom-call | flops 8000000000 | bytes 21696512 | tf_op jit(solution)/shard_map/pallas_call | solution.py:134
  24.6 1.7 %shard_map.90 = (bf16[4,144,1152]{2,1,0:T(8,128)(2,1)S(1)}, bf16[1152,512]{1,0:T(8,128)(2,1)S(1)}, bf16[8,64,1152]{2,1,0:T(8,128)(2,1)S(1)}) custom-call(s32[6]{0:T(128)S(1)} %fusion.spot, bf16[8,64,1152]{2,1,0:T(8,128)(2,1)S(1)} %get-tuple-element.87.att_ref, bf16[4,64,1152]{2,1,0:T(8,128)(2,1)S(1)} %get-tuple-element.68.cot.ab_ref, ...), custom_call_target="tpu_custom_call" | custom-call | flops 700000000 | bytes 6045696 | tf_op jit(solution)/shard_map/pallas_call | solution.py:134
  26.3 0.1 collective-permute-start.6
  26.4 1.0 %shard_map.92.ga_ref = bf16[8,64,1152]{2,1,0:T(8,128)(2,1)S(1)} custom-call(bf16[8,64,1152]{2,1,0:T(8,128)(2,1)S(1)} %get-tuple-element.78.cot, bf16[1152,1152]{1,0:T(8,128)(2,1)S(1)} %copy-done, bf16[8,64,1152]{2,1,0:T(8,128)(2,1)S(1)} %shard_map.88.refs_0_), custom_call_target="tpu_custom_call", output_to_operand_aliasing={{}: (2, {})} | custom-call | flops 700000000 | bytes 6193152 | tf_op jit(solution)/shard_map/pallas_call | solution.py:134
  27.5 1.5 %shard_map.91.mine = f32[5184,128]{1,0:T(8,128)S(1)} custom-call(s32[6]{0:T(128)S(1)} %fusion.spot, bf16[1152,512]{1,0:T(8,128)(2,1)S(1)} %get-tuple-element.75.att_t, bf16[8,64,1152]{2,1,0:T(8,128)(2,1)S(1)} %get-tuple-element.78.cot), custom_call_target="tpu_custom_call" | custom-call | flops 700000000 | bytes 5013504 | tf_op jit(solution)/shard_map/pallas_call | solution.py:134
  28.9 0.5 collective-permute-done.6.got
  29.5 1.0 %shard_map.93 = (f32[4,328,128]{2,1,0:T(8,128)S(1)}, bf16[4,328,128]{2,1,0:T(8,128)(2,1)S(1)}, bf16[4,328,128]{2,1,0:T(8,128)(2,1)S(1)}, bf16[4,328,128]{2,1,0:T(8,128)(2,1)S(1)}) custom-call(s32[6]{0:T(128)S(1)} %fusion.spot, f32[5184,128]{1,0:T(8,128)S(1)} %shard_map.91.mine, bf16[4,144,1152]{2,1,0:T(8,128)(2,1)S(1)} %collective-permute-done.6.got), custom_call_target="tpu_custom_call" | custom-call | flops 700000000 | bytes 5660672 | tf_op jit(solution)/shard_map/pallas_call | solution.py:134
  30.4 2.5 %collective-permute-start.9 = (bf16[4,328,128]{2,1,0:T(8,128)(2,1)S(1)}, bf16[4,328,128]{2,1,0:T(8,128)(2,1)S(1)}, u32[]{:S(2)}, u32[]{:S(2)}) collective-permute-start(bf16[4,328,128]{2,1,0:T(8,128)(2,1)S(1)} %get-tuple-element.105), channel_id=1, source_target_pairs={{0,24},{8,16},{16,8},{24,0},{1,25},{9,17},{17,9},{25,1},{2,26},{10... | collective-permute-start | bytes 1007624 | tf_op jit(solution)/shard_map/ppermute | solution.py:44
  32.9 0.6 collective-permute-start.10
  33.5 0.5 collective-permute-start.11
  34.0 1.9 %shard_map.94 = (bf16[4,64,1152]{2,1,0:T(8,128)(2,1)S(1)}, bf16[2,64,1152]{2,1,0:T(8,128)(2,1)S(1)}, bf16[2,64,1152]{2,1,0:T(8,128)(2,1)S(1)}) custom-call(bf16[8,64,1152]{2,1,0:T(8,128)(2,1)S(1)} %get-tuple-element.87.att_ref, bf16[1152,1152]{1,0:T(8,128)(2,1)S(1)} %copy-done), custom_call_target="tpu_custom_call" | custom-call | flops 1000000 | bytes 1000 | tf_op jit(solution)/shard_map/pallas_call | solution.py:134
  35.8 0.9 %collective-permute-start.7 = (bf16[2,64,1152]{2,1,0:T(8,128)(2,1)S(1)}, bf16[2,64,1152]{2,1,0:T(8,128)(2,1)S(1)}, u32[]{:S(2)}, u32[]{:S(2)}) collective-permute-start(bf16[2,64,1152]{2,1,0:T(8,128)(2,1)S(1)} %get-tuple-element.97), channel_id=1, source_target_pairs={{0,0},{1,1},{2,4},{4,2},{3,5},{5,3},{6,6},{7,7},{8,8},{9,9},{10,12... | collective-permute-start | bytes 884744 | tf_op jit(solution)/shard_map/ppermute | solution.py:447
  36.8 3.4 %collective-permute-start.8 = (bf16[2,64,1152]{2,1,0:T(8,128)(2,1)S(1)}, bf16[2,64,1152]{2,1,0:T(8,128)(2,1)S(1)}, u32[]{:S(2)}, u32[]{:S(2)}) collective-permute-start(bf16[2,64,1152]{2,1,0:T(8,128)(2,1)S(1)} %get-tuple-element.98), channel_id=1, source_target_pairs={{0,2},{1,3},{2,0},{3,1},{4,6},{5,7},{6,4},{7,5},{8,10},{9,11},{10,... | collective-permute-start | bytes 884744 | tf_op jit(solution)/shard_map/ppermute | solution.py:44
  40.2 5.6 %shard_map.95.d_ref = bf16[8,64,3456]{2,1,0:T(8,128)(2,1)S(1)} custom-call(s32[6]{0:T(128)S(1)} %fusion.spot, bf16[8,64,1152]{2,1,0:T(8,128)(2,1)S(1)} %shard_map.92.ga_ref, bf16[8,64,3456]{2,1,0:T(8,128)(2,1)S(1)} %get-tuple-element.91.qkv_ref, f32[16,2048]{1,0:T(8,128)S(1)} %get-tuple-element.92.p_ref, bf16[2048,1152]{1,0:T(8,128)(2,1)S(1)} %get-tuple-element.93.wide_ref, ...), custom_call_target="tpu_custom_call" | custom-call | flops 1000000 | bytes 1000 | tf_op jit(solution)/shard_map/pallas_call | solution.py:134
  45.8 3.0 %shard_map.96 = (bf16[2,64,1152]{2,1,0:T(8,128)(2,1)S(1)}, bf16[2,64,1152]{2,1,0:T(8,128)(2,1)S(1)}) custom-call(bf16[8,64,3456]{2,1,0:T(8,128)(2,1)S(1)} %shard_map.95.d_ref, bf16[1152,3456]{1,0:T(8,128)(2,1)S(1)} %bitcast.6), custom_call_target="tpu_custom_call" | custom-call | flops 1000000 | bytes 1000 | tf_op jit(solution)/shard_map/pallas_call | solution.py:134
  48.9 0.9 %shard_map.97 = (f32[328,128]{1,0:T(8,128)S(1)}, bf16[328,128]{1,0:T(8,128)(2,1)S(1)}, bf16[328,128]{1,0:T(8,128)(2,1)S(1)}, bf16[328,128]{1,0:T(8,128)(2,1)S(1)}) custom-call(s32[6]{0:T(128)S(1)} %fusion.spot, f32[4,328,128]{2,1,0:T(8,128)S(1)} %get-tuple-element.104.own, bf16[4,328,128]{2,1,0:T(8,128)(2,1)S(1)} %collective-permute-done.9.one, ...), custom_call_target="tpu_custom_call" | custom-call | flops 1000000 | bytes 2099200 | tf_op jit(solution)/shard_map/pallas_call | solution.py:134
  49.7 1.6 %collective-permute-start.12 = (bf16[328,128]{1,0:T(8,128)(2,1)S(1)}, bf16[328,128]{1,0:T(8,128)(2,1)S(1)}, u32[]{:S(2)}, u32[]{:S(2)}) collective-permute-start(bf16[328,128]{1,0:T(8,128)(2,1)S(1)} %get-tuple-element.115), channel_id=1, source_target_pairs={{0,2},{1,3},{2,0},{3,1},{4,6},{5,7},{6,4},{7,5},{8,10},{9,11},{10,... | collective-permute-start | bytes 251912 | tf_op jit(solution)/shard_map/ppermute | solution.py:44
  51.3 1.6 %collective-permute-start.13 = (bf16[328,128]{1,0:T(8,128)(2,1)S(1)}, bf16[328,128]{1,0:T(8,128)(2,1)S(1)}, u32[]{:S(2)}, u32[]{:S(2)}) collective-permute-start(bf16[328,128]{1,0:T(8,128)(2,1)S(1)} %get-tuple-element.116), channel_id=1, source_target_pairs={{0,4},{1,5},{2,6},{3,7},{4,0},{5,1},{6,2},{7,3},{8,12},{9,13},{10,... | collective-permute-start | bytes 251912 | tf_op jit(solution)/shard_map/ppermute | solution.py:44
  52.9 1.3 %collective-permute-start.14 = (bf16[328,128]{1,0:T(8,128)(2,1)S(1)}, bf16[328,128]{1,0:T(8,128)(2,1)S(1)}, u32[]{:S(2)}, u32[]{:S(2)}) collective-permute-start(bf16[328,128]{1,0:T(8,128)(2,1)S(1)} %get-tuple-element.117), channel_id=1, source_target_pairs={{0,6},{1,7},{2,4},{3,5},{4,2},{5,3},{6,0},{7,1},{8,14},{9,15},{10,... | collective-permute-start | bytes 251912 | tf_op jit(solution)/shard_map/ppermute | solution.py:44
  54.2 0.7 collective-permute-start.15
  54.8 2.3 %collective-permute-start.16 = (bf16[2,64,1152]{2,1,0:T(8,128)(2,1)S(1)}, bf16[2,64,1152]{2,1,0:T(8,128)(2,1)S(1)}, u32[]{:S(2)}, u32[]{:S(2)}) collective-permute-start(bf16[2,64,1152]{2,1,0:T(8,128)(2,1)S(1)} %get-tuple-element.120), channel_id=1, source_target_pairs={{0,2},{1,3},{2,0},{3,1},{4,6},{5,7},{6,4},{7,5},{8,10},{9,11},{10,... | collective-permute-start | bytes 884744 | tf_op jit(solution)/shard_map/ppermute | solution.py:44
  57.1 3.0 %shard_map.98.refs_3_ = bf16[4,64,1152]{2,1,0:T(8,128)(2,1)S(1)} custom-call(bf16[8,64,3456]{2,1,0:T(8,128)(2,1)S(1)} %shard_map.95.d_ref, bf16[1152,3456]{1,0:T(8,128)(2,1)S(1)} %bitcast.6), custom_call_target="tpu_custom_call" | custom-call | flops 8000000000 | bytes 12091392 | tf_op jit(solution)/shard_map/pallas_call | solution.py:134
  60.1 0.3 collective-permute-done.13.two
  60.5 2.4 %collective-permute-start.20 = (bf16[328,128]{1,0:T(8,128)(2,1)S(1)}, bf16[328,128]{1,0:T(8,128)(2,1)S(1)}, u32[]{:S(2)}, u32[]{:S(2)}) collective-permute-start(bf16[328,128]{1,0:T(8,128)(2,1)S(1)} %shard_map.99.own), channel_id=1, source_target_pairs={{0,24},{8,16},{16,8},{24,0},{1,25},{9,17},{17,9},{25,1},{2,26},{10... | collective-permute-start | bytes 251912 | tf_op jit(solution)/shard_map/ppermute | solution.py:44
  62.9 0.6 collective-permute-start.19
  63.5 0.5 collective-permute-start.18
  64.0 1.6 %collective-permute-done.16.refs_5_ = bf16[2,64,1152]{2,1,0:T(8,128)(2,1)S(1)} collective-permute-done((bf16[2,64,1152]{2,1,0:T(8,128)(2,1)S(1)}, bf16[2,64,1152]{2,1,0:T(8,128)(2,1)S(1)}, u32[]{:S(2)}, u32[]{:S(2)}) %collective-permute-start.16) | collective-permute-done | bytes 294944 | tf_op jit(solution)/shard_map/ppermute | solution.py:44
  65.6 0.7 %shard_map.100 = (bf16[4,64,1152]{2,1,0:T(8,128)(2,1)S(1)}, bf16[4,64,1152]{2,1,0:T(8,128)(2,1)S(1)}) custom-call(s32[6]{0:T(128)S(1)} %fusion.spot, bf16[4,64,1152]{2,1,0:T(8,128)(2,1)S(1)} %get-tuple-element.99.refs_0_, bf16[2,64,1152]{2,1,0:T(8,128)(2,1)S(1)} %collective-permute-done.7.refs_1_, bf16[2,64,1152]{2,1,0:T(8,128)(2,1)S(1)} %collective-permute-done.8.refs_2_, ...), custom_call_target="tpu_custom_call" | custom-call | flops 1000000 | bytes 3538944 | tf_op jit(solution)/shard_map/pallas_call | solution.py:134
  66.4 0.1 collective-permute-start.17
  66.5 0.1 collective-permute-done.20.three
  66.5 0.9 %collective-permute-done.19.two = bf16[328,128]{1,0:T(8,128)(2,1)S(1)} collective-permute-done((bf16[328,128]{1,0:T(8,128)(2,1)S(1)}, bf16[328,128]{1,0:T(8,128)(2,1)S(1)}, u32[]{:S(2)}, u32[]{:S(2)}) %collective-permute-start.19) | collective-permute-done | bytes 84000 | tf_op jit(solution)/shard_map/ppermute | solution.py:44
  67.4 0.5 collective-permute-done.18.one
  67.9 0.6 shard_map.101.rows
  68.6 1.8 %shard_map.102 = (bf16[4,64,1152]{2,1,0:T(8,128)(2,1)}, bf16[4,64,1152]{2,1,0:T(8,128)(2,1)}, f32[144,1152]{1,0:T(8,128)}) custom-call(s32[6]{0:T(128)S(1)} %fusion.spot, bf16[4,64,1152]{2,1,0:T(8,128)(2,1)S(1)} %get-tuple-element.121.own, bf16[4,64,1152]{2,1,0:T(8,128)(2,1)S(1)} %collective-permute-done.17.sib, f32[144,1152]{1,0:T(8,128)S(1)} %shard_map.101.rows), custom_call_target="tpu_custom_call" | custom-call | flops 1000000 | bytes 3686400 | tf_op jit(solution)/shard_map/pallas_call | solution.py:134
  (25 shorter events, 0.1 us)
Async XLA Ops:
  0.6 2.5 %collective-permute-start = (bf16[4,64,1152]{2,1,0:T(8,128)(2,1)}, bf16[4,64,1152]{2,1,0:T(8,128)(2,1)S(1)}, u32[]{:S(2)}, u32[]{:S(2)}) collective-permute-start(bf16[4,64,1152]{2,1,0:T(8,128)(2,1)} %bitcast.9), channel_id=1, source_target_pairs={{0,1},{1,0},{2,3},{3,2},{4,5},{5,4},{6,7},{7,6},{8,9},{9,8},{10,11... | collective-permute-start | bytes 1769480 | tf_op jit(solution)/shard_map/ppermute | solution.py:44
  1.1 12.1 %collective-permute-start.2 = (bf16[4,64,1152]{2,1,0:T(8,128)(2,1)}, bf16[4,64,1152]{2,1,0:T(8,128)(2,1)S(1)}, u32[]{:S(2)}, u32[]{:S(2)}) collective-permute-start(bf16[4,64,1152]{2,1,0:T(8,128)(2,1)} %bitcast.7), channel_id=1, source_target_pairs={{0,1},{1,0},{2,3},{3,2},{4,5},{5,4},{6,7},{7,6},{8,9},{9,8},{10,11... | collective-permute-start | bytes 1769480 | tf_op jit(solution)/shard_map/ppermute | solution.py:44
  2.0 8.5 %slice-start = ((s8[7962624]{0:T(1024)(128)(4,1)}), s8[4194304]{0:T(1024)(128)(4,1)S(1)}, s32[]{:S(2)}) async-start(s8[7962624]{0:T(1024)(128)(4,1)} %bitcast.5), calls=%async_computation | async-start | bytes 8388608
  3.1 7.4 %slice-start.1 = ((s8[7962624]{0:T(1024)(128)(4,1)}), s8[3768320]{0:T(1024)(128)(4,1)S(1)}, s32[]{:S(2)}) async-start(s8[7962624]{0:T(1024)(128)(4,1)} %bitcast.5), calls=%async_computation.1 | async-start | bytes 7536640
  3.8 13.8 %collective-permute-start.1 = (bf16[2,64,1152]{2,1,0:T(8,128)(2,1)S(1)}, bf16[2,64,1152]{2,1,0:T(8,128)(2,1)S(1)}, u32[]{:S(2)}, u32[]{:S(2)}) collective-permute-start(bf16[2,64,1152]{2,1,0:T(8,128)(2,1)S(1)} %get-tuple-element.65), channel_id=1, source_target_pairs={{0,0},{1,1},{2,4},{4,2},{3,5},{5,3},{6,6},{7,7},{8,8},{9,9},{10,12... | collective-permute-start | bytes 884744 | tf_op jit(solution)/shard_map/ppermute | solution.py:447
  4.6 13.3 %collective-permute-start.3 = (bf16[2,64,1152]{2,1,0:T(8,128)(2,1)S(1)}, bf16[2,64,1152]{2,1,0:T(8,128)(2,1)S(1)}, u32[]{:S(2)}, u32[]{:S(2)}) collective-permute-start(bf16[2,64,1152]{2,1,0:T(8,128)(2,1)S(1)} %get-tuple-element.70), channel_id=1, source_target_pairs={{0,2},{1,3},{2,0},{3,1},{4,6},{5,7},{6,4},{7,5},{8,10},{9,11},{10,... | collective-permute-start | bytes 884744 | tf_op jit(solution)/shard_map/ppermute | solution.py:44
  10.5 2.8 %copy-start.1 = (bf16[1,1,256,1152]{3,2,1,0:T(8,128)(2,1)S(1)}, bf16[1,1,256,1152]{3,2,1,0:T(8,128)(2,1)}, u32[]{:S(2)}) copy-start(bf16[1,1,256,1152]{3,2,1,0:T(8,128)(2,1)} %param.9) | copy-start | bytes 1769476
  10.5 6.1 %copy-start = (bf16[1152,1152]{1,0:T(8,128)(2,1)S(1)}, bf16[1152,1152]{1,0:T(8,128)(2,1)}, u32[]{:S(2)}) copy-start(bf16[1152,1152]{1,0:T(8,128)(2,1)} %w_ref.1) | copy-start | bytes 7962628
  13.2 4.7 %copy-start.2 = (bf16[16,1152]{1,0:T(8,128)(2,1)S(1)}, bf16[16,1152]{1,0:T(8,128)(2,1)}, u32[]{:S(2)}) copy-start(bf16[16,1152]{1,0:T(8,128)(2,1)} %constant.28.clone.heads_ref) | copy-start | bytes 110596
  13.9 10.7 %collective-permute-start.4 = (bf16[2,64,1152]{2,1,0:T(8,128)(2,1)S(1)}, bf16[2,64,1152]{2,1,0:T(8,128)(2,1)S(1)}, u32[]{:S(2)}, u32[]{:S(2)}) collective-permute-start(bf16[2,64,1152]{2,1,0:T(8,128)(2,1)S(1)} %get-tuple-element.73), channel_id=1, source_target_pairs={{0,0},{1,1},{2,4},{4,2},{3,5},{5,3},{6,6},{7,7},{8,8},{9,9},{10,12... | collective-permute-start | bytes 884744 | tf_op jit(solution)/shard_map/ppermute | solution.py:447
  14.7 9.8 %collective-permute-start.5 = (bf16[2,64,1152]{2,1,0:T(8,128)(2,1)S(1)}, bf16[2,64,1152]{2,1,0:T(8,128)(2,1)S(1)}, u32[]{:S(2)}, u32[]{:S(2)}) collective-permute-start(bf16[2,64,1152]{2,1,0:T(8,128)(2,1)S(1)} %get-tuple-element.74), channel_id=1, source_target_pairs={{0,2},{1,3},{2,0},{3,1},{4,6},{5,7},{6,4},{7,5},{8,10},{9,11},{10,... | collective-permute-start | bytes 884744 | tf_op jit(solution)/shard_map/ppermute | solution.py:44
  26.3 3.1 %collective-permute-start.6 = (bf16[4,144,1152]{2,1,0:T(8,128)(2,1)S(1)}, bf16[4,144,1152]{2,1,0:T(8,128)(2,1)S(1)}, u32[]{:S(2)}, u32[]{:S(2)}) collective-permute-start(bf16[4,144,1152]{2,1,0:T(8,128)(2,1)S(1)} %get-tuple-element.77), channel_id=1, source_target_pairs={{0,1},{1,0},{2,3},{3,2},{4,5},{5,4},{6,7},{7,6},{8,9},{9,8},{10,11... | collective-permute-start | bytes 3981320 | tf_op jit(solution)/shard_map/ppermute | solution.py:44
  30.4 18.4 %collective-permute-start.9 = (bf16[4,328,128]{2,1,0:T(8,128)(2,1)S(1)}, bf16[4,328,128]{2,1,0:T(8,128)(2,1)S(1)}, u32[]{:S(2)}, u32[]{:S(2)}) collective-permute-start(bf16[4,328,128]{2,1,0:T(8,128)(2,1)S(1)} %get-tuple-element.105), channel_id=1, source_target_pairs={{0,24},{8,16},{16,8},{24,0},{1,25},{9,17},{17,9},{25,1},{2,26},{10... | collective-permute-start | bytes 1007624 | tf_op jit(solution)/shard_map/ppermute | solution.py:44
  32.9 15.9 %collective-permute-start.10 = (bf16[4,328,128]{2,1,0:T(8,128)(2,1)S(1)}, bf16[4,328,128]{2,1,0:T(8,128)(2,1)S(1)}, u32[]{:S(2)}, u32[]{:S(2)}) collective-permute-start(bf16[4,328,128]{2,1,0:T(8,128)(2,1)S(1)} %get-tuple-element.106), channel_id=1, source_target_pairs={{0,8},{8,0},{16,24},{24,16},{1,9},{9,1},{17,25},{25,17},{2,10},{10... | collective-permute-start | bytes 1007624 | tf_op jit(solution)/shard_map/ppermute | solution.py:44
  33.5 15.4 %collective-permute-start.11 = (bf16[4,328,128]{2,1,0:T(8,128)(2,1)S(1)}, bf16[4,328,128]{2,1,0:T(8,128)(2,1)S(1)}, u32[]{:S(2)}, u32[]{:S(2)}) collective-permute-start(bf16[4,328,128]{2,1,0:T(8,128)(2,1)S(1)} %get-tuple-element.107), channel_id=1, source_target_pairs={{0,16},{8,24},{16,0},{24,8},{1,17},{9,25},{17,1},{25,9},{2,18},{10... | collective-permute-start | bytes 1007624 | tf_op jit(solution)/shard_map/ppermute | solution.py:44
  35.8 13.0 %collective-permute-start.7 = (bf16[2,64,1152]{2,1,0:T(8,128)(2,1)S(1)}, bf16[2,64,1152]{2,1,0:T(8,128)(2,1)S(1)}, u32[]{:S(2)}, u32[]{:S(2)}) collective-permute-start(bf16[2,64,1152]{2,1,0:T(8,128)(2,1)S(1)} %get-tuple-element.97), channel_id=1, source_target_pairs={{0,0},{1,1},{2,4},{4,2},{3,5},{5,3},{6,6},{7,7},{8,8},{9,9},{10,12... | collective-permute-start | bytes 884744 | tf_op jit(solution)/shard_map/ppermute | solution.py:447
  36.8 12.1 %collective-permute-start.8 = (bf16[2,64,1152]{2,1,0:T(8,128)(2,1)S(1)}, bf16[2,64,1152]{2,1,0:T(8,128)(2,1)S(1)}, u32[]{:S(2)}, u32[]{:S(2)}) collective-permute-start(bf16[2,64,1152]{2,1,0:T(8,128)(2,1)S(1)} %get-tuple-element.98), channel_id=1, source_target_pairs={{0,2},{1,3},{2,0},{3,1},{4,6},{5,7},{6,4},{7,5},{8,10},{9,11},{10,... | collective-permute-start | bytes 884744 | tf_op jit(solution)/shard_map/ppermute | solution.py:44
  49.7 10.4 %collective-permute-start.12 = (bf16[328,128]{1,0:T(8,128)(2,1)S(1)}, bf16[328,128]{1,0:T(8,128)(2,1)S(1)}, u32[]{:S(2)}, u32[]{:S(2)}) collective-permute-start(bf16[328,128]{1,0:T(8,128)(2,1)S(1)} %get-tuple-element.115), channel_id=1, source_target_pairs={{0,2},{1,3},{2,0},{3,1},{4,6},{5,7},{6,4},{7,5},{8,10},{9,11},{10,... | collective-permute-start | bytes 251912 | tf_op jit(solution)/shard_map/ppermute | solution.py:44
  51.3 9.1 %collective-permute-start.13 = (bf16[328,128]{1,0:T(8,128)(2,1)S(1)}, bf16[328,128]{1,0:T(8,128)(2,1)S(1)}, u32[]{:S(2)}, u32[]{:S(2)}) collective-permute-start(bf16[328,128]{1,0:T(8,128)(2,1)S(1)} %get-tuple-element.116), channel_id=1, source_target_pairs={{0,4},{1,5},{2,6},{3,7},{4,0},{5,1},{6,2},{7,3},{8,12},{9,13},{10,... | collective-permute-start | bytes 251912 | tf_op jit(solution)/shard_map/ppermute | solution.py:44
  52.9 7.5 %collective-permute-start.14 = (bf16[328,128]{1,0:T(8,128)(2,1)S(1)}, bf16[328,128]{1,0:T(8,128)(2,1)S(1)}, u32[]{:S(2)}, u32[]{:S(2)}) collective-permute-start(bf16[328,128]{1,0:T(8,128)(2,1)S(1)} %get-tuple-element.117), channel_id=1, source_target_pairs={{0,6},{1,7},{2,4},{3,5},{4,2},{5,3},{6,0},{7,1},{8,14},{9,15},{10,... | collective-permute-start | bytes 251912 | tf_op jit(solution)/shard_map/ppermute | solution.py:44
  54.2 9.9 %collective-permute-start.15 = (bf16[2,64,1152]{2,1,0:T(8,128)(2,1)S(1)}, bf16[2,64,1152]{2,1,0:T(8,128)(2,1)S(1)}, u32[]{:S(2)}, u32[]{:S(2)}) collective-permute-start(bf16[2,64,1152]{2,1,0:T(8,128)(2,1)S(1)} %get-tuple-element.119), channel_id=1, source_target_pairs={{0,0},{1,1},{2,4},{4,2},{3,5},{5,3},{6,6},{7,7},{8,8},{9,9},{10,12... | collective-permute-start | bytes 884744 | tf_op jit(solution)/shard_map/ppermute | solution.py:447
  54.8 10.8 %collective-permute-start.16 = (bf16[2,64,1152]{2,1,0:T(8,128)(2,1)S(1)}, bf16[2,64,1152]{2,1,0:T(8,128)(2,1)S(1)}, u32[]{:S(2)}, u32[]{:S(2)}) collective-permute-start(bf16[2,64,1152]{2,1,0:T(8,128)(2,1)S(1)} %get-tuple-element.120), channel_id=1, source_target_pairs={{0,2},{1,3},{2,0},{3,1},{4,6},{5,7},{6,4},{7,5},{8,10},{9,11},{10,... | collective-permute-start | bytes 884744 | tf_op jit(solution)/shard_map/ppermute | solution.py:44
  60.5 6.1 %collective-permute-start.20 = (bf16[328,128]{1,0:T(8,128)(2,1)S(1)}, bf16[328,128]{1,0:T(8,128)(2,1)S(1)}, u32[]{:S(2)}, u32[]{:S(2)}) collective-permute-start(bf16[328,128]{1,0:T(8,128)(2,1)S(1)} %shard_map.99.own), channel_id=1, source_target_pairs={{0,24},{8,16},{16,8},{24,0},{1,25},{9,17},{17,9},{25,1},{2,26},{10... | collective-permute-start | bytes 251912 | tf_op jit(solution)/shard_map/ppermute | solution.py:44
  62.9 4.5 %collective-permute-start.19 = (bf16[328,128]{1,0:T(8,128)(2,1)S(1)}, bf16[328,128]{1,0:T(8,128)(2,1)S(1)}, u32[]{:S(2)}, u32[]{:S(2)}) collective-permute-start(bf16[328,128]{1,0:T(8,128)(2,1)S(1)} %shard_map.99.own), channel_id=1, source_target_pairs={{0,16},{8,24},{16,0},{24,8},{1,17},{9,25},{17,1},{25,9},{2,18},{10... | collective-permute-start | bytes 251912 | tf_op jit(solution)/shard_map/ppermute | solution.py:44
  63.5 4.5 %collective-permute-start.18 = (bf16[328,128]{1,0:T(8,128)(2,1)S(1)}, bf16[328,128]{1,0:T(8,128)(2,1)S(1)}, u32[]{:S(2)}, u32[]{:S(2)}) collective-permute-start(bf16[328,128]{1,0:T(8,128)(2,1)S(1)} %shard_map.99.own), channel_id=1, source_target_pairs={{0,8},{8,0},{16,24},{24,16},{1,9},{9,1},{17,25},{25,17},{2,10},{10... | collective-permute-start | bytes 251912 | tf_op jit(solution)/shard_map/ppermute | solution.py:44
  66.4 2.2 %collective-permute-start.17 = (bf16[4,64,1152]{2,1,0:T(8,128)(2,1)S(1)}, bf16[4,64,1152]{2,1,0:T(8,128)(2,1)S(1)}, u32[]{:S(2)}, u32[]{:S(2)}) collective-permute-start(bf16[4,64,1152]{2,1,0:T(8,128)(2,1)S(1)} %get-tuple-element.122), channel_id=1, source_target_pairs={{0,1},{1,0},{2,3},{3,2},{4,5},{5,4},{6,7},{7,6},{8,9},{9,8},{10,11... | collective-permute-start | bytes 1769480 | tf_op jit(solution)/shard_map/ppermute | solution.py:44

commit v3 on v2

--- a/solution.py
+++ b/solution.py
@@ -414,26 +414,31 @@
     out[...] = total.astype(jnp.bfloat16)
 
 
-def gather_kernel(spot, own, one, two, three, out, held, rows):
-    for flip, value in enumerate((own, one, two, three)):
+def arrived_kernel(one, two, three, token):
+    token[...] = (one[:16, :] + two[:16, :]) + three[:16, :]
+
+
+def final_kernel(
+    spot, own, sib, last, one, two, three, _, mixed, grad, out, held, rows, made, sems
+):
+    core = spot[0] % 2
+    here, there = pl.ds(2 * core, 2), pl.ds(2 * (1 - core), 2)
+    moves = []
+    for base, result in ((0, mixed), (2, grad)):
+        moves.append((own.at[base : base + 2], result.at[here]))
+        moves.append((sib.at[base : base + 2], result.at[there]))
+    copies = [pltpu.make_async_copy(x, y, sems.at[i]) for i, (x, y) in enumerate(moves)]
+    for copy in copies:
+        copy.start()
+    for flip, value in enumerate((last, one, two, three)):
         held[spot[1] ^ flip] = value[...].astype(jnp.float32)
     for group in range(4):
         rows[pl.ds(first_row(group, 0), PIECE), :] = held[group]
     height, width = out.shape
     for t in range(width // TILE):
-        out[:, lanes(t)] = rows[t * height : (t + 1) * height, :]
-
-
-def final_kernel(spot, own, sib, rows, mixed, grad, out, sems):
-    core = spot[0] % 2
-    here, there = pl.ds(2 * core, 2), pl.ds(2 * (1 - core), 2)
-    moves = [(rows.at[i : i + 48], out.at[i : i + 48]) for i in range(0, out.shape[0], 48)]
-    for base, made in ((0, mixed), (2, grad)):
-        moves.append((own.at[base : base + 2], made.at[here]))
-        moves.append((sib.at[base : base + 2], made.at[there]))
-    copies = [pltpu.make_async_copy(x, y, sems.at[i]) for i, (x, y) in enumerate(moves)]
-    for copy in copies:
-        copy.start()
+        made[:, lanes(t)] = rows[t * height : (t + 1) * height, :]
+    copies.append(pltpu.make_async_copy(made, out, sems.at[len(copies)]))
+    copies[-1].start()
     for copy in copies:
         copy.wait()
 
@@ -521,7 +526,7 @@
         [(part, wide)],
     )
     grad, keep = after(grad, keep)
-    sends = [swap(x, "seq", 2 * flip) for flip, x in enumerate(sends, 1)]
+    sends = [swap(sends[flip - 1], "seq", 2 * flip) for flip in (2, 3, 1)]
     d_all, grad = after(d_all, grad)
     ours = functools.partial(latents_kernel, first=0)
     (own,) = call(ours, [], [d_all, in_weight], [four], limit=16, flops=8 * 10**9)
@@ -531,13 +536,12 @@
     grad[0], last = after(grad[0], last)
     others = [swap(last, "dp", flip) for flip in (1, 2, 3)]
     own, sib = call(settle_kernel, [spot], [*mixed, *grad], [four, four])
-    (out_grad,) = call(
-        gather_kernel, [spot], [last, *others], [shaped((rows, width), wide)],
-        [(part, wide), ((tiles, TILE), wide)], flops=8 * 10**9,
-    )
+    (token,) = call(arrived_kernel, [], others, [shaped((16, TILE))], flops=8 * 10**9)
     mixed, grad, out_grad = call(
-        final_kernel, [spot], [own, swap(sib, "seq", 1), out_grad],
-        [four, four, shaped((rows, width), wide)], [pltpu.SemaphoreType.DMA((7,))], to_hbm=True,
+        final_kernel, [spot], [own, swap(sib, "seq", 1), last, *others, token],
+        [four, four, shaped((rows, width), wide)],
+        [(part, wide), ((tiles, TILE), wide), ((rows, width), wide), pltpu.SemaphoreType.DMA((5,))],
+        to_hbm=True,
     )
     return mixed.reshape(latents.shape), grad.reshape(latents.shape), out_grad
 

time: 70.8 us -> 71.2 us (level)
  starting transfers between devices: 28.9 us -> 29.8 us
    ppermute x17, starting transfers between devices: 25.7 us -> 26.6 us  [swap(): return lax.ppermute(value, axis, [(i, i ^ flip) for i in range(size)])]
  transfers between devices with their start and end apart: 21 -> 21, of which waited for: 7 -> 7; matrix products, arithmetic and copies ran while one was open for 3% -> 3% of each run, Pallas kernels for 41% -> 40%
where the time goes in v3:
time: 71.2 us; the launch traced here: 71 us
  Pallas kernels  33.9 us (48%)
  starting transfers between devices  29.8 us (42%)
  waiting for transfers between devices  4.34 us (6%)
  local copies, waits for them, and re-layouts  1.16 us (2%)
  between operations  1.1 us (2%)
  other arithmetic  0.73 us (1%)
    pallas_call x18, Pallas kernels, call(): pl.pallas_call(kernel, out_shape=list(outs), in_specs=[SMEM] * len(scalar...  33.9 us
    ppermute x17, starting transfers between devices, swap(): return lax.ppermute(value, axis, [(i, i ^ flip) for i in range(size)])  26.6 us
    ppermute x17, waiting for transfers between devices, swap(): return lax.ppermute(value, axis, [(i, i ^ flip) for i in range(size)])  4.33 us
    ppermute x4, starting transfers between devices, exchange(): return (lax.ppermute(far, 'seq', pairs), swap(near, 'seq', 2))  3.24 us
  transfers between devices with their start and end apart: 21, of which 7 were waited for; matrix products, arithmetic and copies ran while one was open for 3% of the time, Pallas kernels for 40%

profile of v3, /device:TPU:0, one launch (start us, length us, event | category | flops | bytes accessed | tf_op | source)
XLA Modules:
  0.0 71.0 jit_solution(14312326877100872626)
XLA Ops:
  0.6 0.5 collective-permute-start
  1.1 0.1 collective-permute-start.2
  1.2 0.7 %fusion.spot = s32[6]{0:T(128)S(1)} fusion(s32[4]{0:T(128)} %bitcast.11, s32[]{:T(128)S(6)} %axis_index.29, s32[]{:T(128)S(6)} %axis_index.26), kind=kLoop, calls=%fused_computation.2 | loop fusion | flops 30 | bytes 48 | tf_op jit(solution)/shard_map/add | solution.py:461
  2.0 1.1 %constant_dynamic-slice_fusion.own = bf16[2,64,1152]{2,1,0:T(8,128)(2,1)S(1)} fusion(bf16[4,64,1152]{2,1,0:T(8,128)(2,1)} %bitcast.10, s32[]{:T(128)S(6)} %select_n.21), kind=kLoop, calls=%fused_computation.3 | loop fusion | bytes 589828 | tf_op jit(solution)/shard_map/dynamic_slice | solution.py:474
  3.1 0.0 slice-start.1
  3.1 0.6 shard_map.85
  3.8 0.8 %collective-permute-start.1 = (bf16[2,64,1152]{2,1,0:T(8,128)(2,1)S(1)}, bf16[2,64,1152]{2,1,0:T(8,128)(2,1)S(1)}, u32[]{:S(2)}, u32[]{:S(2)}) collective-permute-start(bf16[2,64,1152]{2,1,0:T(8,128)(2,1)S(1)} %get-tuple-element.65), channel_id=1, source_target_pairs={{0,0},{1,1},{2,4},{4,2},{3,5},{5,3},{6,6},{7,7},{8,8},{9,9},{10,12... | collective-permute-start | bytes 884744 | tf_op jit(solution)/shard_map/ppermute | solution.py:452
  4.6 5.9 %collective-permute-start.3 = (bf16[2,64,1152]{2,1,0:T(8,128)(2,1)S(1)}, bf16[2,64,1152]{2,1,0:T(8,128)(2,1)S(1)}, u32[]{:S(2)}, u32[]{:S(2)}) collective-permute-start(bf16[2,64,1152]{2,1,0:T(8,128)(2,1)S(1)} %get-tuple-element.70), channel_id=1, source_target_pairs={{0,2},{1,3},{2,0},{3,1},{4,6},{5,7},{6,4},{7,5},{8,10},{9,11},{10,... | collective-permute-start | bytes 884744 | tf_op jit(solution)/shard_map/ppermute | solution.py:44
  10.5 0.0 copy-start
  10.5 2.7 %shard_map.86._ = bf16[8,64,3456]{2,1,0:T(8,128)(2,1)S(1)} custom-call(bf16[4,64,1152]{2,1,0:T(8,128)(2,1)S(1)} %get-tuple-element.66.lat_ab, bf16[1152,3456]{1,0:T(8,128)(2,1)S(1)} %bitcast.6), custom_call_target="tpu_custom_call" | custom-call | flops 2700000000 | bytes 12091392 | tf_op jit(solution)/shard_map/pallas_call | solution.py:134
  13.2 0.0 copy-start.2
  13.2 0.6 shard_map.87
  13.9 0.9 %collective-permute-start.4 = (bf16[2,64,1152]{2,1,0:T(8,128)(2,1)S(1)}, bf16[2,64,1152]{2,1,0:T(8,128)(2,1)S(1)}, u32[]{:S(2)}, u32[]{:S(2)}) collective-permute-start(bf16[2,64,1152]{2,1,0:T(8,128)(2,1)S(1)} %get-tuple-element.73), channel_id=1, source_target_pairs={{0,0},{1,1},{2,4},{4,2},{3,5},{5,3},{6,6},{7,7},{8,8},{9,9},{10,12... | collective-permute-start | bytes 884744 | tf_op jit(solution)/shard_map/ppermute | solution.py:452
  14.7 1.8 %collective-permute-start.5 = (bf16[2,64,1152]{2,1,0:T(8,128)(2,1)S(1)}, bf16[2,64,1152]{2,1,0:T(8,128)(2,1)S(1)}, u32[]{:S(2)}, u32[]{:S(2)}) collective-permute-start(bf16[2,64,1152]{2,1,0:T(8,128)(2,1)S(1)} %get-tuple-element.74), channel_id=1, source_target_pairs={{0,2},{1,3},{2,0},{3,1},{4,6},{5,7},{6,4},{7,5},{8,10},{9,11},{10,... | collective-permute-start | bytes 884744 | tf_op jit(solution)/shard_map/ppermute | solution.py:44
  16.5 1.0 %shard_map.88.refs_0_ = bf16[8,64,1152]{2,1,0:T(8,128)(2,1)S(1)} custom-call(bf16[4,64,1152]{2,1,0:T(8,128)(2,1)S(1)} %get-tuple-element.68.cot.ab_ref, bf16[1152,1152]{1,0:T(8,128)(2,1)S(1)} %copy-done), custom_call_target="tpu_custom_call" | custom-call | flops 700000000 | bytes 4423680 | tf_op jit(solution)/shard_map/pallas_call | solution.py:134
  17.6 0.3 collective-permute-done.3.near
  17.9 6.7 %shard_map.89 = (bf16[8,64,3456]{2,1,0:T(8,128)(2,1)S(1)}, bf16[8,64,1152]{2,1,0:T(8,128)(2,1)S(1)}, f32[16,2048]{1,0:T(8,128)S(1)}, bf16[2048,1152]{1,0:T(8,128)(2,1)S(1)}) custom-call(s32[6]{0:T(128)S(1)} %fusion.spot, bf16[2,64,1152]{2,1,0:T(8,128)(2,1)S(1)} %collective-permute-done.1.far, ...), custom_call_target="tpu_custom_call", output_to_operand_aliasing={{0}: (4, {})} | custom-call | flops 8000000000 | bytes 21696512 | tf_op jit(solution)/shard_map/pallas_call | solution.py:134
  24.6 1.7 %shard_map.90 = (bf16[4,144,1152]{2,1,0:T(8,128)(2,1)S(1)}, bf16[1152,512]{1,0:T(8,128)(2,1)S(1)}, bf16[8,64,1152]{2,1,0:T(8,128)(2,1)S(1)}) custom-call(s32[6]{0:T(128)S(1)} %fusion.spot, bf16[8,64,1152]{2,1,0:T(8,128)(2,1)S(1)} %get-tuple-element.87.att_ref, bf16[4,64,1152]{2,1,0:T(8,128)(2,1)S(1)} %get-tuple-element.68.cot.ab_ref, ...), custom_call_target="tpu_custom_call" | custom-call | flops 700000000 | bytes 6045696 | tf_op jit(solution)/shard_map/pallas_call | solution.py:134
  26.3 0.1 collective-permute-start.6
  26.4 1.0 %shard_map.92.ga_ref = bf16[8,64,1152]{2,1,0:T(8,128)(2,1)S(1)} custom-call(bf16[8,64,1152]{2,1,0:T(8,128)(2,1)S(1)} %get-tuple-element.78.cot, bf16[1152,1152]{1,0:T(8,128)(2,1)S(1)} %copy-done, bf16[8,64,1152]{2,1,0:T(8,128)(2,1)S(1)} %shard_map.88.refs_0_), custom_call_target="tpu_custom_call", output_to_operand_aliasing={{}: (2, {})} | custom-call | flops 700000000 | bytes 6193152 | tf_op jit(solution)/shard_map/pallas_call | solution.py:134
  27.5 1.5 %shard_map.91.mine = f32[5184,128]{1,0:T(8,128)S(1)} custom-call(s32[6]{0:T(128)S(1)} %fusion.spot, bf16[1152,512]{1,0:T(8,128)(2,1)S(1)} %get-tuple-element.75.att_t, bf16[8,64,1152]{2,1,0:T(8,128)(2,1)S(1)} %get-tuple-element.78.cot), custom_call_target="tpu_custom_call" | custom-call | flops 700000000 | bytes 5013504 | tf_op jit(solution)/shard_map/pallas_call | solution.py:134
  28.9 0.5 collective-permute-done.6.got
  29.5 1.0 %shard_map.93 = (f32[4,328,128]{2,1,0:T(8,128)S(1)}, bf16[4,328,128]{2,1,0:T(8,128)(2,1)S(1)}, bf16[4,328,128]{2,1,0:T(8,128)(2,1)S(1)}, bf16[4,328,128]{2,1,0:T(8,128)(2,1)S(1)}) custom-call(s32[6]{0:T(128)S(1)} %fusion.spot, f32[5184,128]{1,0:T(8,128)S(1)} %shard_map.91.mine, bf16[4,144,1152]{2,1,0:T(8,128)(2,1)S(1)} %collective-permute-done.6.got), custom_call_target="tpu_custom_call" | custom-call | flops 700000000 | bytes 5660672 | tf_op jit(solution)/shard_map/pallas_call | solution.py:134
  30.4 2.5 %collective-permute-start.9 = (bf16[4,328,128]{2,1,0:T(8,128)(2,1)S(1)}, bf16[4,328,128]{2,1,0:T(8,128)(2,1)S(1)}, u32[]{:S(2)}, u32[]{:S(2)}) collective-permute-start(bf16[4,328,128]{2,1,0:T(8,128)(2,1)S(1)} %get-tuple-element.105), channel_id=1, source_target_pairs={{0,24},{8,16},{16,8},{24,0},{1,25},{9,17},{17,9},{25,1},{2,26},{10... | collective-permute-start | bytes 1007624 | tf_op jit(solution)/shard_map/ppermute | solution.py:44
  32.9 0.6 collective-permute-start.10
  33.5 0.5 collective-permute-start.11
  34.0 1.9 %shard_map.94 = (bf16[4,64,1152]{2,1,0:T(8,128)(2,1)S(1)}, bf16[2,64,1152]{2,1,0:T(8,128)(2,1)S(1)}, bf16[2,64,1152]{2,1,0:T(8,128)(2,1)S(1)}) custom-call(bf16[8,64,1152]{2,1,0:T(8,128)(2,1)S(1)} %get-tuple-element.87.att_ref, bf16[1152,1152]{1,0:T(8,128)(2,1)S(1)} %copy-done), custom_call_target="tpu_custom_call" | custom-call | flops 1000000 | bytes 1000 | tf_op jit(solution)/shard_map/pallas_call | solution.py:134
  35.8 0.9 %collective-permute-start.7 = (bf16[2,64,1152]{2,1,0:T(8,128)(2,1)S(1)}, bf16[2,64,1152]{2,1,0:T(8,128)(2,1)S(1)}, u32[]{:S(2)}, u32[]{:S(2)}) collective-permute-start(bf16[2,64,1152]{2,1,0:T(8,128)(2,1)S(1)} %get-tuple-element.97), channel_id=1, source_target_pairs={{0,0},{1,1},{2,4},{4,2},{3,5},{5,3},{6,6},{7,7},{8,8},{9,9},{10,12... | collective-permute-start | bytes 884744 | tf_op jit(solution)/shard_map/ppermute | solution.py:452
  36.8 3.4 %collective-permute-start.8 = (bf16[2,64,1152]{2,1,0:T(8,128)(2,1)S(1)}, bf16[2,64,1152]{2,1,0:T(8,128)(2,1)S(1)}, u32[]{:S(2)}, u32[]{:S(2)}) collective-permute-start(bf16[2,64,1152]{2,1,0:T(8,128)(2,1)S(1)} %get-tuple-element.98), channel_id=1, source_target_pairs={{0,2},{1,3},{2,0},{3,1},{4,6},{5,7},{6,4},{7,5},{8,10},{9,11},{10,... | collective-permute-start | bytes 884744 | tf_op jit(solution)/shard_map/ppermute | solution.py:44
  40.2 5.6 %shard_map.95.d_ref = bf16[8,64,3456]{2,1,0:T(8,128)(2,1)S(1)} custom-call(s32[6]{0:T(128)S(1)} %fusion.spot, bf16[8,64,1152]{2,1,0:T(8,128)(2,1)S(1)} %shard_map.92.ga_ref, bf16[8,64,3456]{2,1,0:T(8,128)(2,1)S(1)} %get-tuple-element.91.qkv_ref, f32[16,2048]{1,0:T(8,128)S(1)} %get-tuple-element.92.p_ref, bf16[2048,1152]{1,0:T(8,128)(2,1)S(1)} %get-tuple-element.93.wide_ref, ...), custom_call_target="tpu_custom_call" | custom-call | flops 1000000 | bytes 1000 | tf_op jit(solution)/shard_map/pallas_call | solution.py:134
  45.8 3.0 %shard_map.96 = (bf16[2,64,1152]{2,1,0:T(8,128)(2,1)S(1)}, bf16[2,64,1152]{2,1,0:T(8,128)(2,1)S(1)}) custom-call(bf16[8,64,3456]{2,1,0:T(8,128)(2,1)S(1)} %shard_map.95.d_ref, bf16[1152,3456]{1,0:T(8,128)(2,1)S(1)} %bitcast.6), custom_call_target="tpu_custom_call" | custom-call | flops 1000000 | bytes 1000 | tf_op jit(solution)/shard_map/pallas_call | solution.py:134
  48.9 0.9 %shard_map.97 = (f32[328,128]{1,0:T(8,128)S(1)}, bf16[328,128]{1,0:T(8,128)(2,1)S(1)}, bf16[328,128]{1,0:T(8,128)(2,1)S(1)}, bf16[328,128]{1,0:T(8,128)(2,1)S(1)}) custom-call(s32[6]{0:T(128)S(1)} %fusion.spot, f32[4,328,128]{2,1,0:T(8,128)S(1)} %get-tuple-element.104.own, bf16[4,328,128]{2,1,0:T(8,128)(2,1)S(1)} %collective-permute-done.9.one, ...), custom_call_target="tpu_custom_call" | custom-call | flops 1000000 | bytes 2099200 | tf_op jit(solution)/shard_map/pallas_call | solution.py:134
  49.7 1.4 %collective-permute-start.12 = (bf16[328,128]{1,0:T(8,128)(2,1)S(1)}, bf16[328,128]{1,0:T(8,128)(2,1)S(1)}, u32[]{:S(2)}, u32[]{:S(2)}) collective-permute-start(bf16[328,128]{1,0:T(8,128)(2,1)S(1)} %get-tuple-element.115), channel_id=1, source_target_pairs={{0,4},{1,5},{2,6},{3,7},{4,0},{5,1},{6,2},{7,3},{8,12},{9,13},{10,... | collective-permute-start | bytes 251912 | tf_op jit(solution)/shard_map/ppermute | solution.py:44
  51.1 2.5 %collective-permute-start.13 = (bf16[328,128]{1,0:T(8,128)(2,1)S(1)}, bf16[328,128]{1,0:T(8,128)(2,1)S(1)}, u32[]{:S(2)}, u32[]{:S(2)}) collective-permute-start(bf16[328,128]{1,0:T(8,128)(2,1)S(1)} %get-tuple-element.116), channel_id=1, source_target_pairs={{0,6},{1,7},{2,4},{3,5},{4,2},{5,3},{6,0},{7,1},{8,14},{9,15},{10,... | collective-permute-start | bytes 251912 | tf_op jit(solution)/shard_map/ppermute | solution.py:44
  53.6 0.7 collective-permute-start.15
  54.3 3.7 %collective-permute-start.16 = (bf16[2,64,1152]{2,1,0:T(8,128)(2,1)S(1)}, bf16[2,64,1152]{2,1,0:T(8,128)(2,1)S(1)}, u32[]{:S(2)}, u32[]{:S(2)}) collective-permute-start(bf16[2,64,1152]{2,1,0:T(8,128)(2,1)S(1)} %get-tuple-element.120), channel_id=1, source_target_pairs={{0,2},{1,3},{2,0},{3,1},{4,6},{5,7},{6,4},{7,5},{8,10},{9,11},{10,... | collective-permute-start | bytes 884744 | tf_op jit(solution)/shard_map/ppermute | solution.py:44
  58.0 3.0 %shard_map.98.refs_3_ = bf16[4,64,1152]{2,1,0:T(8,128)(2,1)S(1)} custom-call(bf16[8,64,3456]{2,1,0:T(8,128)(2,1)S(1)} %shard_map.95.d_ref, bf16[1152,3456]{1,0:T(8,128)(2,1)S(1)} %bitcast.6), custom_call_target="tpu_custom_call" | custom-call | flops 8000000000 | bytes 12091392 | tf_op jit(solution)/shard_map/pallas_call | solution.py:134
  61.1 2.4 %collective-permute-start.20 = (bf16[328,128]{1,0:T(8,128)(2,1)S(1)}, bf16[328,128]{1,0:T(8,128)(2,1)S(1)}, u32[]{:S(2)}, u32[]{:S(2)}) collective-permute-start(bf16[328,128]{1,0:T(8,128)(2,1)S(1)} %shard_map.99.last), channel_id=1, source_target_pairs={{0,24},{8,16},{16,8},{24,0},{1,25},{9,17},{17,9},{25,1},{2,26},{10... | collective-permute-start | bytes 251912 | tf_op jit(solution)/shard_map/ppermute | solution.py:44
  63.5 0.6 collective-permute-start.19
  64.1 0.5 collective-permute-start.18
  64.6 1.5 %collective-permute-done.16.refs_5_ = bf16[2,64,1152]{2,1,0:T(8,128)(2,1)S(1)} collective-permute-done((bf16[2,64,1152]{2,1,0:T(8,128)(2,1)S(1)}, bf16[2,64,1152]{2,1,0:T(8,128)(2,1)S(1)}, u32[]{:S(2)}, u32[]{:S(2)}) %collective-permute-start.16) | collective-permute-done | bytes 294944 | tf_op jit(solution)/shard_map/ppermute | solution.py:44
  66.2 0.7 %shard_map.100 = (bf16[4,64,1152]{2,1,0:T(8,128)(2,1)S(1)}, bf16[4,64,1152]{2,1,0:T(8,128)(2,1)S(1)}) custom-call(s32[6]{0:T(128)S(1)} %fusion.spot, bf16[4,64,1152]{2,1,0:T(8,128)(2,1)S(1)} %get-tuple-element.99.refs_0_, bf16[2,64,1152]{2,1,0:T(8,128)(2,1)S(1)} %collective-permute-done.7.refs_1_, bf16[2,64,1152]{2,1,0:T(8,128)(2,1)S(1)} %collective-permute-done.8.refs_2_, ...), custom_call_target="tpu_custom_call" | custom-call | flops 1000000 | bytes 3538944 | tf_op jit(solution)/shard_map/pallas_call | solution.py:134
  66.9 0.1 collective-permute-start.17
  67.0 0.4 collective-permute-done.20.three
  67.4 0.7 %collective-permute-done.19.two = bf16[328,128]{1,0:T(8,128)(2,1)S(1)} collective-permute-done((bf16[328,128]{1,0:T(8,128)(2,1)S(1)}, bf16[328,128]{1,0:T(8,128)(2,1)S(1)}, u32[]{:S(2)}, u32[]{:S(2)}) %collective-permute-start.19) | collective-permute-done | bytes 84000 | tf_op jit(solution)/shard_map/ppermute | solution.py:44
  68.1 0.5 collective-permute-done.18.one
  68.6 0.4 collective-permute-done.17.sib
  69.0 1.8 %shard_map.102 = (bf16[4,64,1152]{2,1,0:T(8,128)(2,1)}, bf16[4,64,1152]{2,1,0:T(8,128)(2,1)}, f32[144,1152]{1,0:T(8,128)}) custom-call(s32[6]{0:T(128)S(1)} %fusion.spot, bf16[4,64,1152]{2,1,0:T(8,128)(2,1)S(1)} %get-tuple-element.121.own, bf16[4,64,1152]{2,1,0:T(8,128)(2,1)S(1)} %collective-permute-done.17.sib, bf16[328,128]{1,0:T(8,128)(2,1)S(1)} %shard_map.99.last, ...), custom_call_target="tpu_custom_call" | custom-call | flops 1000000 | bytes 3362816 | tf_op jit(solution)/shard_map/pallas_call | solution.py:134
  (25 shorter events, 0.1 us)
Async XLA Ops:
  0.6 2.5 %collective-permute-start = (bf16[4,64,1152]{2,1,0:T(8,128)(2,1)}, bf16[4,64,1152]{2,1,0:T(8,128)(2,1)S(1)}, u32[]{:S(2)}, u32[]{:S(2)}) collective-permute-start(bf16[4,64,1152]{2,1,0:T(8,128)(2,1)} %bitcast.9), channel_id=1, source_target_pairs={{0,1},{1,0},{2,3},{3,2},{4,5},{5,4},{6,7},{7,6},{8,9},{9,8},{10,11... | collective-permute-start | bytes 1769480 | tf_op jit(solution)/shard_map/ppermute | solution.py:44
  1.1 12.1 %collective-permute-start.2 = (bf16[4,64,1152]{2,1,0:T(8,128)(2,1)}, bf16[4,64,1152]{2,1,0:T(8,128)(2,1)S(1)}, u32[]{:S(2)}, u32[]{:S(2)}) collective-permute-start(bf16[4,64,1152]{2,1,0:T(8,128)(2,1)} %bitcast.7), channel_id=1, source_target_pairs={{0,1},{1,0},{2,3},{3,2},{4,5},{5,4},{6,7},{7,6},{8,9},{9,8},{10,11... | collective-permute-start | bytes 1769480 | tf_op jit(solution)/shard_map/ppermute | solution.py:44
  2.0 8.5 %slice-start = ((s8[7962624]{0:T(1024)(128)(4,1)}), s8[4194304]{0:T(1024)(128)(4,1)S(1)}, s32[]{:S(2)}) async-start(s8[7962624]{0:T(1024)(128)(4,1)} %bitcast.5), calls=%async_computation | async-start | bytes 8388608
  3.1 7.4 %slice-start.1 = ((s8[7962624]{0:T(1024)(128)(4,1)}), s8[3768320]{0:T(1024)(128)(4,1)S(1)}, s32[]{:S(2)}) async-start(s8[7962624]{0:T(1024)(128)(4,1)} %bitcast.5), calls=%async_computation.1 | async-start | bytes 7536640
  3.8 13.8 %collective-permute-start.1 = (bf16[2,64,1152]{2,1,0:T(8,128)(2,1)S(1)}, bf16[2,64,1152]{2,1,0:T(8,128)(2,1)S(1)}, u32[]{:S(2)}, u32[]{:S(2)}) collective-permute-start(bf16[2,64,1152]{2,1,0:T(8,128)(2,1)S(1)} %get-tuple-element.65), channel_id=1, source_target_pairs={{0,0},{1,1},{2,4},{4,2},{3,5},{5,3},{6,6},{7,7},{8,8},{9,9},{10,12... | collective-permute-start | bytes 884744 | tf_op jit(solution)/shard_map/ppermute | solution.py:452
  4.6 13.3 %collective-permute-start.3 = (bf16[2,64,1152]{2,1,0:T(8,128)(2,1)S(1)}, bf16[2,64,1152]{2,1,0:T(8,128)(2,1)S(1)}, u32[]{:S(2)}, u32[]{:S(2)}) collective-permute-start(bf16[2,64,1152]{2,1,0:T(8,128)(2,1)S(1)} %get-tuple-element.70), channel_id=1, source_target_pairs={{0,2},{1,3},{2,0},{3,1},{4,6},{5,7},{6,4},{7,5},{8,10},{9,11},{10,... | collective-permute-start | bytes 884744 | tf_op jit(solution)/shard_map/ppermute | solution.py:44
  10.5 2.8 %copy-start.1 = (bf16[1,1,256,1152]{3,2,1,0:T(8,128)(2,1)S(1)}, bf16[1,1,256,1152]{3,2,1,0:T(8,128)(2,1)}, u32[]{:S(2)}) copy-start(bf16[1,1,256,1152]{3,2,1,0:T(8,128)(2,1)} %param.9) | copy-start | bytes 1769476
  10.5 6.1 %copy-start = (bf16[1152,1152]{1,0:T(8,128)(2,1)S(1)}, bf16[1152,1152]{1,0:T(8,128)(2,1)}, u32[]{:S(2)}) copy-start(bf16[1152,1152]{1,0:T(8,128)(2,1)} %w_ref.1) | copy-start | bytes 7962628
  13.2 4.7 %copy-start.2 = (bf16[16,1152]{1,0:T(8,128)(2,1)S(1)}, bf16[16,1152]{1,0:T(8,128)(2,1)}, u32[]{:S(2)}) copy-start(bf16[16,1152]{1,0:T(8,128)(2,1)} %constant.28.clone.heads_ref) | copy-start | bytes 110596
  13.9 10.7 %collective-permute-start.4 = (bf16[2,64,1152]{2,1,0:T(8,128)(2,1)S(1)}, bf16[2,64,1152]{2,1,0:T(8,128)(2,1)S(1)}, u32[]{:S(2)}, u32[]{:S(2)}) collective-permute-start(bf16[2,64,1152]{2,1,0:T(8,128)(2,1)S(1)} %get-tuple-element.73), channel_id=1, source_target_pairs={{0,0},{1,1},{2,4},{4,2},{3,5},{5,3},{6,6},{7,7},{8,8},{9,9},{10,12... | collective-permute-start | bytes 884744 | tf_op jit(solution)/shard_map/ppermute | solution.py:452
  14.7 9.8 %collective-permute-start.5 = (bf16[2,64,1152]{2,1,0:T(8,128)(2,1)S(1)}, bf16[2,64,1152]{2,1,0:T(8,128)(2,1)S(1)}, u32[]{:S(2)}, u32[]{:S(2)}) collective-permute-start(bf16[2,64,1152]{2,1,0:T(8,128)(2,1)S(1)} %get-tuple-element.74), channel_id=1, source_target_pairs={{0,2},{1,3},{2,0},{3,1},{4,6},{5,7},{6,4},{7,5},{8,10},{9,11},{10,... | collective-permute-start | bytes 884744 | tf_op jit(solution)/shard_map/ppermute | solution.py:44
  26.3 3.1 %collective-permute-start.6 = (bf16[4,144,1152]{2,1,0:T(8,128)(2,1)S(1)}, bf16[4,144,1152]{2,1,0:T(8,128)(2,1)S(1)}, u32[]{:S(2)}, u32[]{:S(2)}) collective-permute-start(bf16[4,144,1152]{2,1,0:T(8,128)(2,1)S(1)} %get-tuple-element.77), channel_id=1, source_target_pairs={{0,1},{1,0},{2,3},{3,2},{4,5},{5,4},{6,7},{7,6},{8,9},{9,8},{10,11... | collective-permute-start | bytes 3981320 | tf_op jit(solution)/shard_map/ppermute | solution.py:44
  30.4 18.4 %collective-permute-start.9 = (bf16[4,328,128]{2,1,0:T(8,128)(2,1)S(1)}, bf16[4,328,128]{2,1,0:T(8,128)(2,1)S(1)}, u32[]{:S(2)}, u32[]{:S(2)}) collective-permute-start(bf16[4,328,128]{2,1,0:T(8,128)(2,1)S(1)} %get-tuple-element.105), channel_id=1, source_target_pairs={{0,24},{8,16},{16,8},{24,0},{1,25},{9,17},{17,9},{25,1},{2,26},{10... | collective-permute-start | bytes 1007624 | tf_op jit(solution)/shard_map/ppermute | solution.py:44
  32.9 15.9 %collective-permute-start.10 = (bf16[4,328,128]{2,1,0:T(8,128)(2,1)S(1)}, bf16[4,328,128]{2,1,0:T(8,128)(2,1)S(1)}, u32[]{:S(2)}, u32[]{:S(2)}) collective-permute-start(bf16[4,328,128]{2,1,0:T(8,128)(2,1)S(1)} %get-tuple-element.106), channel_id=1, source_target_pairs={{0,8},{8,0},{16,24},{24,16},{1,9},{9,1},{17,25},{25,17},{2,10},{10... | collective-permute-start | bytes 1007624 | tf_op jit(solution)/shard_map/ppermute | solution.py:44
  33.5 15.4 %collective-permute-start.11 = (bf16[4,328,128]{2,1,0:T(8,128)(2,1)S(1)}, bf16[4,328,128]{2,1,0:T(8,128)(2,1)S(1)}, u32[]{:S(2)}, u32[]{:S(2)}) collective-permute-start(bf16[4,328,128]{2,1,0:T(8,128)(2,1)S(1)} %get-tuple-element.107), channel_id=1, source_target_pairs={{0,16},{8,24},{16,0},{24,8},{1,17},{9,25},{17,1},{25,9},{2,18},{10... | collective-permute-start | bytes 1007624 | tf_op jit(solution)/shard_map/ppermute | solution.py:44
  35.8 13.0 %collective-permute-start.7 = (bf16[2,64,1152]{2,1,0:T(8,128)(2,1)S(1)}, bf16[2,64,1152]{2,1,0:T(8,128)(2,1)S(1)}, u32[]{:S(2)}, u32[]{:S(2)}) collective-permute-start(bf16[2,64,1152]{2,1,0:T(8,128)(2,1)S(1)} %get-tuple-element.97), channel_id=1, source_target_pairs={{0,0},{1,1},{2,4},{4,2},{3,5},{5,3},{6,6},{7,7},{8,8},{9,9},{10,12... | collective-permute-start | bytes 884744 | tf_op jit(solution)/shard_map/ppermute | solution.py:452
  36.8 12.1 %collective-permute-start.8 = (bf16[2,64,1152]{2,1,0:T(8,128)(2,1)S(1)}, bf16[2,64,1152]{2,1,0:T(8,128)(2,1)S(1)}, u32[]{:S(2)}, u32[]{:S(2)}) collective-permute-start(bf16[2,64,1152]{2,1,0:T(8,128)(2,1)S(1)} %get-tuple-element.98), channel_id=1, source_target_pairs={{0,2},{1,3},{2,0},{3,1},{4,6},{5,7},{6,4},{7,5},{8,10},{9,11},{10,... | collective-permute-start | bytes 884744 | tf_op jit(solution)/shard_map/ppermute | solution.py:44
  49.7 11.3 %collective-permute-start.12 = (bf16[328,128]{1,0:T(8,128)(2,1)S(1)}, bf16[328,128]{1,0:T(8,128)(2,1)S(1)}, u32[]{:S(2)}, u32[]{:S(2)}) collective-permute-start(bf16[328,128]{1,0:T(8,128)(2,1)S(1)} %get-tuple-element.115), channel_id=1, source_target_pairs={{0,4},{1,5},{2,6},{3,7},{4,0},{5,1},{6,2},{7,3},{8,12},{9,13},{10,... | collective-permute-start | bytes 251912 | tf_op jit(solution)/shard_map/ppermute | solution.py:44
  51.1 9.9 %collective-permute-start.13 = (bf16[328,128]{1,0:T(8,128)(2,1)S(1)}, bf16[328,128]{1,0:T(8,128)(2,1)S(1)}, u32[]{:S(2)}, u32[]{:S(2)}) collective-permute-start(bf16[328,128]{1,0:T(8,128)(2,1)S(1)} %get-tuple-element.116), channel_id=1, source_target_pairs={{0,6},{1,7},{2,4},{3,5},{4,2},{5,3},{6,0},{7,1},{8,14},{9,15},{10,... | collective-permute-start | bytes 251912 | tf_op jit(solution)/shard_map/ppermute | solution.py:44
  53.6 7.4 %collective-permute-start.14 = (bf16[328,128]{1,0:T(8,128)(2,1)S(1)}, bf16[328,128]{1,0:T(8,128)(2,1)S(1)}, u32[]{:S(2)}, u32[]{:S(2)}) collective-permute-start(bf16[328,128]{1,0:T(8,128)(2,1)S(1)} %get-tuple-element.117), channel_id=1, source_target_pairs={{0,2},{1,3},{2,0},{3,1},{4,6},{5,7},{6,4},{7,5},{8,10},{9,11},{10,... | collective-permute-start | bytes 251912 | tf_op jit(solution)/shard_map/ppermute | solution.py:44
  53.6 11.0 %collective-permute-start.15 = (bf16[2,64,1152]{2,1,0:T(8,128)(2,1)S(1)}, bf16[2,64,1152]{2,1,0:T(8,128)(2,1)S(1)}, u32[]{:S(2)}, u32[]{:S(2)}) collective-permute-start(bf16[2,64,1152]{2,1,0:T(8,128)(2,1)S(1)} %get-tuple-element.119), channel_id=1, source_target_pairs={{0,0},{1,1},{2,4},{4,2},{3,5},{5,3},{6,6},{7,7},{8,8},{9,9},{10,12... | collective-permute-start | bytes 884744 | tf_op jit(solution)/shard_map/ppermute | solution.py:452
  54.3 11.8 %collective-permute-start.16 = (bf16[2,64,1152]{2,1,0:T(8,128)(2,1)S(1)}, bf16[2,64,1152]{2,1,0:T(8,128)(2,1)S(1)}, u32[]{:S(2)}, u32[]{:S(2)}) collective-permute-start(bf16[2,64,1152]{2,1,0:T(8,128)(2,1)S(1)} %get-tuple-element.120), channel_id=1, source_target_pairs={{0,2},{1,3},{2,0},{3,1},{4,6},{5,7},{6,4},{7,5},{8,10},{9,11},{10,... | collective-permute-start | bytes 884744 | tf_op jit(solution)/shard_map/ppermute | solution.py:44
  61.1 6.3 %collective-permute-start.20 = (bf16[328,128]{1,0:T(8,128)(2,1)S(1)}, bf16[328,128]{1,0:T(8,128)(2,1)S(1)}, u32[]{:S(2)}, u32[]{:S(2)}) collective-permute-start(bf16[328,128]{1,0:T(8,128)(2,1)S(1)} %shard_map.99.last), channel_id=1, source_target_pairs={{0,24},{8,16},{16,8},{24,0},{1,25},{9,17},{17,9},{25,1},{2,26},{10... | collective-permute-start | bytes 251912 | tf_op jit(solution)/shard_map/ppermute | solution.py:44
  63.5 4.6 %collective-permute-start.19 = (bf16[328,128]{1,0:T(8,128)(2,1)S(1)}, bf16[328,128]{1,0:T(8,128)(2,1)S(1)}, u32[]{:S(2)}, u32[]{:S(2)}) collective-permute-start(bf16[328,128]{1,0:T(8,128)(2,1)S(1)} %shard_map.99.last), channel_id=1, source_target_pairs={{0,16},{8,24},{16,0},{24,8},{1,17},{9,25},{17,1},{25,9},{2,18},{10... | collective-permute-start | bytes 251912 | tf_op jit(solution)/shard_map/ppermute | solution.py:44
  64.1 4.5 %collective-permute-start.18 = (bf16[328,128]{1,0:T(8,128)(2,1)S(1)}, bf16[328,128]{1,0:T(8,128)(2,1)S(1)}, u32[]{:S(2)}, u32[]{:S(2)}) collective-permute-start(bf16[328,128]{1,0:T(8,128)(2,1)S(1)} %shard_map.99.last), channel_id=1, source_target_pairs={{0,8},{8,0},{16,24},{24,16},{1,9},{9,1},{17,25},{25,17},{2,10},{10... | collective-permute-start | bytes 251912 | tf_op jit(solution)/shard_map/ppermute | solution.py:44
  66.9 2.1 %collective-permute-start.17 = (bf16[4,64,1152]{2,1,0:T(8,128)(2,1)S(1)}, bf16[4,64,1152]{2,1,0:T(8,128)(2,1)S(1)}, u32[]{:S(2)}, u32[]{:S(2)}) collective-permute-start(bf16[4,64,1152]{2,1,0:T(8,128)(2,1)S(1)} %get-tuple-element.122), channel_id=1, source_target_pairs={{0,1},{1,0},{2,3},{3,2},{4,5},{5,4},{6,7},{7,6},{8,9},{9,8},{10,11... | collective-permute-start | bytes 1769480 | tf_op jit(solution)/shard_map/ppermute | solution.py:44

commit v4 on v3

--- a/solution.py
+++ b/solution.py
@@ -526,7 +526,7 @@
         [(part, wide)],
     )
     grad, keep = after(grad, keep)
-    sends = [swap(sends[flip - 1], "seq", 2 * flip) for flip in (2, 3, 1)]
+    sends = [swap(x, "seq", 2 * flip) for flip, x in enumerate(sends, 1)]
     d_all, grad = after(d_all, grad)
     ours = functools.partial(latents_kernel, first=0)
     (own,) = call(ours, [], [d_all, in_weight], [four], limit=16, flops=8 * 10**9)

time: 71.2 us -> 70.7 us (level)
  starting transfers between devices: 29.8 us -> 28.9 us
    ppermute x17, starting transfers between devices: 26.6 us -> 25.7 us  [swap(): return lax.ppermute(value, axis, [(i, i ^ flip) for i in range(size)])]
  transfers between devices with their start and end apart: 21 -> 21, of which waited for: 7 -> 8; matrix products, arithmetic and copies ran while one was open for 3% -> 3% of each run, Pallas kernels for 40% -> 40%
where the time goes in v4:
time: 70.7 us; the launch traced here: 70.5 us
  Pallas kernels  33.8 us (48%)
  starting transfers between devices  28.9 us (41%)
  waiting for transfers between devices  4.73 us (7%)
  local copies, waits for them, and re-layouts  1.16 us (2%)
  between operations  1.09 us (2%)
  other arithmetic  0.73 us (1%)
    pallas_call x18, Pallas kernels, call(): pl.pallas_call(kernel, out_shape=list(outs), in_specs=[SMEM] * len(scalar...  33.8 us
    ppermute x17, starting transfers between devices, swap(): return lax.ppermute(value, axis, [(i, i ^ flip) for i in range(size)])  25.7 us
    ppermute x17, waiting for transfers between devices, swap(): return lax.ppermute(value, axis, [(i, i ^ flip) for i in range(size)])  4.72 us
    ppermute x4, starting transfers between devices, exchange(): return (lax.ppermute(far, 'seq', pairs), swap(near, 'seq', 2))  3.24 us
  transfers between devices with their start and end apart: 21, of which 8 were waited for; matrix products, arithmetic and copies ran while one was open for 3% of the time, Pallas kernels for 40%

profile of v4, /device:TPU:0, one launch (start us, length us, event | category | flops | bytes accessed | tf_op | source)
XLA Modules:
  0.0 70.5 jit_solution(17047088700999153725)
XLA Ops:
  0.6 0.5 collective-permute-start
  1.1 0.1 collective-permute-start.2
  1.2 0.7 %fusion.spot = s32[6]{0:T(128)S(1)} fusion(s32[4]{0:T(128)} %bitcast.11, s32[]{:T(128)S(6)} %axis_index.29, s32[]{:T(128)S(6)} %axis_index.26), kind=kLoop, calls=%fused_computation.2 | loop fusion | flops 30 | bytes 48 | tf_op jit(solution)/shard_map/add | solution.py:461
  2.0 1.1 %constant_dynamic-slice_fusion.own = bf16[2,64,1152]{2,1,0:T(8,128)(2,1)S(1)} fusion(bf16[4,64,1152]{2,1,0:T(8,128)(2,1)} %bitcast.10, s32[]{:T(128)S(6)} %select_n.21), kind=kLoop, calls=%fused_computation.3 | loop fusion | bytes 589828 | tf_op jit(solution)/shard_map/dynamic_slice | solution.py:474
  3.1 0.0 slice-start.1
  3.1 0.6 shard_map.85
  3.8 0.8 %collective-permute-start.1 = (bf16[2,64,1152]{2,1,0:T(8,128)(2,1)S(1)}, bf16[2,64,1152]{2,1,0:T(8,128)(2,1)S(1)}, u32[]{:S(2)}, u32[]{:S(2)}) collective-permute-start(bf16[2,64,1152]{2,1,0:T(8,128)(2,1)S(1)} %get-tuple-element.65), channel_id=1, source_target_pairs={{0,0},{1,1},{2,4},{4,2},{3,5},{5,3},{6,6},{7,7},{8,8},{9,9},{10,12... | collective-permute-start | bytes 884744 | tf_op jit(solution)/shard_map/ppermute | solution.py:452
  4.6 5.9 %collective-permute-start.3 = (bf16[2,64,1152]{2,1,0:T(8,128)(2,1)S(1)}, bf16[2,64,1152]{2,1,0:T(8,128)(2,1)S(1)}, u32[]{:S(2)}, u32[]{:S(2)}) collective-permute-start(bf16[2,64,1152]{2,1,0:T(8,128)(2,1)S(1)} %get-tuple-element.70), channel_id=1, source_target_pairs={{0,2},{1,3},{2,0},{3,1},{4,6},{5,7},{6,4},{7,5},{8,10},{9,11},{10,... | collective-permute-start | bytes 884744 | tf_op jit(solution)/shard_map/ppermute | solution.py:44
  10.5 2.7 %shard_map.86._ = bf16[8,64,3456]{2,1,0:T(8,128)(2,1)S(1)} custom-call(bf16[4,64,1152]{2,1,0:T(8,128)(2,1)S(1)} %get-tuple-element.66.lat_ab, bf16[1152,3456]{1,0:T(8,128)(2,1)S(1)} %bitcast.6), custom_call_target="tpu_custom_call" | custom-call | flops 2700000000 | bytes 12091392 | tf_op jit(solution)/shard_map/pallas_call | solution.py:134
  13.2 0.6 shard_map.87
  13.9 0.9 %collective-permute-start.4 = (bf16[2,64,1152]{2,1,0:T(8,128)(2,1)S(1)}, bf16[2,64,1152]{2,1,0:T(8,128)(2,1)S(1)}, u32[]{:S(2)}, u32[]{:S(2)}) collective-permute-start(bf16[2,64,1152]{2,1,0:T(8,128)(2,1)S(1)} %get-tuple-element.73), channel_id=1, source_target_pairs={{0,0},{1,1},{2,4},{4,2},{3,5},{5,3},{6,6},{7,7},{8,8},{9,9},{10,12... | collective-permute-start | bytes 884744 | tf_op jit(solution)/shard_map/ppermute | solution.py:452
  14.7 1.8 %collective-permute-start.5 = (bf16[2,64,1152]{2,1,0:T(8,128)(2,1)S(1)}, bf16[2,64,1152]{2,1,0:T(8,128)(2,1)S(1)}, u32[]{:S(2)}, u32[]{:S(2)}) collective-permute-start(bf16[2,64,1152]{2,1,0:T(8,128)(2,1)S(1)} %get-tuple-element.74), channel_id=1, source_target_pairs={{0,2},{1,3},{2,0},{3,1},{4,6},{5,7},{6,4},{7,5},{8,10},{9,11},{10,... | collective-permute-start | bytes 884744 | tf_op jit(solution)/shard_map/ppermute | solution.py:44
  16.5 1.0 %shard_map.88.refs_0_ = bf16[8,64,1152]{2,1,0:T(8,128)(2,1)S(1)} custom-call(bf16[4,64,1152]{2,1,0:T(8,128)(2,1)S(1)} %get-tuple-element.68.cot.ab_ref, bf16[1152,1152]{1,0:T(8,128)(2,1)S(1)} %copy-done), custom_call_target="tpu_custom_call" | custom-call | flops 700000000 | bytes 4423680 | tf_op jit(solution)/shard_map/pallas_call | solution.py:134
  17.6 0.3 collective-permute-done.3.near
  17.9 6.7 %shard_map.89 = (bf16[8,64,3456]{2,1,0:T(8,128)(2,1)S(1)}, bf16[8,64,1152]{2,1,0:T(8,128)(2,1)S(1)}, f32[16,2048]{1,0:T(8,128)S(1)}, bf16[2048,1152]{1,0:T(8,128)(2,1)S(1)}) custom-call(s32[6]{0:T(128)S(1)} %fusion.spot, bf16[2,64,1152]{2,1,0:T(8,128)(2,1)S(1)} %collective-permute-done.1.far, ...), custom_call_target="tpu_custom_call", output_to_operand_aliasing={{0}: (4, {})} | custom-call | flops 8000000000 | bytes 21696512 | tf_op jit(solution)/shard_map/pallas_call | solution.py:134
  24.6 1.7 %shard_map.90 = (bf16[4,144,1152]{2,1,0:T(8,128)(2,1)S(1)}, bf16[1152,512]{1,0:T(8,128)(2,1)S(1)}, bf16[8,64,1152]{2,1,0:T(8,128)(2,1)S(1)}) custom-call(s32[6]{0:T(128)S(1)} %fusion.spot, bf16[8,64,1152]{2,1,0:T(8,128)(2,1)S(1)} %get-tuple-element.87.att_ref, bf16[4,64,1152]{2,1,0:T(8,128)(2,1)S(1)} %get-tuple-element.68.cot.ab_ref, ...), custom_call_target="tpu_custom_call" | custom-call | flops 700000000 | bytes 6045696 | tf_op jit(solution)/shard_map/pallas_call | solution.py:134
  26.3 0.1 collective-permute-start.6
  26.4 1.0 %shard_map.92.ga_ref = bf16[8,64,1152]{2,1,0:T(8,128)(2,1)S(1)} custom-call(bf16[8,64,1152]{2,1,0:T(8,128)(2,1)S(1)} %get-tuple-element.78.cot, bf16[1152,1152]{1,0:T(8,128)(2,1)S(1)} %copy-done, bf16[8,64,1152]{2,1,0:T(8,128)(2,1)S(1)} %shard_map.88.refs_0_), custom_call_target="tpu_custom_call", output_to_operand_aliasing={{}: (2, {})} | custom-call | flops 700000000 | bytes 6193152 | tf_op jit(solution)/shard_map/pallas_call | solution.py:134
  27.5 1.5 %shard_map.91.mine = f32[5184,128]{1,0:T(8,128)S(1)} custom-call(s32[6]{0:T(128)S(1)} %fusion.spot, bf16[1152,512]{1,0:T(8,128)(2,1)S(1)} %get-tuple-element.75.att_t, bf16[8,64,1152]{2,1,0:T(8,128)(2,1)S(1)} %get-tuple-element.78.cot), custom_call_target="tpu_custom_call" | custom-call | flops 700000000 | bytes 5013504 | tf_op jit(solution)/shard_map/pallas_call | solution.py:134
  28.9 0.5 collective-permute-done.6.got
  29.5 1.0 %shard_map.93 = (f32[4,328,128]{2,1,0:T(8,128)S(1)}, bf16[4,328,128]{2,1,0:T(8,128)(2,1)S(1)}, bf16[4,328,128]{2,1,0:T(8,128)(2,1)S(1)}, bf16[4,328,128]{2,1,0:T(8,128)(2,1)S(1)}) custom-call(s32[6]{0:T(128)S(1)} %fusion.spot, f32[5184,128]{1,0:T(8,128)S(1)} %shard_map.91.mine, bf16[4,144,1152]{2,1,0:T(8,128)(2,1)S(1)} %collective-permute-done.6.got), custom_call_target="tpu_custom_call" | custom-call | flops 700000000 | bytes 5660672 | tf_op jit(solution)/shard_map/pallas_call | solution.py:134
  30.4 2.5 %collective-permute-start.9 = (bf16[4,328,128]{2,1,0:T(8,128)(2,1)S(1)}, bf16[4,328,128]{2,1,0:T(8,128)(2,1)S(1)}, u32[]{:S(2)}, u32[]{:S(2)}) collective-permute-start(bf16[4,328,128]{2,1,0:T(8,128)(2,1)S(1)} %get-tuple-element.105), channel_id=1, source_target_pairs={{0,24},{8,16},{16,8},{24,0},{1,25},{9,17},{17,9},{25,1},{2,26},{10... | collective-permute-start | bytes 1007624 | tf_op jit(solution)/shard_map/ppermute | solution.py:44
  32.9 0.6 collective-permute-start.10
  33.5 0.5 collective-permute-start.11
  34.0 1.9 %shard_map.94 = (bf16[4,64,1152]{2,1,0:T(8,128)(2,1)S(1)}, bf16[2,64,1152]{2,1,0:T(8,128)(2,1)S(1)}, bf16[2,64,1152]{2,1,0:T(8,128)(2,1)S(1)}) custom-call(bf16[8,64,1152]{2,1,0:T(8,128)(2,1)S(1)} %get-tuple-element.87.att_ref, bf16[1152,1152]{1,0:T(8,128)(2,1)S(1)} %copy-done), custom_call_target="tpu_custom_call" | custom-call | flops 1000000 | bytes 1000 | tf_op jit(solution)/shard_map/pallas_call | solution.py:134
  35.8 0.9 %collective-permute-start.7 = (bf16[2,64,1152]{2,1,0:T(8,128)(2,1)S(1)}, bf16[2,64,1152]{2,1,0:T(8,128)(2,1)S(1)}, u32[]{:S(2)}, u32[]{:S(2)}) collective-permute-start(bf16[2,64,1152]{2,1,0:T(8,128)(2,1)S(1)} %get-tuple-element.97), channel_id=1, source_target_pairs={{0,0},{1,1},{2,4},{4,2},{3,5},{5,3},{6,6},{7,7},{8,8},{9,9},{10,12... | collective-permute-start | bytes 884744 | tf_op jit(solution)/shard_map/ppermute | solution.py:452
  36.8 3.4 %collective-permute-start.8 = (bf16[2,64,1152]{2,1,0:T(8,128)(2,1)S(1)}, bf16[2,64,1152]{2,1,0:T(8,128)(2,1)S(1)}, u32[]{:S(2)}, u32[]{:S(2)}) collective-permute-start(bf16[2,64,1152]{2,1,0:T(8,128)(2,1)S(1)} %get-tuple-element.98), channel_id=1, source_target_pairs={{0,2},{1,3},{2,0},{3,1},{4,6},{5,7},{6,4},{7,5},{8,10},{9,11},{10,... | collective-permute-start | bytes 884744 | tf_op jit(solution)/shard_map/ppermute | solution.py:44
  40.2 5.6 %shard_map.95.d_ref = bf16[8,64,3456]{2,1,0:T(8,128)(2,1)S(1)} custom-call(s32[6]{0:T(128)S(1)} %fusion.spot, bf16[8,64,1152]{2,1,0:T(8,128)(2,1)S(1)} %shard_map.92.ga_ref, bf16[8,64,3456]{2,1,0:T(8,128)(2,1)S(1)} %get-tuple-element.91.qkv_ref, f32[16,2048]{1,0:T(8,128)S(1)} %get-tuple-element.92.p_ref, bf16[2048,1152]{1,0:T(8,128)(2,1)S(1)} %get-tuple-element.93.wide_ref, ...), custom_call_target="tpu_custom_call" | custom-call | flops 1000000 | bytes 1000 | tf_op jit(solution)/shard_map/pallas_call | solution.py:134
  45.8 3.0 %shard_map.96 = (bf16[2,64,1152]{2,1,0:T(8,128)(2,1)S(1)}, bf16[2,64,1152]{2,1,0:T(8,128)(2,1)S(1)}) custom-call(bf16[8,64,3456]{2,1,0:T(8,128)(2,1)S(1)} %shard_map.95.d_ref, bf16[1152,3456]{1,0:T(8,128)(2,1)S(1)} %bitcast.6), custom_call_target="tpu_custom_call" | custom-call | flops 1000000 | bytes 1000 | tf_op jit(solution)/shard_map/pallas_call | solution.py:134
  48.9 0.9 %shard_map.97 = (f32[328,128]{1,0:T(8,128)S(1)}, bf16[328,128]{1,0:T(8,128)(2,1)S(1)}, bf16[328,128]{1,0:T(8,128)(2,1)S(1)}, bf16[328,128]{1,0:T(8,128)(2,1)S(1)}) custom-call(s32[6]{0:T(128)S(1)} %fusion.spot, f32[4,328,128]{2,1,0:T(8,128)S(1)} %get-tuple-element.104.own, bf16[4,328,128]{2,1,0:T(8,128)(2,1)S(1)} %collective-permute-done.9.one, ...), custom_call_target="tpu_custom_call" | custom-call | flops 1000000 | bytes 2099200 | tf_op jit(solution)/shard_map/pallas_call | solution.py:134
  49.7 1.6 %collective-permute-start.12 = (bf16[328,128]{1,0:T(8,128)(2,1)S(1)}, bf16[328,128]{1,0:T(8,128)(2,1)S(1)}, u32[]{:S(2)}, u32[]{:S(2)}) collective-permute-start(bf16[328,128]{1,0:T(8,128)(2,1)S(1)} %get-tuple-element.115), channel_id=1, source_target_pairs={{0,2},{1,3},{2,0},{3,1},{4,6},{5,7},{6,4},{7,5},{8,10},{9,11},{10,... | collective-permute-start | bytes 251912 | tf_op jit(solution)/shard_map/ppermute | solution.py:44
  51.3 1.6 %collective-permute-start.13 = (bf16[328,128]{1,0:T(8,128)(2,1)S(1)}, bf16[328,128]{1,0:T(8,128)(2,1)S(1)}, u32[]{:S(2)}, u32[]{:S(2)}) collective-permute-start(bf16[328,128]{1,0:T(8,128)(2,1)S(1)} %get-tuple-element.116), channel_id=1, source_target_pairs={{0,4},{1,5},{2,6},{3,7},{4,0},{5,1},{6,2},{7,3},{8,12},{9,13},{10,... | collective-permute-start | bytes 251912 | tf_op jit(solution)/shard_map/ppermute | solution.py:44
  52.9 1.3 %collective-permute-start.14 = (bf16[328,128]{1,0:T(8,128)(2,1)S(1)}, bf16[328,128]{1,0:T(8,128)(2,1)S(1)}, u32[]{:S(2)}, u32[]{:S(2)}) collective-permute-start(bf16[328,128]{1,0:T(8,128)(2,1)S(1)} %get-tuple-element.117), channel_id=1, source_target_pairs={{0,6},{1,7},{2,4},{3,5},{4,2},{5,3},{6,0},{7,1},{8,14},{9,15},{10,... | collective-permute-start | bytes 251912 | tf_op jit(solution)/shard_map/ppermute | solution.py:44
  54.2 0.7 collective-permute-start.15
  54.8 2.3 %collective-permute-start.16 = (bf16[2,64,1152]{2,1,0:T(8,128)(2,1)S(1)}, bf16[2,64,1152]{2,1,0:T(8,128)(2,1)S(1)}, u32[]{:S(2)}, u32[]{:S(2)}) collective-permute-start(bf16[2,64,1152]{2,1,0:T(8,128)(2,1)S(1)} %get-tuple-element.120), channel_id=1, source_target_pairs={{0,2},{1,3},{2,0},{3,1},{4,6},{5,7},{6,4},{7,5},{8,10},{9,11},{10,... | collective-permute-start | bytes 884744 | tf_op jit(solution)/shard_map/ppermute | solution.py:44
  57.1 3.0 %shard_map.98.refs_3_ = bf16[4,64,1152]{2,1,0:T(8,128)(2,1)S(1)} custom-call(bf16[8,64,3456]{2,1,0:T(8,128)(2,1)S(1)} %shard_map.95.d_ref, bf16[1152,3456]{1,0:T(8,128)(2,1)S(1)} %bitcast.6), custom_call_target="tpu_custom_call" | custom-call | flops 8000000000 | bytes 12091392 | tf_op jit(solution)/shard_map/pallas_call | solution.py:134
  60.1 0.3 collective-permute-done.13.two
  60.5 2.4 %collective-permute-start.20 = (bf16[328,128]{1,0:T(8,128)(2,1)S(1)}, bf16[328,128]{1,0:T(8,128)(2,1)S(1)}, u32[]{:S(2)}, u32[]{:S(2)}) collective-permute-start(bf16[328,128]{1,0:T(8,128)(2,1)S(1)} %shard_map.99.last), channel_id=1, source_target_pairs={{0,24},{8,16},{16,8},{24,0},{1,25},{9,17},{17,9},{25,1},{2,26},{10... | collective-permute-start | bytes 251912 | tf_op jit(solution)/shard_map/ppermute | solution.py:44
  62.9 0.6 collective-permute-start.19
  63.5 0.5 collective-permute-start.18
  64.0 1.6 %collective-permute-done.16.refs_5_ = bf16[2,64,1152]{2,1,0:T(8,128)(2,1)S(1)} collective-permute-done((bf16[2,64,1152]{2,1,0:T(8,128)(2,1)S(1)}, bf16[2,64,1152]{2,1,0:T(8,128)(2,1)S(1)}, u32[]{:S(2)}, u32[]{:S(2)}) %collective-permute-start.16) | collective-permute-done | bytes 294944 | tf_op jit(solution)/shard_map/ppermute | solution.py:44
  65.6 0.7 %shard_map.100 = (bf16[4,64,1152]{2,1,0:T(8,128)(2,1)S(1)}, bf16[4,64,1152]{2,1,0:T(8,128)(2,1)S(1)}) custom-call(s32[6]{0:T(128)S(1)} %fusion.spot, bf16[4,64,1152]{2,1,0:T(8,128)(2,1)S(1)} %get-tuple-element.99.refs_0_, bf16[2,64,1152]{2,1,0:T(8,128)(2,1)S(1)} %collective-permute-done.7.refs_1_, bf16[2,64,1152]{2,1,0:T(8,128)(2,1)S(1)} %collective-permute-done.8.refs_2_, ...), custom_call_target="tpu_custom_call" | custom-call | flops 1000000 | bytes 3538944 | tf_op jit(solution)/shard_map/pallas_call | solution.py:134
  66.4 0.1 collective-permute-start.17
  66.5 0.1 collective-permute-done.20.three
  66.5 0.9 %collective-permute-done.19.two = bf16[328,128]{1,0:T(8,128)(2,1)S(1)} collective-permute-done((bf16[328,128]{1,0:T(8,128)(2,1)S(1)}, bf16[328,128]{1,0:T(8,128)(2,1)S(1)}, u32[]{:S(2)}, u32[]{:S(2)}) %collective-permute-start.19) | collective-permute-done | bytes 84000 | tf_op jit(solution)/shard_map/ppermute | solution.py:44
  67.4 0.5 collective-permute-done.18.one
  67.9 0.5 collective-permute-done.17.sib
  68.5 1.8 %shard_map.102 = (bf16[4,64,1152]{2,1,0:T(8,128)(2,1)}, bf16[4,64,1152]{2,1,0:T(8,128)(2,1)}, f32[144,1152]{1,0:T(8,128)}) custom-call(s32[6]{0:T(128)S(1)} %fusion.spot, bf16[4,64,1152]{2,1,0:T(8,128)(2,1)S(1)} %get-tuple-element.121.own, bf16[4,64,1152]{2,1,0:T(8,128)(2,1)S(1)} %collective-permute-done.17.sib, bf16[328,128]{1,0:T(8,128)(2,1)S(1)} %shard_map.99.last, ...), custom_call_target="tpu_custom_call" | custom-call | flops 1000000 | bytes 3362816 | tf_op jit(solution)/shard_map/pallas_call | solution.py:134
  (25 shorter events, 0.1 us)
Async XLA Ops:
  0.6 2.5 %collective-permute-start = (bf16[4,64,1152]{2,1,0:T(8,128)(2,1)}, bf16[4,64,1152]{2,1,0:T(8,128)(2,1)S(1)}, u32[]{:S(2)}, u32[]{:S(2)}) collective-permute-start(bf16[4,64,1152]{2,1,0:T(8,128)(2,1)} %bitcast.9), channel_id=1, source_target_pairs={{0,1},{1,0},{2,3},{3,2},{4,5},{5,4},{6,7},{7,6},{8,9},{9,8},{10,11... | collective-permute-start | bytes 1769480 | tf_op jit(solution)/shard_map/ppermute | solution.py:44
  1.1 12.1 %collective-permute-start.2 = (bf16[4,64,1152]{2,1,0:T(8,128)(2,1)}, bf16[4,64,1152]{2,1,0:T(8,128)(2,1)S(1)}, u32[]{:S(2)}, u32[]{:S(2)}) collective-permute-start(bf16[4,64,1152]{2,1,0:T(8,128)(2,1)} %bitcast.7), channel_id=1, source_target_pairs={{0,1},{1,0},{2,3},{3,2},{4,5},{5,4},{6,7},{7,6},{8,9},{9,8},{10,11... | collective-permute-start | bytes 1769480 | tf_op jit(solution)/shard_map/ppermute | solution.py:44
  2.0 8.5 %slice-start = ((s8[7962624]{0:T(1024)(128)(4,1)}), s8[4194304]{0:T(1024)(128)(4,1)S(1)}, s32[]{:S(2)}) async-start(s8[7962624]{0:T(1024)(128)(4,1)} %bitcast.5), calls=%async_computation | async-start | bytes 8388608
  3.1 7.4 %slice-start.1 = ((s8[7962624]{0:T(1024)(128)(4,1)}), s8[3768320]{0:T(1024)(128)(4,1)S(1)}, s32[]{:S(2)}) async-start(s8[7962624]{0:T(1024)(128)(4,1)} %bitcast.5), calls=%async_computation.1 | async-start | bytes 7536640
  3.8 13.8 %collective-permute-start.1 = (bf16[2,64,1152]{2,1,0:T(8,128)(2,1)S(1)}, bf16[2,64,1152]{2,1,0:T(8,128)(2,1)S(1)}, u32[]{:S(2)}, u32[]{:S(2)}) collective-permute-start(bf16[2,64,1152]{2,1,0:T(8,128)(2,1)S(1)} %get-tuple-element.65), channel_id=1, source_target_pairs={{0,0},{1,1},{2,4},{4,2},{3,5},{5,3},{6,6},{7,7},{8,8},{9,9},{10,12... | collective-permute-start | bytes 884744 | tf_op jit(solution)/shard_map/ppermute | solution.py:452
  4.6 13.3 %collective-permute-start.3 = (bf16[2,64,1152]{2,1,0:T(8,128)(2,1)S(1)}, bf16[2,64,1152]{2,1,0:T(8,128)(2,1)S(1)}, u32[]{:S(2)}, u32[]{:S(2)}) collective-permute-start(bf16[2,64,1152]{2,1,0:T(8,128)(2,1)S(1)} %get-tuple-element.70), channel_id=1, source_target_pairs={{0,2},{1,3},{2,0},{3,1},{4,6},{5,7},{6,4},{7,5},{8,10},{9,11},{10,... | collective-permute-start | bytes 884744 | tf_op jit(solution)/shard_map/ppermute | solution.py:44
  10.5 2.8 %copy-start.1 = (bf16[1,1,256,1152]{3,2,1,0:T(8,128)(2,1)S(1)}, bf16[1,1,256,1152]{3,2,1,0:T(8,128)(2,1)}, u32[]{:S(2)}) copy-start(bf16[1,1,256,1152]{3,2,1,0:T(8,128)(2,1)} %param.9) | copy-start | bytes 1769476
  10.5 6.1 %copy-start = (bf16[1152,1152]{1,0:T(8,128)(2,1)S(1)}, bf16[1152,1152]{1,0:T(8,128)(2,1)}, u32[]{:S(2)}) copy-start(bf16[1152,1152]{1,0:T(8,128)(2,1)} %w_ref.1) | copy-start | bytes 7962628
  13.2 4.7 %copy-start.2 = (bf16[16,1152]{1,0:T(8,128)(2,1)S(1)}, bf16[16,1152]{1,0:T(8,128)(2,1)}, u32[]{:S(2)}) copy-start(bf16[16,1152]{1,0:T(8,128)(2,1)} %constant.28.clone.heads_ref) | copy-start | bytes 110596
  13.9 10.7 %collective-permute-start.4 = (bf16[2,64,1152]{2,1,0:T(8,128)(2,1)S(1)}, bf16[2,64,1152]{2,1,0:T(8,128)(2,1)S(1)}, u32[]{:S(2)}, u32[]{:S(2)}) collective-permute-start(bf16[2,64,1152]{2,1,0:T(8,128)(2,1)S(1)} %get-tuple-element.73), channel_id=1, source_target_pairs={{0,0},{1,1},{2,4},{4,2},{3,5},{5,3},{6,6},{7,7},{8,8},{9,9},{10,12... | collective-permute-start | bytes 884744 | tf_op jit(solution)/shard_map/ppermute | solution.py:452
  14.7 9.8 %collective-permute-start.5 = (bf16[2,64,1152]{2,1,0:T(8,128)(2,1)S(1)}, bf16[2,64,1152]{2,1,0:T(8,128)(2,1)S(1)}, u32[]{:S(2)}, u32[]{:S(2)}) collective-permute-start(bf16[2,64,1152]{2,1,0:T(8,128)(2,1)S(1)} %get-tuple-element.74), channel_id=1, source_target_pairs={{0,2},{1,3},{2,0},{3,1},{4,6},{5,7},{6,4},{7,5},{8,10},{9,11},{10,... | collective-permute-start | bytes 884744 | tf_op jit(solution)/shard_map/ppermute | solution.py:44
  26.3 3.1 %collective-permute-start.6 = (bf16[4,144,1152]{2,1,0:T(8,128)(2,1)S(1)}, bf16[4,144,1152]{2,1,0:T(8,128)(2,1)S(1)}, u32[]{:S(2)}, u32[]{:S(2)}) collective-permute-start(bf16[4,144,1152]{2,1,0:T(8,128)(2,1)S(1)} %get-tuple-element.77), channel_id=1, source_target_pairs={{0,1},{1,0},{2,3},{3,2},{4,5},{5,4},{6,7},{7,6},{8,9},{9,8},{10,11... | collective-permute-start | bytes 3981320 | tf_op jit(solution)/shard_map/ppermute | solution.py:44
  30.4 18.4 %collective-permute-start.9 = (bf16[4,328,128]{2,1,0:T(8,128)(2,1)S(1)}, bf16[4,328,128]{2,1,0:T(8,128)(2,1)S(1)}, u32[]{:S(2)}, u32[]{:S(2)}) collective-permute-start(bf16[4,328,128]{2,1,0:T(8,128)(2,1)S(1)} %get-tuple-element.105), channel_id=1, source_target_pairs={{0,24},{8,16},{16,8},{24,0},{1,25},{9,17},{17,9},{25,1},{2,26},{10... | collective-permute-start | bytes 1007624 | tf_op jit(solution)/shard_map/ppermute | solution.py:44
  32.9 15.9 %collective-permute-start.10 = (bf16[4,328,128]{2,1,0:T(8,128)(2,1)S(1)}, bf16[4,328,128]{2,1,0:T(8,128)(2,1)S(1)}, u32[]{:S(2)}, u32[]{:S(2)}) collective-permute-start(bf16[4,328,128]{2,1,0:T(8,128)(2,1)S(1)} %get-tuple-element.106), channel_id=1, source_target_pairs={{0,8},{8,0},{16,24},{24,16},{1,9},{9,1},{17,25},{25,17},{2,10},{10... | collective-permute-start | bytes 1007624 | tf_op jit(solution)/shard_map/ppermute | solution.py:44
  33.5 15.4 %collective-permute-start.11 = (bf16[4,328,128]{2,1,0:T(8,128)(2,1)S(1)}, bf16[4,328,128]{2,1,0:T(8,128)(2,1)S(1)}, u32[]{:S(2)}, u32[]{:S(2)}) collective-permute-start(bf16[4,328,128]{2,1,0:T(8,128)(2,1)S(1)} %get-tuple-element.107), channel_id=1, source_target_pairs={{0,16},{8,24},{16,0},{24,8},{1,17},{9,25},{17,1},{25,9},{2,18},{10... | collective-permute-start | bytes 1007624 | tf_op jit(solution)/shard_map/ppermute | solution.py:44
  35.8 13.0 %collective-permute-start.7 = (bf16[2,64,1152]{2,1,0:T(8,128)(2,1)S(1)}, bf16[2,64,1152]{2,1,0:T(8,128)(2,1)S(1)}, u32[]{:S(2)}, u32[]{:S(2)}) collective-permute-start(bf16[2,64,1152]{2,1,0:T(8,128)(2,1)S(1)} %get-tuple-element.97), channel_id=1, source_target_pairs={{0,0},{1,1},{2,4},{4,2},{3,5},{5,3},{6,6},{7,7},{8,8},{9,9},{10,12... | collective-permute-start | bytes 884744 | tf_op jit(solution)/shard_map/ppermute | solution.py:452
  36.8 12.1 %collective-permute-start.8 = (bf16[2,64,1152]{2,1,0:T(8,128)(2,1)S(1)}, bf16[2,64,1152]{2,1,0:T(8,128)(2,1)S(1)}, u32[]{:S(2)}, u32[]{:S(2)}) collective-permute-start(bf16[2,64,1152]{2,1,0:T(8,128)(2,1)S(1)} %get-tuple-element.98), channel_id=1, source_target_pairs={{0,2},{1,3},{2,0},{3,1},{4,6},{5,7},{6,4},{7,5},{8,10},{9,11},{10,... | collective-permute-start | bytes 884744 | tf_op jit(solution)/shard_map/ppermute | solution.py:44
  49.7 10.4 %collective-permute-start.12 = (bf16[328,128]{1,0:T(8,128)(2,1)S(1)}, bf16[328,128]{1,0:T(8,128)(2,1)S(1)}, u32[]{:S(2)}, u32[]{:S(2)}) collective-permute-start(bf16[328,128]{1,0:T(8,128)(2,1)S(1)} %get-tuple-element.115), channel_id=1, source_target_pairs={{0,2},{1,3},{2,0},{3,1},{4,6},{5,7},{6,4},{7,5},{8,10},{9,11},{10,... | collective-permute-start | bytes 251912 | tf_op jit(solution)/shard_map/ppermute | solution.py:44
  51.3 9.1 %collective-permute-start.13 = (bf16[328,128]{1,0:T(8,128)(2,1)S(1)}, bf16[328,128]{1,0:T(8,128)(2,1)S(1)}, u32[]{:S(2)}, u32[]{:S(2)}) collective-permute-start(bf16[328,128]{1,0:T(8,128)(2,1)S(1)} %get-tuple-element.116), channel_id=1, source_target_pairs={{0,4},{1,5},{2,6},{3,7},{4,0},{5,1},{6,2},{7,3},{8,12},{9,13},{10,... | collective-permute-start | bytes 251912 | tf_op jit(solution)/shard_map/ppermute | solution.py:44
  52.9 7.5 %collective-permute-start.14 = (bf16[328,128]{1,0:T(8,128)(2,1)S(1)}, bf16[328,128]{1,0:T(8,128)(2,1)S(1)}, u32[]{:S(2)}, u32[]{:S(2)}) collective-permute-start(bf16[328,128]{1,0:T(8,128)(2,1)S(1)} %get-tuple-element.117), channel_id=1, source_target_pairs={{0,6},{1,7},{2,4},{3,5},{4,2},{5,3},{6,0},{7,1},{8,14},{9,15},{10,... | collective-permute-start | bytes 251912 | tf_op jit(solution)/shard_map/ppermute | solution.py:44
  54.2 9.9 %collective-permute-start.15 = (bf16[2,64,1152]{2,1,0:T(8,128)(2,1)S(1)}, bf16[2,64,1152]{2,1,0:T(8,128)(2,1)S(1)}, u32[]{:S(2)}, u32[]{:S(2)}) collective-permute-start(bf16[2,64,1152]{2,1,0:T(8,128)(2,1)S(1)} %get-tuple-element.119), channel_id=1, source_target_pairs={{0,0},{1,1},{2,4},{4,2},{3,5},{5,3},{6,6},{7,7},{8,8},{9,9},{10,12... | collective-permute-start | bytes 884744 | tf_op jit(solution)/shard_map/ppermute | solution.py:452
  54.8 10.8 %collective-permute-start.16 = (bf16[2,64,1152]{2,1,0:T(8,128)(2,1)S(1)}, bf16[2,64,1152]{2,1,0:T(8,128)(2,1)S(1)}, u32[]{:S(2)}, u32[]{:S(2)}) collective-permute-start(bf16[2,64,1152]{2,1,0:T(8,128)(2,1)S(1)} %get-tuple-element.120), channel_id=1, source_target_pairs={{0,2},{1,3},{2,0},{3,1},{4,6},{5,7},{6,4},{7,5},{8,10},{9,11},{10,... | collective-permute-start | bytes 884744 | tf_op jit(solution)/shard_map/ppermute | solution.py:44
  60.5 6.1 %collective-permute-start.20 = (bf16[328,128]{1,0:T(8,128)(2,1)S(1)}, bf16[328,128]{1,0:T(8,128)(2,1)S(1)}, u32[]{:S(2)}, u32[]{:S(2)}) collective-permute-start(bf16[328,128]{1,0:T(8,128)(2,1)S(1)} %shard_map.99.last), channel_id=1, source_target_pairs={{0,24},{8,16},{16,8},{24,0},{1,25},{9,17},{17,9},{25,1},{2,26},{10... | collective-permute-start | bytes 251912 | tf_op jit(solution)/shard_map/ppermute | solution.py:44
  62.9 4.5 %collective-permute-start.19 = (bf16[328,128]{1,0:T(8,128)(2,1)S(1)}, bf16[328,128]{1,0:T(8,128)(2,1)S(1)}, u32[]{:S(2)}, u32[]{:S(2)}) collective-permute-start(bf16[328,128]{1,0:T(8,128)(2,1)S(1)} %shard_map.99.last), channel_id=1, source_target_pairs={{0,16},{8,24},{16,0},{24,8},{1,17},{9,25},{17,1},{25,9},{2,18},{10... | collective-permute-start | bytes 251912 | tf_op jit(solution)/shard_map/ppermute | solution.py:44
  63.5 4.5 %collective-permute-start.18 = (bf16[328,128]{1,0:T(8,128)(2,1)S(1)}, bf16[328,128]{1,0:T(8,128)(2,1)S(1)}, u32[]{:S(2)}, u32[]{:S(2)}) collective-permute-start(bf16[328,128]{1,0:T(8,128)(2,1)S(1)} %shard_map.99.last), channel_id=1, source_target_pairs={{0,8},{8,0},{16,24},{24,16},{1,9},{9,1},{17,25},{25,17},{2,10},{10... | collective-permute-start | bytes 251912 | tf_op jit(solution)/shard_map/ppermute | solution.py:44
  66.4 2.1 %collective-permute-start.17 = (bf16[4,64,1152]{2,1,0:T(8,128)(2,1)S(1)}, bf16[4,64,1152]{2,1,0:T(8,128)(2,1)S(1)}, u32[]{:S(2)}, u32[]{:S(2)}) collective-permute-start(bf16[4,64,1152]{2,1,0:T(8,128)(2,1)S(1)} %get-tuple-element.122), channel_id=1, source_target_pairs={{0,1},{1,0},{2,3},{3,2},{4,5},{5,4},{6,7},{7,6},{8,9},{9,8},{10,11... | collective-permute-start | bytes 1769480 | tf_op jit(solution)/shard_map/ppermute | solution.py:44

commit v5 on v3

--- a/solution.py
+++ b/solution.py
@@ -217,7 +217,7 @@
 
 
 def forward_kernel(
-    spot, far, near, wi_ref, _, heads_ref, qkv_ref, att_ref, p_ref, wide_ref,
+    spot, near, far, wi_ref, _, heads_ref, qkv_ref, att_ref, p_ref, wide_ref,
     x_scr, hi_scr, w_scr,
 ):
     x_scr[:2] = near[...]
@@ -369,10 +369,10 @@
                 out[row] = source[block - first]
 
     for base in (0, 2):
-        sources = given[:3] if base == 0 else given[3:]
+        here, far, near = given[:3] if base == 0 else (given[3], given[5], given[4])
         for i in range(2):
-            put(own, base + i, jnp.where(core == 0, where[i], where[2 + i]), *sources)
-            put(sib, base + i, jnp.where(core == 0, where[2 + i], where[i]), *sources)
+            put(own, base + i, jnp.where(core == 0, where[i], where[2 + i]), here, far, near)
+            put(sib, base + i, jnp.where(core == 0, where[2 + i], where[i]), here, far, near)
 
 
 def first_row(group, block):
@@ -484,7 +484,7 @@
     pairs = 2 * PAIRS * ROWS
     products, columns = ((pairs, INNER), bf16), ((pairs, HEADS), bf16)
     qkv, att, probs, wides = call(
-        forward_kernel, [spot], [lat_far, lat_near, in_weight, qkv_ab, heads],
+        forward_kernel, [spot], [lat_near, lat_far, in_weight, qkv_ab, heads],
         [shaped((8, ROWS, 3 * INNER)), eight, shaped((HEADS, pairs), wide), shaped((pairs, INNER))],
         [((4, ROWS, width), bf16), products, columns], limit=24, flops=8 * 10**9, same=(3, 0),
     )
@@ -535,6 +535,7 @@
     (last,) = call(chips_kernel, [], [keep, *sends], [shaped(piece)])
     grad[0], last = after(grad[0], last)
     others = [swap(last, "dp", flip) for flip in (1, 2, 3)]
+    grad = [grad[0], grad[2], grad[1]]
     own, sib = call(settle_kernel, [spot], [*mixed, *grad], [four, four])
     (token,) = call(arrived_kernel, [], others, [shaped((16, TILE))], flops=8 * 10**9)
     mixed, grad, out_grad = call(

time: 71.2 us -> 71.6 us (level)
  waiting for transfers between devices: 4.34 us -> 6.21 us
  starting transfers between devices: 29.8 us -> 28.4 us
    ppermute x17, waiting for transfers between devices: 4.33 us -> 6.2 us  [swap(): return lax.ppermute(value, axis, [(i, i ^ flip) for i in range(size)])]
    ppermute x17, starting transfers between devices: 26.6 us -> 25.3 us  [swap(): return lax.ppermute(value, axis, [(i, i ^ flip) for i in range(size)])]
  transfers between devices with their start and end apart: 21 -> 21, of which waited for: 7 -> 8; matrix products, arithmetic and copies ran while one was open for 3% -> 3% of each run, Pallas kernels for 40% -> 40%
where the time goes in v5:
time: 71.6 us; the launch traced here: 71.4 us
  Pallas kernels  33.8 us (47%)
  starting transfers between devices  28.4 us (40%)
  waiting for transfers between devices  6.21 us (9%)
  local copies, waits for them, and re-layouts  1.17 us (2%)
  between operations  1.13 us (2%)
  other arithmetic  0.73 us (1%)
    pallas_call x18, Pallas kernels, call(): pl.pallas_call(kernel, out_shape=list(outs), in_specs=[SMEM] * len(scalar...  33.8 us
    ppermute x17, starting transfers between devices, swap(): return lax.ppermute(value, axis, [(i, i ^ flip) for i in range(size)])  25.3 us
    ppermute x17, waiting for transfers between devices, swap(): return lax.ppermute(value, axis, [(i, i ^ flip) for i in range(size)])  6.2 us
    ppermute x4, starting transfers between devices, exchange(): return (lax.ppermute(far, 'seq', pairs), swap(near, 'seq', 2))  3.09 us
  transfers between devices with their start and end apart: 21, of which 8 were waited for; matrix products, arithmetic and copies ran while one was open for 3% of the time, Pallas kernels for 40%

profile of v5, /device:TPU:0, one launch (start us, length us, event | category | flops | bytes accessed | tf_op | source)
XLA Modules:
  0.0 71.4 jit_solution(4601790580544899013)
XLA Ops:
  0.6 0.5 collective-permute-start
  1.1 0.1 collective-permute-start.3
  1.2 0.7 %fusion.spot = s32[6]{0:T(128)S(1)} fusion(s32[4]{0:T(128)} %bitcast.11, s32[]{:T(128)S(6)} %axis_index.29, s32[]{:T(128)S(6)} %axis_index.26), kind=kLoop, calls=%fused_computation.2 | loop fusion | flops 30 | bytes 48 | tf_op jit(solution)/shard_map/add | solution.py:461
  2.0 1.1 %constant_dynamic-slice_fusion.own = bf16[2,64,1152]{2,1,0:T(8,128)(2,1)S(1)} fusion(bf16[4,64,1152]{2,1,0:T(8,128)(2,1)} %bitcast.10, s32[]{:T(128)S(6)} %select_n.21), kind=kLoop, calls=%fused_computation.3 | loop fusion | bytes 589828 | tf_op jit(solution)/shard_map/dynamic_slice | solution.py:474
  3.1 0.0 slice-start.1
  3.1 0.6 shard_map.85
  3.8 3.1 %collective-permute-start.1 = (bf16[2,64,1152]{2,1,0:T(8,128)(2,1)S(1)}, bf16[2,64,1152]{2,1,0:T(8,128)(2,1)S(1)}, u32[]{:S(2)}, u32[]{:S(2)}) collective-permute-start(bf16[2,64,1152]{2,1,0:T(8,128)(2,1)S(1)} %get-tuple-element.65), channel_id=1, source_target_pairs={{0,2},{1,3},{2,0},{3,1},{4,6},{5,7},{6,4},{7,5},{8,10},{9,11},{10,... | collective-permute-start | bytes 884744 | tf_op jit(solution)/shard_map/ppermute | solution.py:44
  6.8 0.7 collective-permute-start.2
  7.6 2.7 %shard_map.86._ = bf16[8,64,3456]{2,1,0:T(8,128)(2,1)S(1)} custom-call(bf16[4,64,1152]{2,1,0:T(8,128)(2,1)S(1)} %get-tuple-element.67.lat_ab, bf16[1152,3456]{1,0:T(8,128)(2,1)S(1)} %bitcast.6), custom_call_target="tpu_custom_call" | custom-call | flops 2700000000 | bytes 12091392 | tf_op jit(solution)/shard_map/pallas_call | solution.py:134
  10.3 0.6 shard_map.87
  11.0 0.9 %collective-permute-start.4 = (bf16[2,64,1152]{2,1,0:T(8,128)(2,1)S(1)}, bf16[2,64,1152]{2,1,0:T(8,128)(2,1)S(1)}, u32[]{:S(2)}, u32[]{:S(2)}) collective-permute-start(bf16[2,64,1152]{2,1,0:T(8,128)(2,1)S(1)} %get-tuple-element.73), channel_id=1, source_target_pairs={{0,0},{1,1},{2,4},{4,2},{3,5},{5,3},{6,6},{7,7},{8,8},{9,9},{10,12... | collective-permute-start | bytes 884744 | tf_op jit(solution)/shard_map/ppermute | solution.py:452
  11.8 5.7 %collective-permute-start.5 = (bf16[2,64,1152]{2,1,0:T(8,128)(2,1)S(1)}, bf16[2,64,1152]{2,1,0:T(8,128)(2,1)S(1)}, u32[]{:S(2)}, u32[]{:S(2)}) collective-permute-start(bf16[2,64,1152]{2,1,0:T(8,128)(2,1)S(1)} %get-tuple-element.74), channel_id=1, source_target_pairs={{0,2},{1,3},{2,0},{3,1},{4,6},{5,7},{6,4},{7,5},{8,10},{9,11},{10,... | collective-permute-start | bytes 884744 | tf_op jit(solution)/shard_map/ppermute | solution.py:44
  17.5 1.0 %shard_map.88.refs_0_ = bf16[8,64,1152]{2,1,0:T(8,128)(2,1)S(1)} custom-call(bf16[4,64,1152]{2,1,0:T(8,128)(2,1)S(1)} %get-tuple-element.69.cot.ab_ref, bf16[1152,1152]{1,0:T(8,128)(2,1)S(1)} %copy-done), custom_call_target="tpu_custom_call" | custom-call | flops 700000000 | bytes 4423680 | tf_op jit(solution)/shard_map/pallas_call | solution.py:134
  18.6 6.6 %shard_map.89 = (bf16[8,64,3456]{2,1,0:T(8,128)(2,1)S(1)}, bf16[8,64,1152]{2,1,0:T(8,128)(2,1)S(1)}, f32[16,2048]{1,0:T(8,128)S(1)}, bf16[2048,1152]{1,0:T(8,128)(2,1)S(1)}) custom-call(s32[6]{0:T(128)S(1)} %fusion.spot, bf16[2,64,1152]{2,1,0:T(8,128)(2,1)S(1)} %collective-permute-done.1.near, ...), custom_call_target="tpu_custom_call", output_to_operand_aliasing={{0}: (4, {})} | custom-call | flops 8000000000 | bytes 21696512 | tf_op jit(solution)/shard_map/pallas_call | solution.py:134
  25.3 1.7 %shard_map.90 = (bf16[4,144,1152]{2,1,0:T(8,128)(2,1)S(1)}, bf16[1152,512]{1,0:T(8,128)(2,1)S(1)}, bf16[8,64,1152]{2,1,0:T(8,128)(2,1)S(1)}) custom-call(s32[6]{0:T(128)S(1)} %fusion.spot, bf16[8,64,1152]{2,1,0:T(8,128)(2,1)S(1)} %get-tuple-element.87.att_ref, bf16[4,64,1152]{2,1,0:T(8,128)(2,1)S(1)} %get-tuple-element.69.cot.ab_ref, ...), custom_call_target="tpu_custom_call" | custom-call | flops 700000000 | bytes 6045696 | tf_op jit(solution)/shard_map/pallas_call | solution.py:134
  27.0 0.1 collective-permute-start.6
  27.1 1.0 %shard_map.92.ga_ref = bf16[8,64,1152]{2,1,0:T(8,128)(2,1)S(1)} custom-call(bf16[8,64,1152]{2,1,0:T(8,128)(2,1)S(1)} %get-tuple-element.78.cot, bf16[1152,1152]{1,0:T(8,128)(2,1)S(1)} %copy-done, bf16[8,64,1152]{2,1,0:T(8,128)(2,1)S(1)} %shard_map.88.refs_0_), custom_call_target="tpu_custom_call", output_to_operand_aliasing={{}: (2, {})} | custom-call | flops 700000000 | bytes 6193152 | tf_op jit(solution)/shard_map/pallas_call | solution.py:134
  28.2 1.5 %shard_map.91.mine = f32[5184,128]{1,0:T(8,128)S(1)} custom-call(s32[6]{0:T(128)S(1)} %fusion.spot, bf16[1152,512]{1,0:T(8,128)(2,1)S(1)} %get-tuple-element.75.att_t, bf16[8,64,1152]{2,1,0:T(8,128)(2,1)S(1)} %get-tuple-element.78.cot), custom_call_target="tpu_custom_call" | custom-call | flops 700000000 | bytes 5013504 | tf_op jit(solution)/shard_map/pallas_call | solution.py:134
  29.6 0.5 collective-permute-done.6.got
  30.2 1.0 %shard_map.93 = (f32[4,328,128]{2,1,0:T(8,128)S(1)}, bf16[4,328,128]{2,1,0:T(8,128)(2,1)S(1)}, bf16[4,328,128]{2,1,0:T(8,128)(2,1)S(1)}, bf16[4,328,128]{2,1,0:T(8,128)(2,1)S(1)}) custom-call(s32[6]{0:T(128)S(1)} %fusion.spot, f32[5184,128]{1,0:T(8,128)S(1)} %shard_map.91.mine, bf16[4,144,1152]{2,1,0:T(8,128)(2,1)S(1)} %collective-permute-done.6.got), custom_call_target="tpu_custom_call" | custom-call | flops 700000000 | bytes 5660672 | tf_op jit(solution)/shard_map/pallas_call | solution.py:134
  31.1 2.5 %collective-permute-start.9 = (bf16[4,328,128]{2,1,0:T(8,128)(2,1)S(1)}, bf16[4,328,128]{2,1,0:T(8,128)(2,1)S(1)}, u32[]{:S(2)}, u32[]{:S(2)}) collective-permute-start(bf16[4,328,128]{2,1,0:T(8,128)(2,1)S(1)} %get-tuple-element.105), channel_id=1, source_target_pairs={{0,24},{8,16},{16,8},{24,0},{1,25},{9,17},{17,9},{25,1},{2,26},{10... | collective-permute-start | bytes 1007624 | tf_op jit(solution)/shard_map/ppermute | solution.py:44
  33.6 0.5 collective-permute-start.10
  34.2 0.5 collective-permute-start.11
  34.7 1.9 %shard_map.94 = (bf16[4,64,1152]{2,1,0:T(8,128)(2,1)S(1)}, bf16[2,64,1152]{2,1,0:T(8,128)(2,1)S(1)}, bf16[2,64,1152]{2,1,0:T(8,128)(2,1)S(1)}) custom-call(bf16[8,64,1152]{2,1,0:T(8,128)(2,1)S(1)} %get-tuple-element.87.att_ref, bf16[1152,1152]{1,0:T(8,128)(2,1)S(1)} %copy-done), custom_call_target="tpu_custom_call" | custom-call | flops 1000000 | bytes 1000 | tf_op jit(solution)/shard_map/pallas_call | solution.py:134
  36.5 0.9 %collective-permute-start.7 = (bf16[2,64,1152]{2,1,0:T(8,128)(2,1)S(1)}, bf16[2,64,1152]{2,1,0:T(8,128)(2,1)S(1)}, u32[]{:S(2)}, u32[]{:S(2)}) collective-permute-start(bf16[2,64,1152]{2,1,0:T(8,128)(2,1)S(1)} %get-tuple-element.97), channel_id=1, source_target_pairs={{0,0},{1,1},{2,4},{4,2},{3,5},{5,3},{6,6},{7,7},{8,8},{9,9},{10,12... | collective-permute-start | bytes 884744 | tf_op jit(solution)/shard_map/ppermute | solution.py:452
  37.4 4.2 %collective-permute-start.8 = (bf16[2,64,1152]{2,1,0:T(8,128)(2,1)S(1)}, bf16[2,64,1152]{2,1,0:T(8,128)(2,1)S(1)}, u32[]{:S(2)}, u32[]{:S(2)}) collective-permute-start(bf16[2,64,1152]{2,1,0:T(8,128)(2,1)S(1)} %get-tuple-element.98), channel_id=1, source_target_pairs={{0,2},{1,3},{2,0},{3,1},{4,6},{5,7},{6,4},{7,5},{8,10},{9,11},{10,... | collective-permute-start | bytes 884744 | tf_op jit(solution)/shard_map/ppermute | solution.py:44
  41.6 5.6 %shard_map.95.d_ref = bf16[8,64,3456]{2,1,0:T(8,128)(2,1)S(1)} custom-call(s32[6]{0:T(128)S(1)} %fusion.spot, bf16[8,64,1152]{2,1,0:T(8,128)(2,1)S(1)} %shard_map.92.ga_ref, bf16[8,64,3456]{2,1,0:T(8,128)(2,1)S(1)} %get-tuple-element.91.qkv_ref, f32[16,2048]{1,0:T(8,128)S(1)} %get-tuple-element.92.p_ref, bf16[2048,1152]{1,0:T(8,128)(2,1)S(1)} %get-tuple-element.93.wide_ref, ...), custom_call_target="tpu_custom_call" | custom-call | flops 1000000 | bytes 1000 | tf_op jit(solution)/shard_map/pallas_call | solution.py:134
  47.3 3.0 %shard_map.96 = (bf16[2,64,1152]{2,1,0:T(8,128)(2,1)S(1)}, bf16[2,64,1152]{2,1,0:T(8,128)(2,1)S(1)}) custom-call(bf16[8,64,3456]{2,1,0:T(8,128)(2,1)S(1)} %shard_map.95.d_ref, bf16[1152,3456]{1,0:T(8,128)(2,1)S(1)} %bitcast.6), custom_call_target="tpu_custom_call" | custom-call | flops 1000000 | bytes 1000 | tf_op jit(solution)/shard_map/pallas_call | solution.py:134
  50.3 0.9 %shard_map.97 = (f32[328,128]{1,0:T(8,128)S(1)}, bf16[328,128]{1,0:T(8,128)(2,1)S(1)}, bf16[328,128]{1,0:T(8,128)(2,1)S(1)}, bf16[328,128]{1,0:T(8,128)(2,1)S(1)}) custom-call(s32[6]{0:T(128)S(1)} %fusion.spot, f32[4,328,128]{2,1,0:T(8,128)S(1)} %get-tuple-element.104.own, bf16[4,328,128]{2,1,0:T(8,128)(2,1)S(1)} %collective-permute-done.9.one, ...), custom_call_target="tpu_custom_call" | custom-call | flops 1000000 | bytes 2099200 | tf_op jit(solution)/shard_map/pallas_call | solution.py:134
  51.2 1.4 %collective-permute-start.12 = (bf16[328,128]{1,0:T(8,128)(2,1)S(1)}, bf16[328,128]{1,0:T(8,128)(2,1)S(1)}, u32[]{:S(2)}, u32[]{:S(2)}) collective-permute-start(bf16[328,128]{1,0:T(8,128)(2,1)S(1)} %get-tuple-element.115), channel_id=1, source_target_pairs={{0,4},{1,5},{2,6},{3,7},{4,0},{5,1},{6,2},{7,3},{8,12},{9,13},{10,... | collective-permute-start | bytes 251912 | tf_op jit(solution)/shard_map/ppermute | solution.py:44
  52.5 1.1 %collective-permute-start.13 = (bf16[328,128]{1,0:T(8,128)(2,1)S(1)}, bf16[328,128]{1,0:T(8,128)(2,1)S(1)}, u32[]{:S(2)}, u32[]{:S(2)}) collective-permute-start(bf16[328,128]{1,0:T(8,128)(2,1)S(1)} %get-tuple-element.116), channel_id=1, source_target_pairs={{0,6},{1,7},{2,4},{3,5},{4,2},{5,3},{6,0},{7,1},{8,14},{9,15},{10,... | collective-permute-start | bytes 251912 | tf_op jit(solution)/shard_map/ppermute | solution.py:44
  53.6 1.1 %collective-permute-start.14 = (bf16[328,128]{1,0:T(8,128)(2,1)S(1)}, bf16[328,128]{1,0:T(8,128)(2,1)S(1)}, u32[]{:S(2)}, u32[]{:S(2)}) collective-permute-start(bf16[328,128]{1,0:T(8,128)(2,1)S(1)} %get-tuple-element.117), channel_id=1, source_target_pairs={{0,2},{1,3},{2,0},{3,1},{4,6},{5,7},{6,4},{7,5},{8,10},{9,11},{10,... | collective-permute-start | bytes 251912 | tf_op jit(solution)/shard_map/ppermute | solution.py:44
  54.7 0.9 %collective-permute-start.15 = (bf16[2,64,1152]{2,1,0:T(8,128)(2,1)S(1)}, bf16[2,64,1152]{2,1,0:T(8,128)(2,1)S(1)}, u32[]{:S(2)}, u32[]{:S(2)}) collective-permute-start(bf16[2,64,1152]{2,1,0:T(8,128)(2,1)S(1)} %get-tuple-element.119), channel_id=1, source_target_pairs={{0,2},{1,3},{2,0},{3,1},{4,6},{5,7},{6,4},{7,5},{8,10},{9,11},{10,... | collective-permute-start | bytes 884744 | tf_op jit(solution)/shard_map/ppermute | solution.py:44
  55.6 0.7 collective-permute-start.16
  56.3 3.0 %shard_map.98.refs_3_ = bf16[4,64,1152]{2,1,0:T(8,128)(2,1)S(1)} custom-call(bf16[8,64,3456]{2,1,0:T(8,128)(2,1)S(1)} %shard_map.95.d_ref, bf16[1152,3456]{1,0:T(8,128)(2,1)S(1)} %bitcast.6), custom_call_target="tpu_custom_call" | custom-call | flops 8000000000 | bytes 12091392 | tf_op jit(solution)/shard_map/pallas_call | solution.py:134
  59.3 0.4 collective-permute-done.12.one
  59.7 0.1 collective-permute-done.13.two
  59.7 1.3 %collective-permute-done.14.three = bf16[328,128]{1,0:T(8,128)(2,1)S(1)} collective-permute-done((bf16[328,128]{1,0:T(8,128)(2,1)S(1)}, bf16[328,128]{1,0:T(8,128)(2,1)S(1)}, u32[]{:S(2)}, u32[]{:S(2)}) %collective-permute-start.14) | collective-permute-done | bytes 84000 | tf_op jit(solution)/shard_map/ppermute | solution.py:44
  61.1 2.5 %collective-permute-start.20 = (bf16[328,128]{1,0:T(8,128)(2,1)S(1)}, bf16[328,128]{1,0:T(8,128)(2,1)S(1)}, u32[]{:S(2)}, u32[]{:S(2)}) collective-permute-start(bf16[328,128]{1,0:T(8,128)(2,1)S(1)} %shard_map.99.last), channel_id=1, source_target_pairs={{0,24},{8,16},{16,8},{24,0},{1,25},{9,17},{17,9},{25,1},{2,26},{10... | collective-permute-start | bytes 251912 | tf_op jit(solution)/shard_map/ppermute | solution.py:44
  63.6 0.5 collective-permute-start.19
  64.1 0.5 collective-permute-start.18
  64.6 2.0 %collective-permute-done.15.refs_4_ = bf16[2,64,1152]{2,1,0:T(8,128)(2,1)S(1)} collective-permute-done((bf16[2,64,1152]{2,1,0:T(8,128)(2,1)S(1)}, bf16[2,64,1152]{2,1,0:T(8,128)(2,1)S(1)}, u32[]{:S(2)}, u32[]{:S(2)}) %collective-permute-start.15) | collective-permute-done | bytes 294944 | tf_op jit(solution)/shard_map/ppermute | solution.py:44
  66.6 0.7 %shard_map.100 = (bf16[4,64,1152]{2,1,0:T(8,128)(2,1)S(1)}, bf16[4,64,1152]{2,1,0:T(8,128)(2,1)S(1)}) custom-call(s32[6]{0:T(128)S(1)} %fusion.spot, bf16[4,64,1152]{2,1,0:T(8,128)(2,1)S(1)} %get-tuple-element.99.refs_0_, bf16[2,64,1152]{2,1,0:T(8,128)(2,1)S(1)} %collective-permute-done.7.refs_1_, bf16[2,64,1152]{2,1,0:T(8,128)(2,1)S(1)} %collective-permute-done.8.refs_2_, ...), custom_call_target="tpu_custom_call" | custom-call | flops 1000000 | bytes 3538944 | tf_op jit(solution)/shard_map/pallas_call | solution.py:134
  67.3 0.1 collective-permute-start.17
  67.4 0.6 collective-permute-done.19.two
  68.0 0.5 collective-permute-done.18.one
  68.6 0.9 %collective-permute-done.17.sib = bf16[4,64,1152]{2,1,0:T(8,128)(2,1)S(1)} collective-permute-done((bf16[4,64,1152]{2,1,0:T(8,128)(2,1)S(1)}, bf16[4,64,1152]{2,1,0:T(8,128)(2,1)S(1)}, u32[]{:S(2)}, u32[]{:S(2)}) %collective-permute-start.17) | collective-permute-done | bytes 589856 | tf_op jit(solution)/shard_map/ppermute | solution.py:44
  69.4 1.8 %shard_map.102 = (bf16[4,64,1152]{2,1,0:T(8,128)(2,1)}, bf16[4,64,1152]{2,1,0:T(8,128)(2,1)}, f32[144,1152]{1,0:T(8,128)}) custom-call(s32[6]{0:T(128)S(1)} %fusion.spot, bf16[4,64,1152]{2,1,0:T(8,128)(2,1)S(1)} %get-tuple-element.121.own, bf16[4,64,1152]{2,1,0:T(8,128)(2,1)S(1)} %collective-permute-done.17.sib, bf16[328,128]{1,0:T(8,128)(2,1)S(1)} %shard_map.99.last, ...), custom_call_target="tpu_custom_call" | custom-call | flops 1000000 | bytes 3362816 | tf_op jit(solution)/shard_map/pallas_call | solution.py:134
  (25 shorter events, 0.1 us)
Async XLA Ops:
  0.6 2.5 %collective-permute-start = (bf16[4,64,1152]{2,1,0:T(8,128)(2,1)}, bf16[4,64,1152]{2,1,0:T(8,128)(2,1)S(1)}, u32[]{:S(2)}, u32[]{:S(2)}) collective-permute-start(bf16[4,64,1152]{2,1,0:T(8,128)(2,1)} %bitcast.9), channel_id=1, source_target_pairs={{0,1},{1,0},{2,3},{3,2},{4,5},{5,4},{6,7},{7,6},{8,9},{9,8},{10,11... | collective-permute-start | bytes 1769480 | tf_op jit(solution)/shard_map/ppermute | solution.py:44
  1.1 9.1 %collective-permute-start.3 = (bf16[4,64,1152]{2,1,0:T(8,128)(2,1)}, bf16[4,64,1152]{2,1,0:T(8,128)(2,1)S(1)}, u32[]{:S(2)}, u32[]{:S(2)}) collective-permute-start(bf16[4,64,1152]{2,1,0:T(8,128)(2,1)} %bitcast.7), channel_id=1, source_target_pairs={{0,1},{1,0},{2,3},{3,2},{4,5},{5,4},{6,7},{7,6},{8,9},{9,8},{10,11... | collective-permute-start | bytes 1769480 | tf_op jit(solution)/shard_map/ppermute | solution.py:44
  2.0 5.6 %slice-start = ((s8[7962624]{0:T(1024)(128)(4,1)}), s8[4194304]{0:T(1024)(128)(4,1)S(1)}, s32[]{:S(2)}) async-start(s8[7962624]{0:T(1024)(128)(4,1)} %bitcast.5), calls=%async_computation | async-start | bytes 8388608
  3.1 4.4 %slice-start.1 = ((s8[7962624]{0:T(1024)(128)(4,1)}), s8[3768320]{0:T(1024)(128)(4,1)S(1)}, s32[]{:S(2)}) async-start(s8[7962624]{0:T(1024)(128)(4,1)} %bitcast.5), calls=%async_computation.1 | async-start | bytes 7536640
  3.8 14.8 %collective-permute-start.1 = (bf16[2,64,1152]{2,1,0:T(8,128)(2,1)S(1)}, bf16[2,64,1152]{2,1,0:T(8,128)(2,1)S(1)}, u32[]{:S(2)}, u32[]{:S(2)}) collective-permute-start(bf16[2,64,1152]{2,1,0:T(8,128)(2,1)S(1)} %get-tuple-element.65), channel_id=1, source_target_pairs={{0,2},{1,3},{2,0},{3,1},{4,6},{5,7},{6,4},{7,5},{8,10},{9,11},{10,... | collective-permute-start | bytes 884744 | tf_op jit(solution)/shard_map/ppermute | solution.py:44
  6.8 11.7 %collective-permute-start.2 = (bf16[2,64,1152]{2,1,0:T(8,128)(2,1)S(1)}, bf16[2,64,1152]{2,1,0:T(8,128)(2,1)S(1)}, u32[]{:S(2)}, u32[]{:S(2)}) collective-permute-start(bf16[2,64,1152]{2,1,0:T(8,128)(2,1)S(1)} %get-tuple-element.66), channel_id=1, source_target_pairs={{0,0},{1,1},{2,4},{4,2},{3,5},{5,3},{6,6},{7,7},{8,8},{9,9},{10,12... | collective-permute-start | bytes 884744 | tf_op jit(solution)/shard_map/ppermute | solution.py:452
  7.5 2.8 %copy-start.1 = (bf16[1,1,256,1152]{3,2,1,0:T(8,128)(2,1)S(1)}, bf16[1,1,256,1152]{3,2,1,0:T(8,128)(2,1)}, u32[]{:S(2)}) copy-start(bf16[1,1,256,1152]{3,2,1,0:T(8,128)(2,1)} %param.9) | copy-start | bytes 1769476
  7.6 10.0 %copy-start = (bf16[1152,1152]{1,0:T(8,128)(2,1)S(1)}, bf16[1152,1152]{1,0:T(8,128)(2,1)}, u32[]{:S(2)}) copy-start(bf16[1152,1152]{1,0:T(8,128)(2,1)} %w_ref.1) | copy-start | bytes 7962628
  10.3 8.3 %copy-start.2 = (bf16[16,1152]{1,0:T(8,128)(2,1)S(1)}, bf16[16,1152]{1,0:T(8,128)(2,1)}, u32[]{:S(2)}) copy-start(bf16[16,1152]{1,0:T(8,128)(2,1)} %constant.28.clone.heads_ref) | copy-start | bytes 110596
  11.0 14.3 %collective-permute-start.4 = (bf16[2,64,1152]{2,1,0:T(8,128)(2,1)S(1)}, bf16[2,64,1152]{2,1,0:T(8,128)(2,1)S(1)}, u32[]{:S(2)}, u32[]{:S(2)}) collective-permute-start(bf16[2,64,1152]{2,1,0:T(8,128)(2,1)S(1)} %get-tuple-element.73), channel_id=1, source_target_pairs={{0,0},{1,1},{2,4},{4,2},{3,5},{5,3},{6,6},{7,7},{8,8},{9,9},{10,12... | collective-permute-start | bytes 884744 | tf_op jit(solution)/shard_map/ppermute | solution.py:452
  11.8 13.4 %collective-permute-start.5 = (bf16[2,64,1152]{2,1,0:T(8,128)(2,1)S(1)}, bf16[2,64,1152]{2,1,0:T(8,128)(2,1)S(1)}, u32[]{:S(2)}, u32[]{:S(2)}) collective-permute-start(bf16[2,64,1152]{2,1,0:T(8,128)(2,1)S(1)} %get-tuple-element.74), channel_id=1, source_target_pairs={{0,2},{1,3},{2,0},{3,1},{4,6},{5,7},{6,4},{7,5},{8,10},{9,11},{10,... | collective-permute-start | bytes 884744 | tf_op jit(solution)/shard_map/ppermute | solution.py:44
  27.0 3.1 %collective-permute-start.6 = (bf16[4,144,1152]{2,1,0:T(8,128)(2,1)S(1)}, bf16[4,144,1152]{2,1,0:T(8,128)(2,1)S(1)}, u32[]{:S(2)}, u32[]{:S(2)}) collective-permute-start(bf16[4,144,1152]{2,1,0:T(8,128)(2,1)S(1)} %get-tuple-element.77), channel_id=1, source_target_pairs={{0,1},{1,0},{2,3},{3,2},{4,5},{5,4},{6,7},{7,6},{8,9},{9,8},{10,11... | collective-permute-start | bytes 3981320 | tf_op jit(solution)/shard_map/ppermute | solution.py:44
  31.1 19.2 %collective-permute-start.9 = (bf16[4,328,128]{2,1,0:T(8,128)(2,1)S(1)}, bf16[4,328,128]{2,1,0:T(8,128)(2,1)S(1)}, u32[]{:S(2)}, u32[]{:S(2)}) collective-permute-start(bf16[4,328,128]{2,1,0:T(8,128)(2,1)S(1)} %get-tuple-element.105), channel_id=1, source_target_pairs={{0,24},{8,16},{16,8},{24,0},{1,25},{9,17},{17,9},{25,1},{2,26},{10... | collective-permute-start | bytes 1007624 | tf_op jit(solution)/shard_map/ppermute | solution.py:44
  33.6 16.7 %collective-permute-start.10 = (bf16[4,328,128]{2,1,0:T(8,128)(2,1)S(1)}, bf16[4,328,128]{2,1,0:T(8,128)(2,1)S(1)}, u32[]{:S(2)}, u32[]{:S(2)}) collective-permute-start(bf16[4,328,128]{2,1,0:T(8,128)(2,1)S(1)} %get-tuple-element.106), channel_id=1, source_target_pairs={{0,8},{8,0},{16,24},{24,16},{1,9},{9,1},{17,25},{25,17},{2,10},{10... | collective-permute-start | bytes 1007624 | tf_op jit(solution)/shard_map/ppermute | solution.py:44
  34.2 16.1 %collective-permute-start.11 = (bf16[4,328,128]{2,1,0:T(8,128)(2,1)S(1)}, bf16[4,328,128]{2,1,0:T(8,128)(2,1)S(1)}, u32[]{:S(2)}, u32[]{:S(2)}) collective-permute-start(bf16[4,328,128]{2,1,0:T(8,128)(2,1)S(1)} %get-tuple-element.107), channel_id=1, source_target_pairs={{0,16},{8,24},{16,0},{24,8},{1,17},{9,25},{17,1},{25,9},{2,18},{10... | collective-permute-start | bytes 1007624 | tf_op jit(solution)/shard_map/ppermute | solution.py:44
  36.5 13.7 %collective-permute-start.7 = (bf16[2,64,1152]{2,1,0:T(8,128)(2,1)S(1)}, bf16[2,64,1152]{2,1,0:T(8,128)(2,1)S(1)}, u32[]{:S(2)}, u32[]{:S(2)}) collective-permute-start(bf16[2,64,1152]{2,1,0:T(8,128)(2,1)S(1)} %get-tuple-element.97), channel_id=1, source_target_pairs={{0,0},{1,1},{2,4},{4,2},{3,5},{5,3},{6,6},{7,7},{8,8},{9,9},{10,12... | collective-permute-start | bytes 884744 | tf_op jit(solution)/shard_map/ppermute | solution.py:452
  37.4 12.8 %collective-permute-start.8 = (bf16[2,64,1152]{2,1,0:T(8,128)(2,1)S(1)}, bf16[2,64,1152]{2,1,0:T(8,128)(2,1)S(1)}, u32[]{:S(2)}, u32[]{:S(2)}) collective-permute-start(bf16[2,64,1152]{2,1,0:T(8,128)(2,1)S(1)} %get-tuple-element.98), channel_id=1, source_target_pairs={{0,2},{1,3},{2,0},{3,1},{4,6},{5,7},{6,4},{7,5},{8,10},{9,11},{10,... | collective-permute-start | bytes 884744 | tf_op jit(solution)/shard_map/ppermute | solution.py:44
  51.2 8.5 %collective-permute-start.12 = (bf16[328,128]{1,0:T(8,128)(2,1)S(1)}, bf16[328,128]{1,0:T(8,128)(2,1)S(1)}, u32[]{:S(2)}, u32[]{:S(2)}) collective-permute-start(bf16[328,128]{1,0:T(8,128)(2,1)S(1)} %get-tuple-element.115), channel_id=1, source_target_pairs={{0,4},{1,5},{2,6},{3,7},{4,0},{5,1},{6,2},{7,3},{8,12},{9,13},{10,... | collective-permute-start | bytes 251912 | tf_op jit(solution)/shard_map/ppermute | solution.py:44
  52.5 7.2 %collective-permute-start.13 = (bf16[328,128]{1,0:T(8,128)(2,1)S(1)}, bf16[328,128]{1,0:T(8,128)(2,1)S(1)}, u32[]{:S(2)}, u32[]{:S(2)}) collective-permute-start(bf16[328,128]{1,0:T(8,128)(2,1)S(1)} %get-tuple-element.116), channel_id=1, source_target_pairs={{0,6},{1,7},{2,4},{3,5},{4,2},{5,3},{6,0},{7,1},{8,14},{9,15},{10,... | collective-permute-start | bytes 251912 | tf_op jit(solution)/shard_map/ppermute | solution.py:44
  53.6 7.4 %collective-permute-start.14 = (bf16[328,128]{1,0:T(8,128)(2,1)S(1)}, bf16[328,128]{1,0:T(8,128)(2,1)S(1)}, u32[]{:S(2)}, u32[]{:S(2)}) collective-permute-start(bf16[328,128]{1,0:T(8,128)(2,1)S(1)} %get-tuple-element.117), channel_id=1, source_target_pairs={{0,2},{1,3},{2,0},{3,1},{4,6},{5,7},{6,4},{7,5},{8,10},{9,11},{10,... | collective-permute-start | bytes 251912 | tf_op jit(solution)/shard_map/ppermute | solution.py:44
  54.7 11.9 %collective-permute-start.15 = (bf16[2,64,1152]{2,1,0:T(8,128)(2,1)S(1)}, bf16[2,64,1152]{2,1,0:T(8,128)(2,1)S(1)}, u32[]{:S(2)}, u32[]{:S(2)}) collective-permute-start(bf16[2,64,1152]{2,1,0:T(8,128)(2,1)S(1)} %get-tuple-element.119), channel_id=1, source_target_pairs={{0,2},{1,3},{2,0},{3,1},{4,6},{5,7},{6,4},{7,5},{8,10},{9,11},{10,... | collective-permute-start | bytes 884744 | tf_op jit(solution)/shard_map/ppermute | solution.py:44
  55.6 11.0 %collective-permute-start.16 = (bf16[2,64,1152]{2,1,0:T(8,128)(2,1)S(1)}, bf16[2,64,1152]{2,1,0:T(8,128)(2,1)S(1)}, u32[]{:S(2)}, u32[]{:S(2)}) collective-permute-start(bf16[2,64,1152]{2,1,0:T(8,128)(2,1)S(1)} %get-tuple-element.120), channel_id=1, source_target_pairs={{0,0},{1,1},{2,4},{4,2},{3,5},{5,3},{6,6},{7,7},{8,8},{9,9},{10,12... | collective-permute-start | bytes 884744 | tf_op jit(solution)/shard_map/ppermute | solution.py:452
  61.1 6.4 %collective-permute-start.20 = (bf16[328,128]{1,0:T(8,128)(2,1)S(1)}, bf16[328,128]{1,0:T(8,128)(2,1)S(1)}, u32[]{:S(2)}, u32[]{:S(2)}) collective-permute-start(bf16[328,128]{1,0:T(8,128)(2,1)S(1)} %shard_map.99.last), channel_id=1, source_target_pairs={{0,24},{8,16},{16,8},{24,0},{1,25},{9,17},{17,9},{25,1},{2,26},{10... | collective-permute-start | bytes 251912 | tf_op jit(solution)/shard_map/ppermute | solution.py:44
  63.6 4.5 %collective-permute-start.19 = (bf16[328,128]{1,0:T(8,128)(2,1)S(1)}, bf16[328,128]{1,0:T(8,128)(2,1)S(1)}, u32[]{:S(2)}, u32[]{:S(2)}) collective-permute-start(bf16[328,128]{1,0:T(8,128)(2,1)S(1)} %shard_map.99.last), channel_id=1, source_target_pairs={{0,16},{8,24},{16,0},{24,8},{1,17},{9,25},{17,1},{25,9},{2,18},{10... | collective-permute-start | bytes 251912 | tf_op jit(solution)/shard_map/ppermute | solution.py:44
  64.1 4.5 %collective-permute-start.18 = (bf16[328,128]{1,0:T(8,128)(2,1)S(1)}, bf16[328,128]{1,0:T(8,128)(2,1)S(1)}, u32[]{:S(2)}, u32[]{:S(2)}) collective-permute-start(bf16[328,128]{1,0:T(8,128)(2,1)S(1)} %shard_map.99.last), channel_id=1, source_target_pairs={{0,8},{8,0},{16,24},{24,16},{1,9},{9,1},{17,25},{25,17},{2,10},{10... | collective-permute-start | bytes 251912 | tf_op jit(solution)/shard_map/ppermute | solution.py:44
  67.3 2.1 %collective-permute-start.17 = (bf16[4,64,1152]{2,1,0:T(8,128)(2,1)S(1)}, bf16[4,64,1152]{2,1,0:T(8,128)(2,1)S(1)}, u32[]{:S(2)}, u32[]{:S(2)}) collective-permute-start(bf16[4,64,1152]{2,1,0:T(8,128)(2,1)S(1)} %get-tuple-element.122), channel_id=1, source_target_pairs={{0,1},{1,0},{2,3},{3,2},{4,5},{5,4},{6,7},{7,6},{8,9},{9,8},{10,11... | collective-permute-start | bytes 1769480 | tf_op jit(solution)/shard_map/ppermute | solution.py:44

commit v6 on v2

--- a/solution.py
+++ b/solution.py
@@ -521,7 +521,7 @@
         [(part, wide)],
     )
     grad, keep = after(grad, keep)
-    sends = [swap(x, "seq", 2 * flip) for flip, x in enumerate(sends, 1)]
+    sends = [swap(sends[flip - 1], "seq", 2 * flip) for flip in (3, 1, 2)]
     d_all, grad = after(d_all, grad)
     ours = functools.partial(latents_kernel, first=0)
     (own,) = call(ours, [], [d_all, in_weight], [four], limit=16, flops=8 * 10**9)

time: 70.8 us -> 71.5 us (level)
  no operation moved by 1% of the time
where the time goes in v6:
time: 71.5 us; the launch traced here: 71.3 us
  Pallas kernels  34.5 us (48%)
  starting transfers between devices  29.6 us (41%)
  waiting for transfers between devices  4.26 us (6%)
  local copies, waits for them, and re-layouts  1.16 us (2%)
  between operations  1.11 us (2%)
  other arithmetic  0.73 us (1%)
    pallas_call x18, Pallas kernels, call(): pl.pallas_call(kernel, out_shape=list(outs), in_specs=[SMEM] * len(scalar...  34.5 us
    ppermute x17, starting transfers between devices, swap(): return lax.ppermute(value, axis, [(i, i ^ flip) for i in range(size)])  26.3 us
    ppermute x17, waiting for transfers between devices, swap(): return lax.ppermute(value, axis, [(i, i ^ flip) for i in range(size)])  4.25 us
    ppermute x4, starting transfers between devices, exchange(): return (lax.ppermute(far, 'seq', pairs), swap(near, 'seq', 2))  3.24 us
  transfers between devices with their start and end apart: 21, of which 7 were waited for; matrix products, arithmetic and copies ran while one was open for 3% of the time, Pallas kernels for 41%

profile of v6, /device:TPU:0, one launch (start us, length us, event | category | flops | bytes accessed | tf_op | source)
XLA Modules:
  0.0 71.3 jit_solution(17636051974709724795)
XLA Ops:
  0.6 0.5 collective-permute-start
  1.1 0.1 collective-permute-start.2
  1.2 0.7 %fusion.spot = s32[6]{0:T(128)S(1)} fusion(s32[4]{0:T(128)} %bitcast.11, s32[]{:T(128)S(6)} %axis_index.29, s32[]{:T(128)S(6)} %axis_index.26), kind=kLoop, calls=%fused_computation.2 | loop fusion | flops 30 | bytes 48 | tf_op jit(solution)/shard_map/add | solution.py:456
  2.0 1.1 %constant_dynamic-slice_fusion.own = bf16[2,64,1152]{2,1,0:T(8,128)(2,1)S(1)} fusion(bf16[4,64,1152]{2,1,0:T(8,128)(2,1)} %bitcast.10, s32[]{:T(128)S(6)} %select_n.21), kind=kLoop, calls=%fused_computation.3 | loop fusion | bytes 589828 | tf_op jit(solution)/shard_map/dynamic_slice | solution.py:469
  3.1 0.0 slice-start.1
  3.1 0.6 shard_map.85
  3.8 0.8 %collective-permute-start.1 = (bf16[2,64,1152]{2,1,0:T(8,128)(2,1)S(1)}, bf16[2,64,1152]{2,1,0:T(8,128)(2,1)S(1)}, u32[]{:S(2)}, u32[]{:S(2)}) collective-permute-start(bf16[2,64,1152]{2,1,0:T(8,128)(2,1)S(1)} %get-tuple-element.65), channel_id=1, source_target_pairs={{0,0},{1,1},{2,4},{4,2},{3,5},{5,3},{6,6},{7,7},{8,8},{9,9},{10,12... | collective-permute-start | bytes 884744 | tf_op jit(solution)/shard_map/ppermute | solution.py:447
  4.6 5.9 %collective-permute-start.3 = (bf16[2,64,1152]{2,1,0:T(8,128)(2,1)S(1)}, bf16[2,64,1152]{2,1,0:T(8,128)(2,1)S(1)}, u32[]{:S(2)}, u32[]{:S(2)}) collective-permute-start(bf16[2,64,1152]{2,1,0:T(8,128)(2,1)S(1)} %get-tuple-element.70), channel_id=1, source_target_pairs={{0,2},{1,3},{2,0},{3,1},{4,6},{5,7},{6,4},{7,5},{8,10},{9,11},{10,... | collective-permute-start | bytes 884744 | tf_op jit(solution)/shard_map/ppermute | solution.py:44
  10.5 2.7 %shard_map.86._ = bf16[8,64,3456]{2,1,0:T(8,128)(2,1)S(1)} custom-call(bf16[4,64,1152]{2,1,0:T(8,128)(2,1)S(1)} %get-tuple-element.66.lat_ab, bf16[1152,3456]{1,0:T(8,128)(2,1)S(1)} %bitcast.6), custom_call_target="tpu_custom_call" | custom-call | flops 2700000000 | bytes 12091392 | tf_op jit(solution)/shard_map/pallas_call | solution.py:134
  13.2 0.0 copy-start.2
  13.2 0.6 shard_map.87
  13.9 0.9 %collective-permute-start.4 = (bf16[2,64,1152]{2,1,0:T(8,128)(2,1)S(1)}, bf16[2,64,1152]{2,1,0:T(8,128)(2,1)S(1)}, u32[]{:S(2)}, u32[]{:S(2)}) collective-permute-start(bf16[2,64,1152]{2,1,0:T(8,128)(2,1)S(1)} %get-tuple-element.73), channel_id=1, source_target_pairs={{0,0},{1,1},{2,4},{4,2},{3,5},{5,3},{6,6},{7,7},{8,8},{9,9},{10,12... | collective-permute-start | bytes 884744 | tf_op jit(solution)/shard_map/ppermute | solution.py:447
  14.7 1.8 %collective-permute-start.5 = (bf16[2,64,1152]{2,1,0:T(8,128)(2,1)S(1)}, bf16[2,64,1152]{2,1,0:T(8,128)(2,1)S(1)}, u32[]{:S(2)}, u32[]{:S(2)}) collective-permute-start(bf16[2,64,1152]{2,1,0:T(8,128)(2,1)S(1)} %get-tuple-element.74), channel_id=1, source_target_pairs={{0,2},{1,3},{2,0},{3,1},{4,6},{5,7},{6,4},{7,5},{8,10},{9,11},{10,... | collective-permute-start | bytes 884744 | tf_op jit(solution)/shard_map/ppermute | solution.py:44
  16.5 1.0 %shard_map.88.refs_0_ = bf16[8,64,1152]{2,1,0:T(8,128)(2,1)S(1)} custom-call(bf16[4,64,1152]{2,1,0:T(8,128)(2,1)S(1)} %get-tuple-element.68.cot.ab_ref, bf16[1152,1152]{1,0:T(8,128)(2,1)S(1)} %copy-done), custom_call_target="tpu_custom_call" | custom-call | flops 700000000 | bytes 4423680 | tf_op jit(solution)/shard_map/pallas_call | solution.py:134
  17.6 0.3 collective-permute-done.3.near
  17.9 6.7 %shard_map.89 = (bf16[8,64,3456]{2,1,0:T(8,128)(2,1)S(1)}, bf16[8,64,1152]{2,1,0:T(8,128)(2,1)S(1)}, f32[16,2048]{1,0:T(8,128)S(1)}, bf16[2048,1152]{1,0:T(8,128)(2,1)S(1)}) custom-call(s32[6]{0:T(128)S(1)} %fusion.spot, bf16[2,64,1152]{2,1,0:T(8,128)(2,1)S(1)} %collective-permute-done.1.far, ...), custom_call_target="tpu_custom_call", output_to_operand_aliasing={{0}: (4, {})} | custom-call | flops 8000000000 | bytes 21696512 | tf_op jit(solution)/shard_map/pallas_call | solution.py:134
  24.6 1.7 %shard_map.90 = (bf16[4,144,1152]{2,1,0:T(8,128)(2,1)S(1)}, bf16[1152,512]{1,0:T(8,128)(2,1)S(1)}, bf16[8,64,1152]{2,1,0:T(8,128)(2,1)S(1)}) custom-call(s32[6]{0:T(128)S(1)} %fusion.spot, bf16[8,64,1152]{2,1,0:T(8,128)(2,1)S(1)} %get-tuple-element.87.att_ref, bf16[4,64,1152]{2,1,0:T(8,128)(2,1)S(1)} %get-tuple-element.68.cot.ab_ref, ...), custom_call_target="tpu_custom_call" | custom-call | flops 700000000 | bytes 6045696 | tf_op jit(solution)/shard_map/pallas_call | solution.py:134
  26.3 0.1 collective-permute-start.6
  26.4 1.0 %shard_map.92.ga_ref = bf16[8,64,1152]{2,1,0:T(8,128)(2,1)S(1)} custom-call(bf16[8,64,1152]{2,1,0:T(8,128)(2,1)S(1)} %get-tuple-element.78.cot, bf16[1152,1152]{1,0:T(8,128)(2,1)S(1)} %copy-done, bf16[8,64,1152]{2,1,0:T(8,128)(2,1)S(1)} %shard_map.88.refs_0_), custom_call_target="tpu_custom_call", output_to_operand_aliasing={{}: (2, {})} | custom-call | flops 700000000 | bytes 6193152 | tf_op jit(solution)/shard_map/pallas_call | solution.py:134
  27.5 1.5 %shard_map.91.mine = f32[5184,128]{1,0:T(8,128)S(1)} custom-call(s32[6]{0:T(128)S(1)} %fusion.spot, bf16[1152,512]{1,0:T(8,128)(2,1)S(1)} %get-tuple-element.75.att_t, bf16[8,64,1152]{2,1,0:T(8,128)(2,1)S(1)} %get-tuple-element.78.cot), custom_call_target="tpu_custom_call" | custom-call | flops 700000000 | bytes 5013504 | tf_op jit(solution)/shard_map/pallas_call | solution.py:134
  28.9 0.5 collective-permute-done.6.got
  29.5 1.0 %shard_map.93 = (f32[4,328,128]{2,1,0:T(8,128)S(1)}, bf16[4,328,128]{2,1,0:T(8,128)(2,1)S(1)}, bf16[4,328,128]{2,1,0:T(8,128)(2,1)S(1)}, bf16[4,328,128]{2,1,0:T(8,128)(2,1)S(1)}) custom-call(s32[6]{0:T(128)S(1)} %fusion.spot, f32[5184,128]{1,0:T(8,128)S(1)} %shard_map.91.mine, bf16[4,144,1152]{2,1,0:T(8,128)(2,1)S(1)} %collective-permute-done.6.got), custom_call_target="tpu_custom_call" | custom-call | flops 700000000 | bytes 5660672 | tf_op jit(solution)/shard_map/pallas_call | solution.py:134
  30.4 2.5 %collective-permute-start.9 = (bf16[4,328,128]{2,1,0:T(8,128)(2,1)S(1)}, bf16[4,328,128]{2,1,0:T(8,128)(2,1)S(1)}, u32[]{:S(2)}, u32[]{:S(2)}) collective-permute-start(bf16[4,328,128]{2,1,0:T(8,128)(2,1)S(1)} %get-tuple-element.105), channel_id=1, source_target_pairs={{0,24},{8,16},{16,8},{24,0},{1,25},{9,17},{17,9},{25,1},{2,26},{10... | collective-permute-start | bytes 1007624 | tf_op jit(solution)/shard_map/ppermute | solution.py:44
  32.9 0.6 collective-permute-start.10
  33.5 0.5 collective-permute-start.11
  34.0 1.9 %shard_map.94 = (bf16[4,64,1152]{2,1,0:T(8,128)(2,1)S(1)}, bf16[2,64,1152]{2,1,0:T(8,128)(2,1)S(1)}, bf16[2,64,1152]{2,1,0:T(8,128)(2,1)S(1)}) custom-call(bf16[8,64,1152]{2,1,0:T(8,128)(2,1)S(1)} %get-tuple-element.87.att_ref, bf16[1152,1152]{1,0:T(8,128)(2,1)S(1)} %copy-done), custom_call_target="tpu_custom_call" | custom-call | flops 1000000 | bytes 1000 | tf_op jit(solution)/shard_map/pallas_call | solution.py:134
  35.8 0.9 %collective-permute-start.7 = (bf16[2,64,1152]{2,1,0:T(8,128)(2,1)S(1)}, bf16[2,64,1152]{2,1,0:T(8,128)(2,1)S(1)}, u32[]{:S(2)}, u32[]{:S(2)}) collective-permute-start(bf16[2,64,1152]{2,1,0:T(8,128)(2,1)S(1)} %get-tuple-element.97), channel_id=1, source_target_pairs={{0,0},{1,1},{2,4},{4,2},{3,5},{5,3},{6,6},{7,7},{8,8},{9,9},{10,12... | collective-permute-start | bytes 884744 | tf_op jit(solution)/shard_map/ppermute | solution.py:447
  36.8 3.4 %collective-permute-start.8 = (bf16[2,64,1152]{2,1,0:T(8,128)(2,1)S(1)}, bf16[2,64,1152]{2,1,0:T(8,128)(2,1)S(1)}, u32[]{:S(2)}, u32[]{:S(2)}) collective-permute-start(bf16[2,64,1152]{2,1,0:T(8,128)(2,1)S(1)} %get-tuple-element.98), channel_id=1, source_target_pairs={{0,2},{1,3},{2,0},{3,1},{4,6},{5,7},{6,4},{7,5},{8,10},{9,11},{10,... | collective-permute-start | bytes 884744 | tf_op jit(solution)/shard_map/ppermute | solution.py:44
  40.2 5.6 %shard_map.95.d_ref = bf16[8,64,3456]{2,1,0:T(8,128)(2,1)S(1)} custom-call(s32[6]{0:T(128)S(1)} %fusion.spot, bf16[8,64,1152]{2,1,0:T(8,128)(2,1)S(1)} %shard_map.92.ga_ref, bf16[8,64,3456]{2,1,0:T(8,128)(2,1)S(1)} %get-tuple-element.91.qkv_ref, f32[16,2048]{1,0:T(8,128)S(1)} %get-tuple-element.92.p_ref, bf16[2048,1152]{1,0:T(8,128)(2,1)S(1)} %get-tuple-element.93.wide_ref, ...), custom_call_target="tpu_custom_call" | custom-call | flops 1000000 | bytes 1000 | tf_op jit(solution)/shard_map/pallas_call | solution.py:134
  45.8 3.0 %shard_map.96 = (bf16[2,64,1152]{2,1,0:T(8,128)(2,1)S(1)}, bf16[2,64,1152]{2,1,0:T(8,128)(2,1)S(1)}) custom-call(bf16[8,64,3456]{2,1,0:T(8,128)(2,1)S(1)} %shard_map.95.d_ref, bf16[1152,3456]{1,0:T(8,128)(2,1)S(1)} %bitcast.6), custom_call_target="tpu_custom_call" | custom-call | flops 1000000 | bytes 1000 | tf_op jit(solution)/shard_map/pallas_call | solution.py:134
  48.9 0.9 %shard_map.97 = (f32[328,128]{1,0:T(8,128)S(1)}, bf16[328,128]{1,0:T(8,128)(2,1)S(1)}, bf16[328,128]{1,0:T(8,128)(2,1)S(1)}, bf16[328,128]{1,0:T(8,128)(2,1)S(1)}) custom-call(s32[6]{0:T(128)S(1)} %fusion.spot, f32[4,328,128]{2,1,0:T(8,128)S(1)} %get-tuple-element.104.own, bf16[4,328,128]{2,1,0:T(8,128)(2,1)S(1)} %collective-permute-done.9.one, ...), custom_call_target="tpu_custom_call" | custom-call | flops 1000000 | bytes 2099200 | tf_op jit(solution)/shard_map/pallas_call | solution.py:134
  49.7 2.6 %collective-permute-start.12 = (bf16[328,128]{1,0:T(8,128)(2,1)S(1)}, bf16[328,128]{1,0:T(8,128)(2,1)S(1)}, u32[]{:S(2)}, u32[]{:S(2)}) collective-permute-start(bf16[328,128]{1,0:T(8,128)(2,1)S(1)} %get-tuple-element.115), channel_id=1, source_target_pairs={{0,6},{1,7},{2,4},{3,5},{4,2},{5,3},{6,0},{7,1},{8,14},{9,15},{10,... | collective-permute-start | bytes 251912 | tf_op jit(solution)/shard_map/ppermute | solution.py:44
  52.3 1.8 %collective-permute-start.14 = (bf16[328,128]{1,0:T(8,128)(2,1)S(1)}, bf16[328,128]{1,0:T(8,128)(2,1)S(1)}, u32[]{:S(2)}, u32[]{:S(2)}) collective-permute-start(bf16[328,128]{1,0:T(8,128)(2,1)S(1)} %get-tuple-element.117), channel_id=1, source_target_pairs={{0,4},{1,5},{2,6},{3,7},{4,0},{5,1},{6,2},{7,3},{8,12},{9,13},{10,... | collective-permute-start | bytes 251912 | tf_op jit(solution)/shard_map/ppermute | solution.py:44
  54.2 0.7 collective-permute-start.15
  54.8 2.9 %collective-permute-start.16 = (bf16[2,64,1152]{2,1,0:T(8,128)(2,1)S(1)}, bf16[2,64,1152]{2,1,0:T(8,128)(2,1)S(1)}, u32[]{:S(2)}, u32[]{:S(2)}) collective-permute-start(bf16[2,64,1152]{2,1,0:T(8,128)(2,1)S(1)} %get-tuple-element.120), channel_id=1, source_target_pairs={{0,2},{1,3},{2,0},{3,1},{4,6},{5,7},{6,4},{7,5},{8,10},{9,11},{10,... | collective-permute-start | bytes 884744 | tf_op jit(solution)/shard_map/ppermute | solution.py:44
  57.8 3.0 %shard_map.98.refs_3_ = bf16[4,64,1152]{2,1,0:T(8,128)(2,1)S(1)} custom-call(bf16[8,64,3456]{2,1,0:T(8,128)(2,1)S(1)} %shard_map.95.d_ref, bf16[1152,3456]{1,0:T(8,128)(2,1)S(1)} %bitcast.6), custom_call_target="tpu_custom_call" | custom-call | flops 8000000000 | bytes 12091392 | tf_op jit(solution)/shard_map/pallas_call | solution.py:134
  60.8 0.3 collective-permute-done.14.three
  61.2 2.5 %collective-permute-start.20 = (bf16[328,128]{1,0:T(8,128)(2,1)S(1)}, bf16[328,128]{1,0:T(8,128)(2,1)S(1)}, u32[]{:S(2)}, u32[]{:S(2)}) collective-permute-start(bf16[328,128]{1,0:T(8,128)(2,1)S(1)} %shard_map.99.own), channel_id=1, source_target_pairs={{0,24},{8,16},{16,8},{24,0},{1,25},{9,17},{17,9},{25,1},{2,26},{10... | collective-permute-start | bytes 251912 | tf_op jit(solution)/shard_map/ppermute | solution.py:44
  63.7 0.5 collective-permute-start.19
  64.2 0.5 collective-permute-start.18
  64.7 0.9 %collective-permute-done.16.refs_5_ = bf16[2,64,1152]{2,1,0:T(8,128)(2,1)S(1)} collective-permute-done((bf16[2,64,1152]{2,1,0:T(8,128)(2,1)S(1)}, bf16[2,64,1152]{2,1,0:T(8,128)(2,1)S(1)}, u32[]{:S(2)}, u32[]{:S(2)}) %collective-permute-start.16) | collective-permute-done | bytes 294944 | tf_op jit(solution)/shard_map/ppermute | solution.py:44
  65.7 0.7 %shard_map.100 = (bf16[4,64,1152]{2,1,0:T(8,128)(2,1)S(1)}, bf16[4,64,1152]{2,1,0:T(8,128)(2,1)S(1)}) custom-call(s32[6]{0:T(128)S(1)} %fusion.spot, bf16[4,64,1152]{2,1,0:T(8,128)(2,1)S(1)} %get-tuple-element.99.refs_0_, bf16[2,64,1152]{2,1,0:T(8,128)(2,1)S(1)} %collective-permute-done.7.refs_1_, bf16[2,64,1152]{2,1,0:T(8,128)(2,1)S(1)} %collective-permute-done.8.refs_2_, ...), custom_call_target="tpu_custom_call" | custom-call | flops 1000000 | bytes 3538944 | tf_op jit(solution)/shard_map/pallas_call | solution.py:134
  66.4 0.1 collective-permute-start.17
  66.5 0.9 %collective-permute-done.20.three = bf16[328,128]{1,0:T(8,128)(2,1)S(1)} collective-permute-done((bf16[328,128]{1,0:T(8,128)(2,1)S(1)}, bf16[328,128]{1,0:T(8,128)(2,1)S(1)}, u32[]{:S(2)}, u32[]{:S(2)}) %collective-permute-start.20) | collective-permute-done | bytes 84000 | tf_op jit(solution)/shard_map/ppermute | solution.py:44
  67.3 0.8 %collective-permute-done.19.two = bf16[328,128]{1,0:T(8,128)(2,1)S(1)} collective-permute-done((bf16[328,128]{1,0:T(8,128)(2,1)S(1)}, bf16[328,128]{1,0:T(8,128)(2,1)S(1)}, u32[]{:S(2)}, u32[]{:S(2)}) %collective-permute-start.19) | collective-permute-done | bytes 84000 | tf_op jit(solution)/shard_map/ppermute | solution.py:44
  68.2 0.5 collective-permute-done.18.one
  68.7 0.6 shard_map.101.rows
  69.3 1.8 %shard_map.102 = (bf16[4,64,1152]{2,1,0:T(8,128)(2,1)}, bf16[4,64,1152]{2,1,0:T(8,128)(2,1)}, f32[144,1152]{1,0:T(8,128)}) custom-call(s32[6]{0:T(128)S(1)} %fusion.spot, bf16[4,64,1152]{2,1,0:T(8,128)(2,1)S(1)} %get-tuple-element.121.own, bf16[4,64,1152]{2,1,0:T(8,128)(2,1)S(1)} %collective-permute-done.17.sib, f32[144,1152]{1,0:T(8,128)S(1)} %shard_map.101.rows), custom_call_target="tpu_custom_call" | custom-call | flops 1000000 | bytes 3686400 | tf_op jit(solution)/shard_map/pallas_call | solution.py:134
  (25 shorter events, 0.1 us)
Async XLA Ops:
  0.6 2.5 %collective-permute-start = (bf16[4,64,1152]{2,1,0:T(8,128)(2,1)}, bf16[4,64,1152]{2,1,0:T(8,128)(2,1)S(1)}, u32[]{:S(2)}, u32[]{:S(2)}) collective-permute-start(bf16[4,64,1152]{2,1,0:T(8,128)(2,1)} %bitcast.9), channel_id=1, source_target_pairs={{0,1},{1,0},{2,3},{3,2},{4,5},{5,4},{6,7},{7,6},{8,9},{9,8},{10,11... | collective-permute-start | bytes 1769480 | tf_op jit(solution)/shard_map/ppermute | solution.py:44
  1.1 12.1 %collective-permute-start.2 = (bf16[4,64,1152]{2,1,0:T(8,128)(2,1)}, bf16[4,64,1152]{2,1,0:T(8,128)(2,1)S(1)}, u32[]{:S(2)}, u32[]{:S(2)}) collective-permute-start(bf16[4,64,1152]{2,1,0:T(8,128)(2,1)} %bitcast.7), channel_id=1, source_target_pairs={{0,1},{1,0},{2,3},{3,2},{4,5},{5,4},{6,7},{7,6},{8,9},{9,8},{10,11... | collective-permute-start | bytes 1769480 | tf_op jit(solution)/shard_map/ppermute | solution.py:44
  2.0 8.5 %slice-start = ((s8[7962624]{0:T(1024)(128)(4,1)}), s8[4194304]{0:T(1024)(128)(4,1)S(1)}, s32[]{:S(2)}) async-start(s8[7962624]{0:T(1024)(128)(4,1)} %bitcast.5), calls=%async_computation | async-start | bytes 8388608
  3.1 7.4 %slice-start.1 = ((s8[7962624]{0:T(1024)(128)(4,1)}), s8[3768320]{0:T(1024)(128)(4,1)S(1)}, s32[]{:S(2)}) async-start(s8[7962624]{0:T(1024)(128)(4,1)} %bitcast.5), calls=%async_computation.1 | async-start | bytes 7536640
  3.8 13.8 %collective-permute-start.1 = (bf16[2,64,1152]{2,1,0:T(8,128)(2,1)S(1)}, bf16[2,64,1152]{2,1,0:T(8,128)(2,1)S(1)}, u32[]{:S(2)}, u32[]{:S(2)}) collective-permute-start(bf16[2,64,1152]{2,1,0:T(8,128)(2,1)S(1)} %get-tuple-element.65), channel_id=1, source_target_pairs={{0,0},{1,1},{2,4},{4,2},{3,5},{5,3},{6,6},{7,7},{8,8},{9,9},{10,12... | collective-permute-start | bytes 884744 | tf_op jit(solution)/shard_map/ppermute | solution.py:447
  4.6 13.3 %collective-permute-start.3 = (bf16[2,64,1152]{2,1,0:T(8,128)(2,1)S(1)}, bf16[2,64,1152]{2,1,0:T(8,128)(2,1)S(1)}, u32[]{:S(2)}, u32[]{:S(2)}) collective-permute-start(bf16[2,64,1152]{2,1,0:T(8,128)(2,1)S(1)} %get-tuple-element.70), channel_id=1, source_target_pairs={{0,2},{1,3},{2,0},{3,1},{4,6},{5,7},{6,4},{7,5},{8,10},{9,11},{10,... | collective-permute-start | bytes 884744 | tf_op jit(solution)/shard_map/ppermute | solution.py:44
  10.5 2.8 %copy-start.1 = (bf16[1,1,256,1152]{3,2,1,0:T(8,128)(2,1)S(1)}, bf16[1,1,256,1152]{3,2,1,0:T(8,128)(2,1)}, u32[]{:S(2)}) copy-start(bf16[1,1,256,1152]{3,2,1,0:T(8,128)(2,1)} %param.9) | copy-start | bytes 1769476
  10.5 6.1 %copy-start = (bf16[1152,1152]{1,0:T(8,128)(2,1)S(1)}, bf16[1152,1152]{1,0:T(8,128)(2,1)}, u32[]{:S(2)}) copy-start(bf16[1152,1152]{1,0:T(8,128)(2,1)} %w_ref.1) | copy-start | bytes 7962628
  13.2 4.7 %copy-start.2 = (bf16[16,1152]{1,0:T(8,128)(2,1)S(1)}, bf16[16,1152]{1,0:T(8,128)(2,1)}, u32[]{:S(2)}) copy-start(bf16[16,1152]{1,0:T(8,128)(2,1)} %constant.28.clone.heads_ref) | copy-start | bytes 110596
  13.9 10.7 %collective-permute-start.4 = (bf16[2,64,1152]{2,1,0:T(8,128)(2,1)S(1)}, bf16[2,64,1152]{2,1,0:T(8,128)(2,1)S(1)}, u32[]{:S(2)}, u32[]{:S(2)}) collective-permute-start(bf16[2,64,1152]{2,1,0:T(8,128)(2,1)S(1)} %get-tuple-element.73), channel_id=1, source_target_pairs={{0,0},{1,1},{2,4},{4,2},{3,5},{5,3},{6,6},{7,7},{8,8},{9,9},{10,12... | collective-permute-start | bytes 884744 | tf_op jit(solution)/shard_map/ppermute | solution.py:447
  14.7 9.8 %collective-permute-start.5 = (bf16[2,64,1152]{2,1,0:T(8,128)(2,1)S(1)}, bf16[2,64,1152]{2,1,0:T(8,128)(2,1)S(1)}, u32[]{:S(2)}, u32[]{:S(2)}) collective-permute-start(bf16[2,64,1152]{2,1,0:T(8,128)(2,1)S(1)} %get-tuple-element.74), channel_id=1, source_target_pairs={{0,2},{1,3},{2,0},{3,1},{4,6},{5,7},{6,4},{7,5},{8,10},{9,11},{10,... | collective-permute-start | bytes 884744 | tf_op jit(solution)/shard_map/ppermute | solution.py:44
  26.3 3.1 %collective-permute-start.6 = (bf16[4,144,1152]{2,1,0:T(8,128)(2,1)S(1)}, bf16[4,144,1152]{2,1,0:T(8,128)(2,1)S(1)}, u32[]{:S(2)}, u32[]{:S(2)}) collective-permute-start(bf16[4,144,1152]{2,1,0:T(8,128)(2,1)S(1)} %get-tuple-element.77), channel_id=1, source_target_pairs={{0,1},{1,0},{2,3},{3,2},{4,5},{5,4},{6,7},{7,6},{8,9},{9,8},{10,11... | collective-permute-start | bytes 3981320 | tf_op jit(solution)/shard_map/ppermute | solution.py:44
  30.4 18.4 %collective-permute-start.9 = (bf16[4,328,128]{2,1,0:T(8,128)(2,1)S(1)}, bf16[4,328,128]{2,1,0:T(8,128)(2,1)S(1)}, u32[]{:S(2)}, u32[]{:S(2)}) collective-permute-start(bf16[4,328,128]{2,1,0:T(8,128)(2,1)S(1)} %get-tuple-element.105), channel_id=1, source_target_pairs={{0,24},{8,16},{16,8},{24,0},{1,25},{9,17},{17,9},{25,1},{2,26},{10... | collective-permute-start | bytes 1007624 | tf_op jit(solution)/shard_map/ppermute | solution.py:44
  32.9 15.9 %collective-permute-start.10 = (bf16[4,328,128]{2,1,0:T(8,128)(2,1)S(1)}, bf16[4,328,128]{2,1,0:T(8,128)(2,1)S(1)}, u32[]{:S(2)}, u32[]{:S(2)}) collective-permute-start(bf16[4,328,128]{2,1,0:T(8,128)(2,1)S(1)} %get-tuple-element.106), channel_id=1, source_target_pairs={{0,8},{8,0},{16,24},{24,16},{1,9},{9,1},{17,25},{25,17},{2,10},{10... | collective-permute-start | bytes 1007624 | tf_op jit(solution)/shard_map/ppermute | solution.py:44
  33.5 15.4 %collective-permute-start.11 = (bf16[4,328,128]{2,1,0:T(8,128)(2,1)S(1)}, bf16[4,328,128]{2,1,0:T(8,128)(2,1)S(1)}, u32[]{:S(2)}, u32[]{:S(2)}) collective-permute-start(bf16[4,328,128]{2,1,0:T(8,128)(2,1)S(1)} %get-tuple-element.107), channel_id=1, source_target_pairs={{0,16},{8,24},{16,0},{24,8},{1,17},{9,25},{17,1},{25,9},{2,18},{10... | collective-permute-start | bytes 1007624 | tf_op jit(solution)/shard_map/ppermute | solution.py:44
  35.8 13.0 %collective-permute-start.7 = (bf16[2,64,1152]{2,1,0:T(8,128)(2,1)S(1)}, bf16[2,64,1152]{2,1,0:T(8,128)(2,1)S(1)}, u32[]{:S(2)}, u32[]{:S(2)}) collective-permute-start(bf16[2,64,1152]{2,1,0:T(8,128)(2,1)S(1)} %get-tuple-element.97), channel_id=1, source_target_pairs={{0,0},{1,1},{2,4},{4,2},{3,5},{5,3},{6,6},{7,7},{8,8},{9,9},{10,12... | collective-permute-start | bytes 884744 | tf_op jit(solution)/shard_map/ppermute | solution.py:447
  36.8 12.1 %collective-permute-start.8 = (bf16[2,64,1152]{2,1,0:T(8,128)(2,1)S(1)}, bf16[2,64,1152]{2,1,0:T(8,128)(2,1)S(1)}, u32[]{:S(2)}, u32[]{:S(2)}) collective-permute-start(bf16[2,64,1152]{2,1,0:T(8,128)(2,1)S(1)} %get-tuple-element.98), channel_id=1, source_target_pairs={{0,2},{1,3},{2,0},{3,1},{4,6},{5,7},{6,4},{7,5},{8,10},{9,11},{10,... | collective-permute-start | bytes 884744 | tf_op jit(solution)/shard_map/ppermute | solution.py:44
  49.7 11.1 %collective-permute-start.12 = (bf16[328,128]{1,0:T(8,128)(2,1)S(1)}, bf16[328,128]{1,0:T(8,128)(2,1)S(1)}, u32[]{:S(2)}, u32[]{:S(2)}) collective-permute-start(bf16[328,128]{1,0:T(8,128)(2,1)S(1)} %get-tuple-element.115), channel_id=1, source_target_pairs={{0,6},{1,7},{2,4},{3,5},{4,2},{5,3},{6,0},{7,1},{8,14},{9,15},{10,... | collective-permute-start | bytes 251912 | tf_op jit(solution)/shard_map/ppermute | solution.py:44
  52.3 8.5 %collective-permute-start.13 = (bf16[328,128]{1,0:T(8,128)(2,1)S(1)}, bf16[328,128]{1,0:T(8,128)(2,1)S(1)}, u32[]{:S(2)}, u32[]{:S(2)}) collective-permute-start(bf16[328,128]{1,0:T(8,128)(2,1)S(1)} %get-tuple-element.116), channel_id=1, source_target_pairs={{0,2},{1,3},{2,0},{3,1},{4,6},{5,7},{6,4},{7,5},{8,10},{9,11},{10,... | collective-permute-start | bytes 251912 | tf_op jit(solution)/shard_map/ppermute | solution.py:44
  52.3 8.8 %collective-permute-start.14 = (bf16[328,128]{1,0:T(8,128)(2,1)S(1)}, bf16[328,128]{1,0:T(8,128)(2,1)S(1)}, u32[]{:S(2)}, u32[]{:S(2)}) collective-permute-start(bf16[328,128]{1,0:T(8,128)(2,1)S(1)} %get-tuple-element.117), channel_id=1, source_target_pairs={{0,4},{1,5},{2,6},{3,7},{4,0},{5,1},{6,2},{7,3},{8,12},{9,13},{10,... | collective-permute-start | bytes 251912 | tf_op jit(solution)/shard_map/ppermute | solution.py:44
  54.2 10.6 %collective-permute-start.15 = (bf16[2,64,1152]{2,1,0:T(8,128)(2,1)S(1)}, bf16[2,64,1152]{2,1,0:T(8,128)(2,1)S(1)}, u32[]{:S(2)}, u32[]{:S(2)}) collective-permute-start(bf16[2,64,1152]{2,1,0:T(8,128)(2,1)S(1)} %get-tuple-element.119), channel_id=1, source_target_pairs={{0,0},{1,1},{2,4},{4,2},{3,5},{5,3},{6,6},{7,7},{8,8},{9,9},{10,12... | collective-permute-start | bytes 884744 | tf_op jit(solution)/shard_map/ppermute | solution.py:447
  54.8 10.8 %collective-permute-start.16 = (bf16[2,64,1152]{2,1,0:T(8,128)(2,1)S(1)}, bf16[2,64,1152]{2,1,0:T(8,128)(2,1)S(1)}, u32[]{:S(2)}, u32[]{:S(2)}) collective-permute-start(bf16[2,64,1152]{2,1,0:T(8,128)(2,1)S(1)} %get-tuple-element.120), channel_id=1, source_target_pairs={{0,2},{1,3},{2,0},{3,1},{4,6},{5,7},{6,4},{7,5},{8,10},{9,11},{10,... | collective-permute-start | bytes 884744 | tf_op jit(solution)/shard_map/ppermute | solution.py:44
  61.2 6.2 %collective-permute-start.20 = (bf16[328,128]{1,0:T(8,128)(2,1)S(1)}, bf16[328,128]{1,0:T(8,128)(2,1)S(1)}, u32[]{:S(2)}, u32[]{:S(2)}) collective-permute-start(bf16[328,128]{1,0:T(8,128)(2,1)S(1)} %shard_map.99.own), channel_id=1, source_target_pairs={{0,24},{8,16},{16,8},{24,0},{1,25},{9,17},{17,9},{25,1},{2,26},{10... | collective-permute-start | bytes 251912 | tf_op jit(solution)/shard_map/ppermute | solution.py:44
  63.7 4.5 %collective-permute-start.19 = (bf16[328,128]{1,0:T(8,128)(2,1)S(1)}, bf16[328,128]{1,0:T(8,128)(2,1)S(1)}, u32[]{:S(2)}, u32[]{:S(2)}) collective-permute-start(bf16[328,128]{1,0:T(8,128)(2,1)S(1)} %shard_map.99.own), channel_id=1, source_target_pairs={{0,16},{8,24},{16,0},{24,8},{1,17},{9,25},{17,1},{25,9},{2,18},{10... | collective-permute-start | bytes 251912 | tf_op jit(solution)/shard_map/ppermute | solution.py:44
  64.2 4.5 %collective-permute-start.18 = (bf16[328,128]{1,0:T(8,128)(2,1)S(1)}, bf16[328,128]{1,0:T(8,128)(2,1)S(1)}, u32[]{:S(2)}, u32[]{:S(2)}) collective-permute-start(bf16[328,128]{1,0:T(8,128)(2,1)S(1)} %shard_map.99.own), channel_id=1, source_target_pairs={{0,8},{8,0},{16,24},{24,16},{1,9},{9,1},{17,25},{25,17},{2,10},{10... | collective-permute-start | bytes 251912 | tf_op jit(solution)/shard_map/ppermute | solution.py:44
  66.4 2.9 %collective-permute-start.17 = (bf16[4,64,1152]{2,1,0:T(8,128)(2,1)S(1)}, bf16[4,64,1152]{2,1,0:T(8,128)(2,1)S(1)}, u32[]{:S(2)}, u32[]{:S(2)}) collective-permute-start(bf16[4,64,1152]{2,1,0:T(8,128)(2,1)S(1)} %get-tuple-element.122), channel_id=1, source_target_pairs={{0,1},{1,0},{2,3},{3,2},{4,5},{5,4},{6,7},{7,6},{8,9},{9,8},{10,11... | collective-permute-start | bytes 1769480 | tf_op jit(solution)/shard_map/ppermute | solution.py:44
